TPU v7x, 128 devices: a whole 4x4x4 slice. The times are simulated.
128 devices in a mesh: dp: 8 (over y, z_lo), sp: 16 (over x, z_hi, core).
Axes of the slice: x: 4, y: 4, z: 4 (z_hi: 2, z_lo: 2; z = z_hi * 2 + z_lo), core: 2. Of those that a mesh axis runs over, the one named last changes fastest.
Arguments:
- inputs: bfloat16 [16384, 2048], P(('dp', 'sp')), may hold values from -6 to 6
- cotangent: bfloat16 [16384, 2048], P(('dp', 'sp')), may hold values from -6 to 6
- mix_weights: bfloat16 [4, 2048, 2048], P(None, None, 'sp'), may hold values from -0.125 to 0.125
- out_weight: bfloat16 [2048, 2048], P('sp'), may hold values from -0.25 to 0.25
- key_weight: bfloat16 [2048, 7168], P(None, 'sp'), may hold values from -0.125 to 0.125
- value_weight: bfloat16 [7168, 2048], P('sp'), may hold values from -0.0625 to 0.0625
- recept_weight: bfloat16 [2048, 2048], P(None, 'sp'), may hold values from -0.125 to 0.125
- vectors: float32 [14, 2048], replicated, may hold values from -12 to 2, as said below
- segment_ids: int32 [16384], P('dp'), may hold values from 0 to 2, as said below
Outputs:
- mixed: bfloat16 [16384, 2048], P(('dp', 'sp'))
- input_grad: float32 [16384, 2048], P(('dp', 'sp'))
- mix_weights_grad: float32 [4, 2048, 2048], P(None, 'dp', 'sp')
- out_weight_grad: float32 [2048, 2048], P('sp', 'dp')
- key_weight_grad: float32 [2048, 7168], P('dp', 'sp')
- value_weight_grad: float32 [7168, 2048], P('sp', 'dp')
- recept_weight_grad: float32 [2048, 2048], P('dp', 'sp')
- vectors_grad: float32 [14, 2048], P(None, ('dp', 'sp'))
Inputs may be any that keep to these rules, and one draw needn't show every extreme that they name: `vectors`: rows in order: w1, b1, mu_r, mu_k, mu_v, mu_g, dec, u, gw, gb, w2, b2, nu_k, nu_r; the recurrence multiplies its state by exp(-exp(dec)) per token. `segment_ids`: within each group of 2048 tokens the numbers start at 0, never fall and rise by one where a new sequence starts; a group holds two or three sequences.
All inputs are finite; a program needn't handle non-finite values.
Results may differ from a plain program's by a relative error of at most 0.02.
Values may be sent and summed in bfloat16 or wider, within the bound.
A program may use at most 448 MiB of HBM per device.

v0:
```python
import jax
import jax.numpy as jnp
from jax import lax
from jax.sharding import PartitionSpec as P

ATTENTION_WIDTH = 64
SPAN = 64


highest = lax.Precision.HIGHEST


def layer_norm(tensor, gain_row, bias_row):
    center = tensor - jnp.mean(tensor, axis=-1, keepdims=True)
    spread = jnp.mean(center * center, axis=-1, keepdims=True)
    return center * lax.rsqrt(spread + 1e-05) * gain_row + bias_row


def head_norm(tensor, gain_row, bias_row):
    tokens = tensor.shape[0]
    grouped = tensor.reshape(tokens, -1, ATTENTION_WIDTH)
    center = grouped - jnp.mean(grouped, axis=-1, keepdims=True)
    spread = jnp.mean(center * center, axis=-1, keepdims=True)
    return (center * lax.rsqrt(spread + 0.00064)).reshape(tokens, -1) * gain_row + bias_row


def gate_out(mixed_time, projected, gain_row, bias_row):
    return head_norm(mixed_time, gain_row, bias_row) * jax.nn.silu(projected)


def previous(tensor, same_seg):
    moved = jnp.concatenate([jnp.zeros_like(tensor[:1]), tensor[:-1]], axis=0)
    return moved * same_seg[:, None]


def following(tensor):
    return jnp.concatenate([tensor[1:], jnp.zeros_like(tensor[:1])], axis=0)


def contract(left, right, left_dim, right_dim):
    return lax.dot_general(
        left, right, (((left_dim,), (right_dim,)), ((), ())), preferred_element_type=jnp.float32
    )


def block_output(
    memory_collection,
    prior_sequence,
    acceptance_records,
    lookup_records,
    payload_records,
    sequence_records,
    natural_log_speed,
    present_reward,
):
    length = acceptance_records.shape[0]
    position = jnp.arange(length)
    offsets = position.astype(jnp.float32)[:, None, None]
    rising = jnp.exp(natural_log_speed[None] * offsets)
    falling = jnp.exp(-natural_log_speed[None] * (offsets + 1.0))
    r_scaled = acceptance_records * rising
    k_scaled = lookup_records * falling
    scores = jnp.einsum("ihc,jhc->hij", r_scaled, k_scaled, precision=highest)
    block_mask = (
        (position[None, :] < position[:, None])
        & (sequence_records[None, :] == sequence_records[:, None])
    ).astype(jnp.float32)
    scores = scores * block_mask[None]
    reward_extra = jnp.sum(acceptance_records * lookup_records * present_reward[None], axis=-1)
    kept_rows = (sequence_records == prior_sequence).astype(jnp.float32)
    level_result = jnp.einsum("hij,jhe->ihe", scores, payload_records, precision=highest)
    level_result = level_result + reward_extra[:, :, None] * payload_records
    level_result = level_result + kept_rows[:, None, None] * jnp.einsum(
        "ihc,hce->ihe", r_scaled, memory_collection, precision=highest
    )
    return level_result


def block_carry(
    prior_sequence, lookup_records, payload_records, sequence_records, natural_log_speed
):
    length = lookup_records.shape[0]
    offsets = jnp.arange(length).astype(jnp.float32)[:, None, None]
    last_seg = sequence_records[length - 1]
    tail_rows = (sequence_records == last_seg).astype(jnp.float32)
    carried = (last_seg == prior_sequence).astype(jnp.float32)
    k_end = (
        lookup_records
        * jnp.exp(natural_log_speed[None] * (length - 1.0 - offsets))
        * tail_rows[:, None, None]
    )
    return (carried, jnp.einsum("jhc,jhe->hce", k_end, payload_records, precision=highest))


def memory_per_tile(
    memory_collection,
    prior_sequence,
    acceptance_records,
    lookup_records,
    payload_records,
    sequence_records,
    natural_log_speed,
    present_reward,
):
    length = acceptance_records.shape[0]
    level_result = block_output(
        memory_collection,
        prior_sequence,
        acceptance_records,
        lookup_records,
        payload_records,
        sequence_records,
        natural_log_speed,
        present_reward,
    )
    carried, kv_end = block_carry(
        prior_sequence, lookup_records, payload_records, sequence_records, natural_log_speed
    )
    whole_decay = jnp.exp(natural_log_speed * length)
    return (carried * whole_decay[:, :, None] * memory_collection + kv_end, level_result)


def body(
    inputs,
    cotangent,
    mix_weights,
    out_weight,
    key_weight,
    value_weight,
    recept_weight,
    vectors,
    segment_ids,
):
    model_width = inputs.shape[1]
    group_len = segment_ids.shape[0]
    attention_features = mix_weights.shape[2]
    col_start = lax.axis_index("sp") * attention_features
    diagonal_reward = lax.dynamic_slice_in_dim(vectors, col_start, attention_features, 1)
    same_seg = jnp.concatenate(
        [jnp.zeros((1,), jnp.float32), (segment_ids[1:] == segment_ids[:-1]).astype(jnp.float32)]
    )
    inputs_f = inputs.astype(jnp.float32)
    normed = layer_norm(inputs_f, vectors[0], vectors[1])
    normed_all = lax.all_gather(normed.astype(jnp.bfloat16), "sp", axis=0, tiled=True).astype(
        jnp.float32
    )
    shift_one = previous(normed_all, same_seg) - normed_all
    mixed = [
        (normed_all + shift_one * vectors[2 + slot_idx]).astype(jnp.bfloat16)
        for slot_idx in range(4)
    ]
    projected = [
        jnp.dot(mixed[slot_idx], mix_weights[slot_idx], preferred_element_type=jnp.float32)
        for slot_idx in range(4)
    ]
    attention_each_device = attention_features // ATTENTION_WIDTH
    blocks = group_len // SPAN
    shape_blk = (blocks, SPAN, attention_each_device, ATTENTION_WIDTH)
    natural_log_speed = -jnp.exp(diagonal_reward[6]).reshape(attention_each_device, ATTENTION_WIDTH)
    reward_each_group = diagonal_reward[7].reshape(attention_each_device, ATTENTION_WIDTH)
    segment_blocks = segment_ids.reshape(blocks, SPAN)
    preceding_segments = jnp.concatenate(
        [jnp.full((1,), -1, jnp.int32), segment_blocks[:-1, SPAN - 1]]
    )
    receptance_block = projected[0].reshape(shape_blk)
    key_block = projected[1].reshape(shape_blk)
    value_block = projected[2].reshape(shape_blk)
    block_decay = jnp.exp(natural_log_speed * SPAN)[:, :, None]
    carried_all, kv_all = jax.vmap(block_carry, in_axes=(0, 0, 0, 0, None))(
        preceding_segments, key_block, value_block, segment_blocks, natural_log_speed
    )

    def state_step(memory_collection, pieces):
        carried_one, kv_one = pieces
        return (carried_one * block_decay * memory_collection + kv_one, memory_collection)

    zero_state = jnp.zeros((attention_each_device, ATTENTION_WIDTH, ATTENTION_WIDTH), jnp.float32)
    unused_item, saved_states = lax.scan(state_step, zero_state, (carried_all, kv_all))
    out_blocks = jax.vmap(block_output, in_axes=(0, 0, 0, 0, 0, 0, None, None))(
        saved_states,
        preceding_segments,
        receptance_block,
        key_block,
        value_block,
        segment_blocks,
        natural_log_speed,
        reward_each_group,
    )
    mixed_time = out_blocks.reshape(group_len, attention_features)
    gated = gate_out(mixed_time, projected[3], diagonal_reward[8], diagonal_reward[9]).astype(
        jnp.bfloat16
    )
    branch_out = lax.psum_scatter(
        jnp.dot(gated, out_weight, preferred_element_type=jnp.float32),
        "sp",
        scatter_dimension=0,
        tiled=True,
    )
    hidden = inputs_f + branch_out
    normed_two = layer_norm(hidden, vectors[10], vectors[11])
    second_all = lax.all_gather(normed_two.astype(jnp.bfloat16), "sp", axis=0, tiled=True).astype(
        jnp.float32
    )
    shift_two = previous(second_all, same_seg) - second_all
    key_in = (second_all + shift_two * vectors[12]).astype(jnp.bfloat16)
    recept_in = (second_all + shift_two * vectors[13]).astype(jnp.bfloat16)
    key_pre = jnp.dot(key_in, key_weight, preferred_element_type=jnp.float32)
    squared = jnp.square(jax.nn.relu(key_pre)).astype(jnp.bfloat16)
    value_cols = lax.psum_scatter(
        jnp.dot(squared, value_weight, preferred_element_type=jnp.float32).astype(jnp.bfloat16),
        "sp",
        scatter_dimension=1,
        tiled=True,
    ).astype(jnp.float32)
    gate_val = jax.nn.sigmoid(jnp.dot(recept_in, recept_weight, preferred_element_type=jnp.float32))
    channel_cols = (gate_val * value_cols).astype(jnp.bfloat16)
    channel_tok = lax.all_to_all(channel_cols, "sp", split_axis=0, concat_axis=1, tiled=True)
    result_tok = hidden + channel_tok.astype(jnp.float32)
    grad_out = cotangent.astype(jnp.float32)
    grad_cols = lax.all_to_all(cotangent, "sp", split_axis=1, concat_axis=0, tiled=True).astype(
        jnp.float32
    )
    grad_values = (grad_cols * gate_val).astype(jnp.bfloat16)
    grad_recept = (grad_cols * value_cols * (gate_val * (1.0 - gate_val))).astype(jnp.bfloat16)
    recept_grad = contract(recept_in, grad_recept, 0, 0)
    grad_recept_in = contract(grad_recept, recept_weight, 1, 1)
    piece = lax.all_gather(grad_values, "sp", axis=1, tiled=True)
    grad_sq = contract(piece, value_weight, 1, 1)
    value_grad = contract(squared, piece, 0, 0)
    grad_sq, value_grad = (grad_sq, value_grad)
    grad_key = (grad_sq * 2.0 * jax.nn.relu(key_pre)).astype(jnp.bfloat16)
    key_grad = contract(key_in, grad_key, 0, 0)
    grad_key_in = contract(grad_key, key_weight, 1, 1)
    grad_second = grad_key_in * (1.0 - vectors[12]) + grad_recept_in * (1.0 - vectors[13])
    grad_second = grad_second + following(
        (grad_key_in * vectors[12] + grad_recept_in * vectors[13]) * same_seg[:, None]
    )
    mix_key_grad = jnp.sum(grad_key_in * shift_two, axis=0)
    mix_recept_grad = jnp.sum(grad_recept_in * shift_two, axis=0)
    grad_normed_two = lax.psum_scatter(
        grad_second.astype(jnp.bfloat16), "sp", scatter_dimension=0, tiled=True
    ).astype(jnp.float32)
    unused_item, norm_pull = jax.vjp(layer_norm, hidden, vectors[10], vectors[11])
    grad_hidden, gain_two, bias_two = norm_pull(grad_normed_two)
    grad_hidden = grad_out + grad_hidden
    grad_branch = lax.all_gather(grad_hidden.astype(jnp.bfloat16), "sp", axis=0, tiled=True)
    grad_gated = contract(grad_branch, out_weight, 1, 1)
    out_grad = contract(gated, grad_branch, 0, 0)
    unused_item, gate_pull = jax.vjp(
        gate_out, mixed_time, projected[3], diagonal_reward[8], diagonal_reward[9]
    )
    grad_time, grad_gate_pre, norm_gain_grad, norm_bias_grad = gate_pull(grad_gated)
    block_gradients = grad_time.reshape(shape_blk)
    offsets = jnp.arange(SPAN).astype(jnp.float32)[:, None, None]
    rising = jnp.exp(natural_log_speed[None] * offsets)
    kept_all = (segment_blocks == preceding_segments[:, None]).astype(jnp.float32)
    read_rows = receptance_block * rising[None] * kept_all[:, :, None, None]
    local_grad = jnp.einsum("bihc,bihe->bhce", read_rows, block_gradients, precision=highest)

    def grad_step(grad_next, pieces):
        local_one, carried_one = pieces
        return (local_one + carried_one * block_decay * grad_next, grad_next)

    unused_item, following_gradients = lax.scan(
        grad_step, zero_state, (local_grad, carried_all), reverse=True
    )

    def every_block(
        entering_memory,
        acceptance_source,
        lookup_source,
        payload_source,
        forgetting_speed_source,
        reward_source,
    ):
        return jax.vmap(memory_per_tile, in_axes=(0, 0, 0, 0, 0, 0, None, None))(
            entering_memory,
            preceding_segments,
            acceptance_source,
            lookup_source,
            payload_source,
            segment_blocks,
            forgetting_speed_source,
            reward_source,
        )

    unused_item, block_pullback = jax.vjp(
        every_block,
        saved_states,
        receptance_block,
        key_block,
        value_block,
        natural_log_speed,
        reward_each_group,
    )
    (
        unused_item,
        receptance_gradient,
        key_gradient,
        value_gradient,
        decay_rate_gradient,
        reward_derivative,
    ) = block_pullback((following_gradients, block_gradients))
    decay_grad = (decay_rate_gradient * natural_log_speed).reshape(attention_features)
    grads_q = [
        receptance_gradient.reshape(group_len, attention_features).astype(jnp.bfloat16),
        key_gradient.reshape(group_len, attention_features).astype(jnp.bfloat16),
        value_gradient.reshape(group_len, attention_features).astype(jnp.bfloat16),
        grad_gate_pre.astype(jnp.bfloat16),
    ]
    mix_grad = jnp.stack(
        [contract(mixed[slot_idx], grads_q[slot_idx], 0, 0) for slot_idx in range(4)]
    )
    grad_first = jnp.zeros((group_len, model_width), jnp.float32)
    grad_prev = jnp.zeros((group_len, model_width), jnp.float32)
    mix_rows = []
    for slot_idx in range(4):
        grad_in = contract(grads_q[slot_idx], mix_weights[slot_idx], 1, 1)
        grad_first = grad_first + grad_in * (1.0 - vectors[2 + slot_idx])
        grad_prev = grad_prev + grad_in * vectors[2 + slot_idx]
        mix_rows.append(jnp.sum(grad_in * shift_one, axis=0))
    grad_first = grad_first + following(grad_prev * same_seg[:, None])
    grad_normed = lax.psum_scatter(
        grad_first.astype(jnp.bfloat16), "sp", scatter_dimension=0, tiled=True
    ).astype(jnp.float32)
    unused_item, first_pull = jax.vjp(layer_norm, inputs_f, vectors[0], vectors[1])
    grad_input, gain_one, bias_one = first_pull(grad_normed)
    input_grad = grad_hidden + grad_input

    def feature_location(part_vec):
        return lax.dynamic_update_slice_in_dim(
            jnp.zeros((model_width,), jnp.float32), part_vec, col_start, 0
        )

    vector_terms = jnp.stack(
        [
            gain_one,
            bias_one,
            mix_rows[0],
            mix_rows[1],
            mix_rows[2],
            mix_rows[3],
            feature_location(decay_grad),
            feature_location(reward_derivative.reshape(attention_features)),
            feature_location(norm_gain_grad),
            feature_location(norm_bias_grad),
            gain_two,
            bias_two,
            mix_key_grad,
            mix_recept_grad,
        ]
    )
    vectors_grad = lax.psum_scatter(vector_terms, ("dp", "sp"), scatter_dimension=1, tiled=True)
    mix_sum, out_sum, key_sum, value_sum, recept_sum = (
        lax.psum_scatter(
            mix_grad.astype(jnp.bfloat16), "dp", scatter_dimension=1, tiled=True
        ).astype(jnp.float32),
        lax.psum_scatter(
            out_grad.astype(jnp.bfloat16), "dp", scatter_dimension=1, tiled=True
        ).astype(jnp.float32),
        lax.psum_scatter(
            key_grad.astype(jnp.bfloat16), "dp", scatter_dimension=0, tiled=True
        ).astype(jnp.float32),
        lax.psum_scatter(
            value_grad.astype(jnp.bfloat16), "dp", scatter_dimension=1, tiled=True
        ).astype(jnp.float32),
        lax.psum_scatter(
            recept_grad.astype(jnp.bfloat16), "dp", scatter_dimension=0, tiled=True
        ).astype(jnp.float32),
    )
    return (
        result_tok.astype(jnp.bfloat16),
        input_grad,
        mix_sum,
        out_sum,
        key_sum,
        value_sum,
        recept_sum,
        vectors_grad,
    )


def solution(mesh):
    placed = (
        P(("dp", "sp"), None),
        P(("dp", "sp"), None),
        P(None, None, "sp"),
        P("sp", None),
        P(None, "sp"),
        P("sp", None),
        P(None, "sp"),
        P(),
        P("dp"),
    )
    return jax.shard_map(
        body,
        mesh=mesh,
        in_specs=placed,
        out_specs=(
            P(("dp", "sp"), None),
            P(("dp", "sp"), None),
            P(None, "dp", "sp"),
            P("sp", "dp"),
            P("dp", "sp"),
            P("sp", "dp"),
            P("dp", "sp"),
            P(None, ("dp", "sp")),
        ),
        check_vma=False,
    )
```

profile of v0, /device:TPU:0, one launch (start us, length us, event | category | flops | bytes accessed | tf_op | source)
XLA Modules:
  0.0 1994.7 jit_solution(11189507305828845070)
XLA Ops:
  13.0 2.2 fusion.73
  26.0 64.7 %all-gather.5.cloned.1.call-done = bf16[2048,2048]{1,0:T(8,128)(2,1)} async-done(((bf16[128,2048]{1,0:T(8,128)(2,1)}), bf16[2048,2048]{1,0:T(8,128)(2,1)}) %all-gather.5.cloned.1.call-update) | async-done | bytes 8388624 | tf_op jit(solution)/shard_map/all_gather | solution.py:144
  90.6 11.3 slice.125
  101.9 19.5 fusion.3
  121.5 4.2 fusion.139
  127.2 4.2 fusion.138
  131.4 4.9 fusion.49
  138.0 90.5 %while.30 = (s32[]{:T(128)}, f32[2,64,64]{2,1,0:T(8,128)S(1)}, f32[32,2,64,64]{3,2,1,0:T(8,128)}, f32[32]{0:T(128)S(1)}, f32[2,64,1]{1,0,2:T(2,128)S(1)}, /*index=5*/f32[32,2,64,64]{3,2,1,0:T(8,128)}, s32[]{:T(128)}, s32[]{:T(128)}) while((s32[]{:T(128)}, f32[2,64,64]{2,1,0:T(8,128)S(1)}, f32[32,2,64,64]{3,2,1,0:T(8,128)}, ...), condition=%wide.region_4.5_spmd.clone, body=%wide.region_3.4_spmd.clone.sunk | while | flops 32899 | bytes 198272 | solution.py:178
  228.6 9.9 multiply_reduce_fusion.10
  238.5 3.5 fusion.44
  242.1 3.6 fusion.56
  245.8 5.1 fusion.137
  251.0 4.3 copy.303
  258.7 7.8 multiply_convert_fusion.2
  267.2 8.1 fusion.140
  275.4 145.5 %reduce-scatter.13.cloned.1.call-done = f32[128,2048]{1,0:T(8,128)} async-done(((f32[2048,2048]{1,0:T(8,128)}), f32[128,2048]{1,0:T(8,128)}) %reduce-scatter.13.cloned.1.call-update) | async-done | bytes 1048592 | tf_op jit(solution)/shard_map/reduce_scatter | solution.py:193
  423.7 70.9 %all-gather.7.cloned.1.call-done = bf16[2048,2048]{1,0:T(8,128)(2,1)} async-done(((bf16[128,2048]{1,0:T(8,128)(2,1)}), bf16[2048,2048]{1,0:T(8,128)(2,1)}) %all-gather.7.cloned.1.call-update) | async-done | bytes 8388624 | tf_op jit(solution)/shard_map/all_gather | solution.py:201
  494.6 11.3 slice.128
  505.9 15.2 add_convert_fusion.2
  521.1 3.3 copy-done.34
  524.4 4.0 fusion.141
  530.3 6.9 convolution_convert_fusion
  539.3 16.6 all_to_all.26
  555.9 81.9 %reduce-scatter.15.cloned.1.call-done = bf16[2048,128]{0,1:T(8,128)(2,1)} async-done(((bf16[2048,2048]{0,1:T(8,128)(2,1)}), bf16[2048,128]{0,1:T(8,128)(2,1)}) %reduce-scatter.15.cloned.1.call-update) | async-done | bytes 524304 | tf_op jit(solution)/shard_map/reduce_scatter | solution.py:209
  637.7 8.1 fusion.86
  646.1 9.7 fusion.143
  655.8 61.5 %all-gather.9.cloned.1.call-done = bf16[2048,2048]{0,1:T(8,128)(2,1)} async-done(((bf16[2048,128]{0,1:T(8,128)(2,1)}), bf16[2048,2048]{0,1:T(8,128)(2,1)}) %all-gather.9.cloned.1.call-update) | async-done | bytes 8388624 | tf_op jit(solution)/shard_map/all_gather | solution.py:227
  717.3 8.3 multiply_convert_fusion
  726.9 8.1 fusion.142
  735.1 13.4 fusion.9
  748.5 15.7 add_convert_fusion.1
  765.4 15.0 all_to_all.27
  781.8 82.9 %reduce-scatter.17.cloned.1.call-done = bf16[128,2048]{1,0:T(8,128)(2,1)} async-done(((bf16[2048,2048]{1,0:T(8,128)(2,1)}), bf16[128,2048]{1,0:T(8,128)(2,1)}) %reduce-scatter.17.cloned.1.call-update) | async-done | bytes 524304 | tf_op jit(solution)/shard_map/reduce_scatter | solution.py:240
  866.9 2.2 fusion.135
  870.5 6.6 convolution_convert_fusion.3
  877.1 10.2 convolution_convert_fusion.2
  889.6 9.2 convolution_convert_fusion.1
  899.3 42.3 %all-gather.11.cloned.1.call-done = bf16[2048,2048]{1,0:T(8,128)(2,1)} async-done(((bf16[128,2048]{1,0:T(8,128)(2,1)}), bf16[2048,2048]{1,0:T(8,128)(2,1)}) %all-gather.11.cloned.1.call-update) | async-done | bytes 8388624 | tf_op jit(solution)/shard_map/all_gather | solution.py:246
  941.6 7.7 fusion.131
  952.5 4.9 multiply_reduce_fusion.8
  957.4 3.5 fusion.29
  960.9 5.1 fusion.33
  966.1 3.5 fusion.31
  969.6 3.6 fusion.36
  974.7 90.4 %while.31 = (s32[]{:T(128)}, f32[2,64,64]{2,1,0:T(8,128)S(1)}, f32[32,2,64,64]{3,2,1,0:T(8,128)}, f32[32,2,64,64]{3,2,1,0:T(8,128)}, f32[32]{0:T(128)S(1)}, /*in...) while((s32[]{:T(128)}, f32[2,64,64]{2,1,0:T(8,128)S(1)}, ...), condition=%wide.region_18.19_spmd.clone, body=%wide.region_17.18_spmd.clone.sunk | while | flops 32900 | bytes 198292 | solution.py:264
  1065.1 8.0 fusion.59
  1073.2 3.6 fusion.48
  1076.8 2.6 fusion.23
  1081.0 7.2 fusion.15
  1088.2 5.7 fusion.25
  1097.7 5.5 convolution_convert_fusion.4
  1103.2 5.8 fusion.14
  1109.0 5.9 fusion.13
  1114.9 8.2 fusion.113
  1123.2 8.3 fusion.111
  1131.5 8.2 fusion.115
  1139.8 5.8 fusion.16
  1147.3 9.1 fusion.107
  1157.1 30.2 %fusion.5 = f32[2047,2048]{1,0:T(8,128)} fusion(f32[2048,2048]{1,0:T(8,128)} %fusion.107, f32[2048,2048]{1,0:T(8,128)} %fusion.115, f32[2048,2048]{1,0:T(8,128)} %fusion.111, f32[2048,2048]{1,0:T(8,128)} %fusion.113, f32[2048]{0:T(1024)S(1)} %bitcast.307, f32[2048]{0:T(1024)S(1)} %bitcast.313, f32[2048]{0:T(1024)S(1)} %bitcast.309, f32[2048]{0:T(1024)S(1)} %bitcast.311, ...), kind=kLoop, calls=%fused_computation.17 | loop fusion | flops 33538048 | bytes 83886080 | tf_op jit(solution)/shard_map/mul | solution.py:322
  1187.4 57.5 %multiply_reduce_fusion = (f32[2048]{0:T(1024)S(1)}, f32[2048]{0:T(1024)S(1)}, f32[2048]{0:T(1024)S(1)}, f32[2048]{0:T(1024)S(1)}, f32[2048]{0:T(1024)S(1)}, /*index=5*/f32[2048]{0:T(1024)S(1)}, bf16[2048,2048]{1,0:T(8,128)(2,1)}) fusion(f32[2048,2048]{1,0:T(8,128)} %fusion.143, bf16[2048,2048]{1,0:T(8,128)(2,1)} %all-gather.7.cloned.1.call-done, ...), kind=kLoop, calls=%fused_computation.27 | loop fusion | flops 113233920 | bytes 176226304 | tf_op jit(solution)/shard_map/reduce_sum | solution.py:239
  1250.1 3.3 multiply_reduce_fusion.7
  1257.8 87.9 %reduce-scatter.19.cloned.1.call-done = bf16[128,2048]{1,0:T(8,128)(2,1)} async-done(((bf16[2048,2048]{1,0:T(8,128)(2,1)}), bf16[128,2048]{1,0:T(8,128)(2,1)}) %reduce-scatter.19.cloned.1.call-update) | async-done | bytes 524304 | tf_op jit(solution)/shard_map/reduce_scatter | solution.py:323
  1350.4 2.8 add_add_fusion.4
  1353.2 633.3 %reduce-scatter.31.cloned.1.call-done = f32[16,14]{1,0:T(8,128)} async-done(((f32[2048,14]{1,0:T(8,128)}), f32[16,14]{1,0:T(8,128)}) %reduce-scatter.31.cloned.1.call-update) | async-done | bytes 912
  (636 shorter events, 247.4 us)
Async XLA Ops:
  7.2 523.2 %copy-start = (bf16[448,2048]{1,0:T(8,128)(2,1)S(1)}, bf16[448,2048]{1,0:T(8,128)(2,1)}, u32[]{:S(2)}) copy-start(bf16[448,2048]{1,0:T(8,128)(2,1)} %param.18) | copy-start | bytes 5505028
  7.2 12.2 copy-start.79
  7.2 83.4 %all-gather.5.cloned.1.call-start = ((), (), s32[]{:S(2)}) async-start(), calls=%async_computation.12 | async-start | bytes 8912896 | tf_op jit(solution)/shard_map/all_gather | solution.py:144
  8.6 10.7 copy-start.90
  12.4 89.5 %copy-start.71 = (f32[1,2048]{1,0:T(1,128)}, f32[1,2048]{1,0:T(1,128)S(1)}, u32[]{:S(2)}) copy-start(f32[1,2048]{1,0:T(1,128)S(1)} %get-tuple-element.293) | copy-start | bytes 24580
  12.4 89.5 %copy-start.73 = (f32[1,2048]{1,0:T(1,128)}, f32[1,2048]{1,0:T(1,128)S(1)}, u32[]{:S(2)}) copy-start(f32[1,2048]{1,0:T(1,128)S(1)} %get-tuple-element.294) | copy-start | bytes 24580
  12.4 89.5 %copy-start.75 = (f32[1,2048]{1,0:T(1,128)}, f32[1,2048]{1,0:T(1,128)S(1)}, u32[]{:S(2)}) copy-start(f32[1,2048]{1,0:T(1,128)S(1)} %get-tuple-element.295) | copy-start | bytes 24580
  12.4 89.5 %copy-start.77 = (f32[1,2048]{1,0:T(1,128)}, f32[1,2048]{1,0:T(1,128)S(1)}, u32[]{:S(2)}) copy-start(f32[1,2048]{1,0:T(1,128)S(1)} %get-tuple-element.296) | copy-start | bytes 24580
  15.3 405.7 %reduce-scatter.13.cloned.1.call-start = ((), (), s32[]{:S(2)}) async-start(), calls=%async_computation.13 | async-start | bytes 17825792 | tf_op jit(solution)/shard_map/reduce_scatter | solution.py:193
  23.9 77.9 %copy-start.99 = (f32[64]{0:T(128)}, f32[64]{0:T(128)S(1)}, u32[]{:S(2)}) copy-start(f32[64]{0:T(128)S(1)} %broadcast_add_fusion) | copy-start | bytes 772
  24.0 77.9 %copy-start.101 = (f32[64]{0:T(128)}, f32[64]{0:T(128)S(1)}, u32[]{:S(2)}) copy-start(f32[64]{0:T(128)S(1)} %broadcast_subtract_fusion.6) | copy-start | bytes 772
  24.0 77.9 %copy-start.103 = (f32[64]{0:T(128)}, f32[64]{0:T(128)S(1)}, u32[]{:S(2)}) copy-start(f32[64]{0:T(128)S(1)} %iota_convert_fusion) | copy-start | bytes 772
  24.4 621.6 %copy-start.65 = (f32[2048]{0:T(1024)}, f32[2048]{0:T(1024)S(1)}, u32[]{:S(2)}) copy-start(f32[2048]{0:T(1024)S(1)} %add_convert_fusion.6) | copy-start | bytes 24580
  24.8 106.6 %copy-start.61 = (f32[32,64]{1,0:T(8,128)}, f32[32,64]{1,0:T(8,128)S(1)}, u32[]{:S(2)}) copy-start(f32[32,64]{1,0:T(8,128)S(1)} %get-tuple-element.311) | copy-start | bytes 24580
  24.8 221.0 %copy-start.59 = (f32[32,64]{1,0:T(8,128)}, f32[32,64]{1,0:T(8,128)S(1)}, u32[]{:S(2)}) copy-start(f32[32,64]{1,0:T(8,128)S(1)} %get-tuple-element.310) | copy-start | bytes 24580
  25.6 105.8 %copy-start.46 = (f32[64,2,64]{0,2,1:T(8,128)}, f32[64,2,64]{0,2,1:T(8,128)S(1)}, u32[]{:S(2)}) copy-start(f32[64,2,64]{0,2,1:T(8,128)S(1)} %get-tuple-element.313) | copy-start | bytes 98308
  25.6 212.9 %copy-start.48 = (f32[64,2,64]{0,2,1:T(8,128)}, f32[64,2,64]{0,2,1:T(8,128)S(1)}, u32[]{:S(2)}) copy-start(f32[64,2,64]{0,2,1:T(8,128)S(1)} %get-tuple-element.319) | copy-start | bytes 98308
  25.6 216.5 %copy-start.42 = (f32[64,2,64]{0,2,1:T(8,128)}, f32[64,2,64]{0,2,1:T(8,128)S(1)}, u32[]{:S(2)}) copy-start(f32[64,2,64]{0,2,1:T(8,128)S(1)} %get-tuple-element.312) | copy-start | bytes 98308
  25.9 219.8 %copy-start.20 = (f32[32,64,64]{2,1,0:T(8,128)}, f32[32,64,64]{2,1,0:T(8,128)S(1)}, u32[]{:S(2)}) copy-start(f32[32,64,64]{2,1,0:T(8,128)S(1)} %and_convert_fusion) | copy-start | bytes 1572868
  101.9 19.5 copy-start.53
  136.4 92.2 %copy-start.110 = (f32[2,64]{1,0:T(2,128)S(1)}, f32[2,64]{1,0:T(2,128)}, u32[]{:S(2)}) copy-start(f32[2,64]{1,0:T(2,128)} %mul.895) | copy-start | bytes 1540
  228.5 10.0 copy-start.69
  228.5 10.0 copy-start.107
  228.6 10.0 copy-start.8
  275.4 145.6 %copy-start.22 = (bf16[128,2048]{1,0:T(8,128)(2,1)S(1)}, bf16[128,2048]{1,0:T(8,128)(2,1)}, u32[]{:S(2)}) copy-start(bf16[128,2048]{1,0:T(8,128)(2,1)} %param.13) | copy-start | bytes 1572868
  275.4 147.2 %copy-start.89 = (f32[1,2048]{1,0:T(1,128)S(1)}, f32[1,2048]{1,0:T(1,128)}, u32[]{:S(2)}) copy-start(f32[1,2048]{1,0:T(1,128)} %get-tuple-element.291) | copy-start | bytes 24580
  275.4 219.2 %all-gather.7.cloned.1.call-start = ((), (), s32[]{:S(2)}) async-start(), calls=%async_computation.14 | async-start | bytes 8912896 | tf_op jit(solution)/shard_map/all_gather | solution.py:201
  423.7 82.2 %copy-start.80 = (f32[1,2048]{1,0:T(1,128)S(1)}, f32[1,2048]{1,0:T(1,128)}, u32[]{:S(2)}) copy-start(f32[1,2048]{1,0:T(1,128)} %get-tuple-element.300) | copy-start | bytes 24580
  423.7 214.0 %reduce-scatter.15.cloned.1.call-start = ((), (), s32[]{:S(2)}) async-start(), calls=%async_computation.15 | async-start | bytes 8912896 | tf_op jit(solution)/shard_map/reduce_scatter | solution.py:209
  505.9 18.5 copy-start.114
  537.3 180.1 %all-gather.9.cloned.1.call-start = ((), (), s32[]{:S(2)}) async-start(), calls=%async_computation.16 | async-start | bytes 8912896 | tf_op jit(solution)/shard_map/all_gather | solution.py:227
  645.8 218.9 %reduce-scatter.17.cloned.1.call-start = ((), (), s32[]{:S(2)}) async-start(), calls=%async_computation.17 | async-start | bytes 8912896 | tf_op jit(solution)/shard_map/reduce_scatter | solution.py:240
  717.3 9.6 copy-start.115
  717.3 17.7 slice-start
  717.3 17.7 slice-start.1
  717.3 17.7 slice-start.2
  735.0 13.4 copy-start.87
  735.1 13.4 copy-start.88
  764.2 177.4 %all-gather.11.cloned.1.call-start = ((), (), s32[]{:S(2)}) async-start(), calls=%async_computation.18 | async-start | bytes 8912896 | tf_op jit(solution)/shard_map/all_gather | solution.py:246
  870.1 374.9 %reduce-scatter.29.cloned.1.call-start = ((), (), s32[]{:S(2)}) async-start(), calls=%async_computation.24 | async-start | bytes 589824 | tf_op jit(solution)/shard_map/reduce_scatter | solution.py:367
  877.1 369.4 %reduce-scatter.27.cloned.1.call-start = ((), (), s32[]{:S(2)}) async-start(), calls=%async_computation.23 | async-start | bytes 2064384 | tf_op jit(solution)/shard_map/reduce_scatter | solution.py:364
  887.4 360.9 %reduce-scatter.25.cloned.1.call-start = ((), (), s32[]{:S(2)}) async-start(), calls=%async_computation.22 | async-start | bytes 2064384 | tf_op jit(solution)/shard_map/reduce_scatter | solution.py:361
  898.8 42.8 %copy-start.30 = (f32[2048,128]{0,1:T(8,128)S(1)}, f32[2048,128]{0,1:T(8,128)}, u32[]{:S(2)}) copy-start(f32[2048,128]{0,1:T(8,128)} %copy-done.29) | copy-start | bytes 3145732
  898.8 42.8 %copy-start.45 = (bf16[128,2048]{1,0:T(8,128)(2,1)S(1)}, bf16[128,2048]{1,0:T(8,128)(2,1)}, u32[]{:S(2)}) copy-start(bf16[128,2048]{1,0:T(8,128)(2,1)} %param.16) | copy-start | bytes 1572868
  898.8 355.6 %reduce-scatter.23.cloned.1.call-start = ((), (), s32[]{:S(2)}) async-start(), calls=%async_computation.21 | async-start | bytes 589824 | tf_op jit(solution)/shard_map/reduce_scatter | solution.py:358
  973.1 92.0 %copy-start.49 = (f32[64,2,64]{0,2,1:T(8,128)S(1)}, f32[64,2,64]{0,2,1:T(8,128)}, u32[]{:S(2)}) copy-start(f32[64,2,64]{0,2,1:T(8,128)} %copy-done.48) | copy-start | bytes 98308
  1139.7 116.3 %reduce-scatter.21.cloned.1.call-start = ((), (), s32[]{:S(2)}) async-start(), calls=%async_computation.20 | async-start | bytes 2359296 | tf_op jit(solution)/shard_map/reduce_scatter | solution.py:355
  1156.4 30.9 %copy-start.66 = (f32[2048]{0:T(1024)S(1)}, f32[2048]{0:T(1024)}, u32[]{:S(2)}) copy-start(f32[2048]{0:T(1024)} %copy-done.65) | copy-start | bytes 24580
  1156.4 30.9 %copy-start.83 = (f32[1,2048]{1,0:T(1,128)S(1)}, f32[1,2048]{1,0:T(1,128)}, u32[]{:S(2)}) copy-start(f32[1,2048]{1,0:T(1,128)} %get-tuple-element.285) | copy-start | bytes 24580
  1156.5 30.9 %copy-start.84 = (f32[1,2048]{1,0:T(1,128)S(1)}, f32[1,2048]{1,0:T(1,128)}, u32[]{:S(2)}) copy-start(f32[1,2048]{1,0:T(1,128)} %get-tuple-element.286) | copy-start | bytes 24580
  1156.5 30.9 %copy-start.85 = (f32[1,2048]{1,0:T(1,128)S(1)}, f32[1,2048]{1,0:T(1,128)}, u32[]{:S(2)}) copy-start(f32[1,2048]{1,0:T(1,128)} %get-tuple-element.287) | copy-start | bytes 24580
  1156.5 30.9 %copy-start.86 = (f32[1,2048]{1,0:T(1,128)S(1)}, f32[1,2048]{1,0:T(1,128)}, u32[]{:S(2)}) copy-start(f32[1,2048]{1,0:T(1,128)} %get-tuple-element.288) | copy-start | bytes 24580
  1156.5 189.2 %reduce-scatter.19.cloned.1.call-start = ((), (), s32[]{:S(2)}) async-start(), calls=%async_computation.19 | async-start | bytes 8912896 | tf_op jit(solution)/shard_map/reduce_scatter | solution.py:323
  1244.9 741.6 %reduce-scatter.31.cloned.1.call-start = ((), (), s32[]{:S(2)}) async-start(), calls=%async_computation.25 | async-start | bytes 1056768
  1250.0 95.6 %copy-start.23 = (bf16[128,2048]{1,0:T(8,128)(2,1)S(1)}, bf16[128,2048]{1,0:T(8,128)(2,1)}, u32[]{:S(2)}) copy-start(bf16[128,2048]{1,0:T(8,128)(2,1)} %param.13) | copy-start | bytes 1572868
  1250.0 95.6 %copy-start.64 = (f32[1,2048]{1,0:T(1,128)S(1)}, f32[1,2048]{1,0:T(1,128)}, u32[]{:S(2)}) copy-start(f32[1,2048]{1,0:T(1,128)} %copy-done.63) | copy-start | bytes 24580
  1250.1 95.6 %copy-start.91 = (f32[128]{0:T(128)S(1)}, f32[128]{0:T(128)}, u32[]{:S(2)}) copy-start(f32[128]{0:T(128)} %copy-done.90) | copy-start | bytes 1540
  1253.3 93.8 %copy-start.113 = (f32[128]{0:T(128)S(1)}, f32[128]{0:T(128)}, u32[]{:S(2)}) copy-start(f32[128]{0:T(128)} %copy-done.112) | copy-start | bytes 1540
  1253.3 93.8 %copy-start.97 = (f32[128]{0:T(128)S(1)}, f32[128]{0:T(128)}, u32[]{:S(2)}) copy-start(f32[128]{0:T(128)} %copy-done.96) | copy-start | bytes 1540
  1253.4 95.4 %copy-start.81 = (f32[2048]{0:T(1024)S(1)}, f32[2048]{0:T(1024)}, u32[]{:S(2)}) copy-start(f32[2048]{0:T(1024)} %get-tuple-element.214) | copy-start | bytes 24580
  1253.4 95.4 %copy-start.82 = (f32[2048]{0:T(1024)S(1)}, f32[2048]{0:T(1024)}, u32[]{:S(2)}) copy-start(f32[2048]{0:T(1024)} %get-tuple-element.220) | copy-start | bytes 24580
  1257.8 92.6 %copy-start.28 = (f32[128,2048]{1,0:T(8,128)S(1)}, f32[128,2048]{1,0:T(8,128)}, u32[]{:S(2)}) copy-start(f32[128,2048]{1,0:T(8,128)} %copy-done.27) | copy-start | bytes 3145732
  1257.8 92.6 %copy-start.106 = (f32[128]{0:T(128)S(1)}, f32[128]{0:T(128)}, u32[]{:S(2)}) copy-start(f32[128]{0:T(128)} %copy-done.105) | copy-start | bytes 1540
  1350.4 637.6 %copy-start.1 = (bf16[448,2048]{1,0:T(8,128)(2,1)S(1)}, bf16[448,2048]{1,0:T(8,128)(2,1)}, u32[]{:S(2)}) copy-start(bf16[448,2048]{1,0:T(8,128)(2,1)} %param.18) | copy-start | bytes 5505028
  (72 other events, 313.1 us)
Sparse Core Ops, SparseCore 0:
  15.4 75.1 all-gather.4
  275.5 145.3 reduce-scatter.12
  424.2 70.4 all-gather.6
  537.4 100.3 reduce-scatter.14
  646.0 71.3 all-gather.8
  764.4 100.3 reduce-scatter.16
  870.2 71.3 all-gather.10
  944.1 35.5 reduce-scatter.28
  982.1 45.7 reduce-scatter.26
  1030.2 48.0 reduce-scatter.24
  1139.8 35.7 reduce-scatter.22
  1178.0 49.5 reduce-scatter.20
  1245.1 100.5 reduce-scatter.18
  1350.5 636.0 reduce-scatter.30
where the time goes:
time: 2010 us; the launch traced here: 1990 us
  waiting for transfers between devices  1270 us (63%)
  other arithmetic  338 us (17%)
  matrix products  230 us (11%)
  local copies, waits for them, and re-layouts  105 us (5%)
  blocking collectives  31.6 us (2%)
    unnamed x15, waiting for transfers between devices  634 us
    reduce_scatter x1, waiting for transfers between devices, body(): lax.psum_scatter(jnp.dot(gated, out_weight, preferred_element_type=jnp.fl...  145 us
    dot_general x16, matrix products, contract(): lax.dot_general(left, right, (((left_dim,), (right_dim,)), ((), ())), pre...  124 us
    reduce_scatter x1, waiting for transfers between devices, body(): lax.psum_scatter(grad_first.astype(jnp.bfloat16), 'sp', scatter_dimension...  87.9 us
    reduce_scatter x1, waiting for transfers between devices, body(): lax.psum_scatter(grad_second.astype(jnp.bfloat16), 'sp', scatter_dimensio...  82.9 us
    reduce_scatter x1, waiting for transfers between devices, body(): lax.psum_scatter(jnp.dot(squared, value_weight, preferred_element_type=jn...  81.9 us
    all_gather x1, waiting for transfers between devices, body(): lax.all_gather(normed_two.astype(jnp.bfloat16), 'sp', axis=0, tiled=True)  70.9 us
    all_gather x1, waiting for transfers between devices, body(): lax.all_gather(normed.astype(jnp.bfloat16), 'sp', axis=0, tiled=True)  64.7 us
  transfers between devices with their start and end apart: 14, of which 9 were waited for; matrix products, arithmetic and copies ran while one was open for 18% of the time, Pallas kernels for 0%

commit v1 on v0

v1 whole, which is shorter than its diff:
```python
import functools

import jax
import jax.numpy as jnp
from jax import lax
from jax.experimental import pallas as pl
from jax.experimental.pallas import tpu as pltpu
from jax.sharding import PartitionSpec as P

MESH = pl.DeviceIdType.MESH
VMEM = pltpu.VMEM
DMA = pltpu.SemaphoreType.DMA

ATTENTION_WIDTH = 64
SPAN = 64


class Place:
    def __init__(self):
        self.dp = lax.axis_index("dp")
        s = lax.axis_index("sp")
        self.s = s
        self.x, self.z, self.c = s // 4, (s // 2) % 2, s % 2

    def at(self, dx=0, dz=0, dc=0):
        x = (self.x + dx) % 4
        z = (self.z + dz) % 2
        c = (self.c + dc) % 2
        return x * 4 + z * 2 + c

    def dev(self, s):
        return (self.dp, s)


def greet(place, peers):
    barrier = pltpu.get_barrier_semaphore()
    for peer in peers:
        pl.semaphore_signal(barrier, inc=1, device_id=place.dev(peer), device_id_type=MESH)
    pl.semaphore_wait(barrier, len(peers))


def ag_kernel(a_ref, o_ref, ss, rs, ls):
    p = Place()
    R = a_ref.shape[0]
    H = R // 2
    here, core = p.at(), p.at(dc=1)
    xp, xm, zz = p.at(dx=1), p.at(dx=-1), p.at(dz=1)
    greet(p, [core, xp, xm, zz])

    def rows(s, off=0, n=R):
        return o_ref.at[pl.ds(pl.multiple_of(s * R + off, 16), n)]

    def send(k, src, dst, to):
        cp = pltpu.make_async_remote_copy(src_ref=src, dst_ref=dst, send_sem=ss.at[k], recv_sem=rs.at[k], device_id=p.dev(to), device_id_type=MESH)
        cp.start()
        sent.append(cp)

    def landed(k, ref):
        pltpu.make_async_remote_copy(src_ref=ref, dst_ref=ref, send_sem=ss.at[k], recv_sem=rs.at[k], device_id=p.dev(here), device_id_type=MESH).wait_recv()

    sent = []
    own = pltpu.make_async_copy(a_ref, rows(here), ls.at[0])
    own.start()
    send(0, a_ref, rows(here), xp)
    send(1, a_ref, rows(here), xm)
    send(2, a_ref, rows(here), zz)
    send(3, a_ref, rows(here), core)
    b_xm, b_xp, b_z = p.at(dx=-1), p.at(dx=1), p.at(dz=1)
    b_d2 = p.at(dx=2)
    landed(0, rows(b_xm))
    send(4, rows(b_xm, 0, H), rows(b_xm, 0, H), xp)
    landed(1, rows(b_xp))
    send(5, rows(b_xp, H, H), rows(b_xp, H, H), xm)
    send(6, rows(b_xm), rows(b_xm), core)
    send(7, rows(b_xp), rows(b_xp), core)
    landed(2, rows(b_z))
    send(8, rows(b_z), rows(b_z), xp)
    send(9, rows(b_z), rows(b_z), xm)
    send(10, rows(b_z), rows(b_z), core)
    landed(4, rows(b_d2, 0, H))
    send(11, rows(b_d2, 0, H), rows(b_d2, 0, H), zz)
    landed(5, rows(b_d2, H, H))
    send(12, rows(b_d2, H, H), rows(b_d2, H, H), zz)
    send(13, rows(b_d2), rows(b_d2), core)
    b_zxm, b_zxp, b_zd2 = p.at(dx=-1, dz=1), p.at(dx=1, dz=1), p.at(dx=2, dz=1)
    landed(8, rows(b_zxm))
    send(14, rows(b_zxm), rows(b_zxm), core)
    landed(9, rows(b_zxp))
    send(15, rows(b_zxp), rows(b_zxp), core)
    landed(11, rows(b_zd2, 0, H))
    send(16, rows(b_zd2, 0, H), rows(b_zd2, 0, H), core)
    landed(12, rows(b_zd2, H, H))
    send(17, rows(b_zd2, H, H), rows(b_zd2, H, H), core)
    o = lambda **k: p.at(dc=1, **k)
    landed(3, rows(core))
    landed(6, rows(o(dx=-1)))
    landed(7, rows(o(dx=1)))
    landed(10, rows(o(dz=1)))
    landed(13, rows(o(dx=2)))
    landed(14, rows(o(dx=-1, dz=1)))
    landed(15, rows(o(dx=1, dz=1)))
    landed(16, rows(o(dx=2, dz=1), 0, H))
    landed(17, rows(o(dx=2, dz=1), H, H))
    own.wait()
    for cp in sent:
        cp.wait_send()


def all_gather(a, cid):
    R, C = a.shape
    return pl.pallas_call(
        ag_kernel,
        out_shape=jax.ShapeDtypeStruct((16 * R, C), a.dtype),
        in_specs=[pl.BlockSpec(memory_space=pl.ANY)],
        out_specs=pl.BlockSpec(memory_space=pl.ANY),
        scratch_shapes=[DMA((18,)), DMA((18,)), DMA((1,))],
        compiler_params=pltpu.CompilerParams(collective_id=cid, has_side_effects=True),
        name="gather_tokens",
    )(a)


def rs_kernel(a_hbm, o_ref, pa, cb, zt, xs, zf, hv, xf, ss, rs, ls):
    p = Place()
    R = o_ref.shape[0]
    H = R // 2
    here, core = p.at(), p.at(dc=1)
    xp, xm, zz = p.at(dx=1), p.at(dx=-1), p.at(dz=1)
    f32, bf = jnp.float32, jnp.bfloat16
    order = [(2, 1), (-1, 1), (1, 1), (2, 0), (0, 1), (1, 0), (-1, 0), (0, 0)]
    loads = []
    for i, (dx, dz) in enumerate(order):
        for j, dc in enumerate((1, 0)):
            b = p.at(dx, dz, dc)
            cp = pltpu.make_async_copy(a_hbm.at[pl.ds(pl.multiple_of(b * R, 16), R)], pa.at[i, j], ls.at[2 * i + j])
            cp.start()
            loads.append(cp)
    greet(p, [core, xp, xm, zz])
    sent = []

    def send(k, src, dst, to):
        cp = pltpu.make_async_remote_copy(src_ref=src, dst_ref=dst, send_sem=ss.at[k], recv_sem=rs.at[k], device_id=p.dev(to), device_id_type=MESH)
        cp.start()
        sent.append(cp)

    def landed(k, ref):
        pltpu.make_async_remote_copy(src_ref=ref, dst_ref=ref, send_sem=ss.at[k], recv_sem=rs.at[k], device_id=p.dev(here), device_id_type=MESH).wait_recv()

    for i in range(8):
        loads[2 * i].wait()
        send(i, pa.at[i, 0], cb.at[i], core)

    def pair(i):
        loads[2 * i + 1].wait()
        landed(i, cb.at[i])
        pa[i, 1] = (pa[i, 1].astype(f32) + cb[i].astype(f32)).astype(bf)

    upper, lower = pl.ds(0, H), pl.ds(H, H)
    pair(0)
    send(8, pa.at[0, 1], zt, zz)
    pair(1)
    send(9, pa.at[1, 1], xs.at[1], xm)
    pair(2)
    send(10, pa.at[2, 1], xs.at[0], xp)
    pair(3)
    pair(4)
    pair(5)
    send(11, pa.at[5, 1, lower], xf.at[0, lower], xp)
    pair(6)
    send(12, pa.at[6, 1, upper], xf.at[1, upper], xm)
    pair(7)
    landed(8, zt)
    pa[3, 1] = (pa[3, 1].astype(f32) + zt[...].astype(f32)).astype(bf)
    send(13, pa.at[3, 1, upper], hv.at[0], xp)
    send(14, pa.at[3, 1, lower], hv.at[1], xm)
    landed(9, xs.at[1])
    landed(10, xs.at[0])
    pa[4, 1] = (pa[4, 1].astype(f32) + xs[0].astype(f32) + xs[1].astype(f32)).astype(bf)
    send(15, pa.at[4, 1], zf, zz)
    landed(13, hv.at[0])
    pa[5, 1, upper] = (pa[5, 1, upper].astype(f32) + hv[0].astype(f32)).astype(bf)
    send(16, pa.at[5, 1, upper], xf.at[0, upper], xp)
    landed(14, hv.at[1])
    pa[6, 1, lower] = (pa[6, 1, lower].astype(f32) + hv[1].astype(f32)).astype(bf)
    send(17, pa.at[6, 1, lower], xf.at[1, lower], xm)
    landed(15, zf)
    landed(11, xf.at[0, lower])
    landed(12, xf.at[1, upper])
    landed(16, xf.at[0, upper])
    landed(17, xf.at[1, lower])
    o_ref[...] = pa[7, 1].astype(f32) + zf[...].astype(f32) + xf[0].astype(f32) + xf[1].astype(f32)
    for cp in sent:
        cp.wait_send()


def reduce_scatter(a, cid):
    R, C = a.shape[0] // 16, a.shape[1]
    bf = jnp.bfloat16
    return pl.pallas_call(
        rs_kernel,
        out_shape=jax.ShapeDtypeStruct((R, C), jnp.float32),
        in_specs=[pl.BlockSpec(memory_space=pl.ANY)],
        out_specs=pl.BlockSpec(memory_space=VMEM),
        scratch_shapes=[
            VMEM((8, 2, R, C), bf), VMEM((8, R, C), bf), VMEM((R, C), bf), VMEM((2, R, C), bf), VMEM((R, C), bf),
            VMEM((2, R // 2, C), bf), VMEM((2, R, C), bf), DMA((18,)), DMA((18,)), DMA((16,)),
        ],
        compiler_params=pltpu.CompilerParams(collective_id=cid, has_side_effects=True, vmem_limit_bytes=40 * 2**20),
        name="sum_tokens",
    )(a)


def swap_kernel(a_ref, o_ref, ss, rs, ls):
    p = Place()
    n = 16
    greet(p, [(p.s + k) % n for k in range(1, n)])
    cps = []
    for k in range(1, n):
        to = (p.s + k) % n
        cp = pltpu.make_async_remote_copy(src_ref=a_ref.at[to], dst_ref=o_ref.at[p.s], send_sem=ss.at[k], recv_sem=rs.at[k], device_id=p.dev(to), device_id_type=MESH)
        cp.start()
        cps.append(cp)
    own = pltpu.make_async_copy(a_ref.at[p.s], o_ref.at[p.s], ls.at[0])
    own.start()
    own.wait()
    for cp in cps:
        cp.wait()


def swap(a, cid, space=VMEM):
    n = a.shape[0]
    return pl.pallas_call(
        swap_kernel,
        out_shape=jax.ShapeDtypeStruct(a.shape, a.dtype),
        in_specs=[pl.BlockSpec(memory_space=space)],
        out_specs=pl.BlockSpec(memory_space=space),
        scratch_shapes=[DMA((n,)), DMA((n,)), DMA((1,))],
        compiler_params=pltpu.CompilerParams(collective_id=cid, has_side_effects=True),
        name="swap_blocks",
    )(a)


def vec_kernel(nd, a_ref, o_ref, b1, t1, b2, ss, rs, ss2, rs2):
    p = Place()
    n = 16
    d = p.dp
    barrier = pltpu.get_barrier_semaphore()
    for k in range(1, n):
        pl.semaphore_signal(barrier, inc=1, device_id=(d, (p.s + k) % n), device_id_type=MESH)
    for k in range(1, nd):
        pl.semaphore_signal(barrier, inc=1, device_id=((d + k) % nd, p.s), device_id_type=MESH)
    pl.semaphore_wait(barrier, n + nd - 2)
    cps = []
    for k in range(1, n):
        to = (p.s + k) % n
        cp = pltpu.make_async_remote_copy(src_ref=a_ref.at[to], dst_ref=b1.at[k - 1], send_sem=ss.at[k], recv_sem=rs.at[k], device_id=(d, to), device_id_type=MESH)
        cp.start()
        cps.append(cp)
    total = a_ref[p.s]
    for k in range(1, n):
        cps[k - 1].wait_recv()
        total = total + b1[k - 1]
    t1[...] = total
    cps2 = []
    for k in range(1, nd):
        to = (d + k) % nd
        cp = pltpu.make_async_remote_copy(src_ref=t1.at[to], dst_ref=b2.at[k - 1], send_sem=ss2.at[k], recv_sem=rs2.at[k], device_id=(to, p.s), device_id_type=MESH)
        cp.start()
        cps2.append(cp)
    acc = t1[d]
    for k in range(1, nd):
        cps2[k - 1].wait_recv()
        acc = acc + b2[k - 1]
    o_ref[...] = acc
    for cp in cps + cps2:
        cp.wait_send()


def vec_sum(a, cid):
    n, nd = a.shape[:2]
    piece = a.shape[2:]
    return pl.pallas_call(
        functools.partial(vec_kernel, nd),
        out_shape=jax.ShapeDtypeStruct(piece, a.dtype),
        in_specs=[pl.BlockSpec(memory_space=VMEM)],
        out_specs=pl.BlockSpec(memory_space=VMEM),
        scratch_shapes=[VMEM((n - 1, nd) + piece, a.dtype), VMEM((nd,) + piece, a.dtype), VMEM((max(nd - 1, 1),) + piece, a.dtype), DMA((n,)), DMA((n,)), DMA((nd,)), DMA((nd,))],
        compiler_params=pltpu.CompilerParams(collective_id=cid, has_side_effects=True),
        name="sum_vectors",
    )(a)


highest = lax.Precision.HIGHEST
BF = jnp.bfloat16
F32 = jnp.float32


def layer_norm(tensor, gain_row, bias_row):
    center = tensor - jnp.mean(tensor, axis=-1, keepdims=True)
    spread = jnp.mean(center * center, axis=-1, keepdims=True)
    return center * lax.rsqrt(spread + 1e-05) * gain_row + bias_row


def head_norm(tensor, gain_row, bias_row):
    tokens = tensor.shape[0]
    grouped = tensor.reshape(tokens, -1, ATTENTION_WIDTH)
    center = grouped - jnp.mean(grouped, axis=-1, keepdims=True)
    spread = jnp.mean(center * center, axis=-1, keepdims=True)
    return (center * lax.rsqrt(spread + 0.00064)).reshape(tokens, -1) * gain_row + bias_row


def gate_out(mixed_time, projected, gain_row, bias_row):
    return head_norm(mixed_time, gain_row, bias_row) * jax.nn.silu(projected)


def later(tensor):
    return jnp.concatenate([jnp.zeros_like(tensor[:1]), tensor[:-1]], axis=0)


def earlier(tensor):
    return jnp.concatenate([tensor[1:], jnp.zeros_like(tensor[:1])], axis=0)


def contract(left, right, left_dim, right_dim):
    return lax.dot_general(left, right, (((left_dim,), (right_dim,)), ((), ())), preferred_element_type=F32)


def scan_kernel(reverse, keep_ref, decay_ref, add_ref, out_ref):
    blocks = add_ref.shape[0]

    def step(i, state):
        at = blocks - 1 - i if reverse else i
        out_ref[at] = state
        return add_ref[at] + keep_ref[at] * decay_ref[...] * state

    lax.fori_loop(0, blocks, step, jnp.zeros(add_ref.shape[1:], F32))


def state_scan(keep, decay, add, reverse):
    return pl.pallas_call(
        functools.partial(scan_kernel, reverse),
        out_shape=jax.ShapeDtypeStruct(add.shape, F32),
        in_specs=[pl.BlockSpec(memory_space=pltpu.SMEM), pl.BlockSpec(memory_space=VMEM), pl.BlockSpec(memory_space=VMEM)],
        out_specs=pl.BlockSpec(memory_space=VMEM),
        name="scan_states",
    )(keep, decay, add)


def block_output(memory, prior, r, k, v, seq, lam, bonus):
    length = r.shape[0]
    position = jnp.arange(length)
    offsets = position.astype(F32)[:, None, None]
    r_scaled = r * jnp.exp(lam[None] * offsets)
    k_scaled = k * jnp.exp(-lam[None] * (offsets + 1.0))
    scores = jnp.einsum("ihc,jhc->hij", r_scaled, k_scaled, precision=highest)
    block_mask = ((position[None, :] < position[:, None]) & (seq[None, :] == seq[:, None])).astype(F32)
    scores = scores * block_mask[None]
    reward = jnp.sum(r * k * bonus[None], axis=-1)
    kept = (seq == prior).astype(F32)
    out = jnp.einsum("hij,jhe->ihe", scores, v, precision=highest)
    out = out + reward[:, :, None] * v
    return out + kept[:, None, None] * jnp.einsum("ihc,hce->ihe", r_scaled, memory, precision=highest)


def block_carry(prior, k, v, seq, lam):
    length = k.shape[0]
    offsets = jnp.arange(length).astype(F32)[:, None, None]
    last = seq[length - 1]
    tail = (seq == last).astype(F32)
    carried = (last == prior).astype(F32)
    k_end = k * jnp.exp(lam[None] * (length - 1.0 - offsets)) * tail[:, None, None]
    return (carried, jnp.einsum("jhc,jhe->hce", k_end, v, precision=highest))


def block_whole(memory, prior, r, k, v, seq, lam, bonus):
    out = block_output(memory, prior, r, k, v, seq, lam, bonus)
    carried, kv_end = block_carry(prior, k, v, seq, lam)
    decay = jnp.exp(lam * r.shape[0])
    return (carried * decay[:, :, None] * memory + kv_end, out)


def body(nd, inputs, cotangent, mix_weights, out_weight, key_weight, value_weight, recept_weight, vectors, segment_ids):
    tokens, width = inputs.shape
    group = segment_ids.shape[0]
    cols = mix_weights.shape[2]
    heads = cols // ATTENTION_WIDTH
    s = lax.axis_index("sp")
    ring = group // tokens
    own = lax.dynamic_slice_in_dim(vectors, s * cols, cols, 1)
    same = jnp.concatenate([jnp.zeros((1,), F32), (segment_ids[1:] == segment_ids[:-1]).astype(F32)])
    same_next = earlier(same)
    here = s * tokens
    same_here = lax.dynamic_slice_in_dim(same, here, tokens, 0)[:, None]
    mu = vectors[2:6]
    nu_k, nu_r = vectors[12], vectors[13]

    out_full = lax.all_gather(out_weight, "sp", axis=0, tiled=True)
    recept_full = lax.all_gather(recept_weight, "sp", axis=0)
    recept_full = recept_full.transpose(1, 0, 2).reshape(width, width)

    mix_f = mix_weights.astype(F32)
    folded = jnp.concatenate(
        [((1.0 - mu)[:, :, None] * mix_f).astype(BF), (mu[:, :, None] * mix_f).astype(BF)], axis=0
    )
    folded = folded.transpose(1, 0, 2).reshape(width, 8 * cols)
    x = inputs.astype(F32)
    n1 = layer_norm(x, vectors[0], vectors[1]).astype(BF)
    n1_all = all_gather(n1, 0)
    half = 4 * cols
    n1_f = n1_all.astype(F32)
    shift_one = later(n1_f) * same[:, None] - n1_f
    r, k, v, p = (
        jnp.dot((n1_f + shift_one * mu[q]).astype(BF), mix_weights[q], preferred_element_type=F32) for q in range(4)
    )

    blocks = group // SPAN
    shape_blk = (blocks, SPAN, heads, ATTENTION_WIDTH)
    lam = -jnp.exp(own[6]).reshape(heads, ATTENTION_WIDTH)
    bonus = own[7].reshape(heads, ATTENTION_WIDTH)
    seg_blk = segment_ids.reshape(blocks, SPAN)
    prior = jnp.concatenate([jnp.full((1,), -1, jnp.int32), seg_blk[:-1, SPAN - 1]])
    r_blk, k_blk, v_blk = r.reshape(shape_blk), k.reshape(shape_blk), v.reshape(shape_blk)
    decay = jnp.exp(lam * SPAN)[:, :, None] * jnp.ones((1, 1, ATTENTION_WIDTH), F32)
    carried, kv_end = jax.vmap(block_carry, in_axes=(0, 0, 0, 0, None))(prior, k_blk, v_blk, seg_blk, lam)
    states = state_scan(carried, decay, kv_end, False)
    out_blk = jax.vmap(block_output, in_axes=(0, 0, 0, 0, 0, 0, None, None))(
        states, prior, r_blk, k_blk, v_blk, seg_blk, lam, bonus
    )
    mixed_time = out_blk.reshape(group, cols)
    z = gate_out(mixed_time, p, own[8], own[9]).astype(BF)

    z_here = swap(z.reshape(ring, tokens, cols), 1).transpose(1, 0, 2).reshape(tokens, width)
    hidden = x + jnp.dot(z_here, out_full, preferred_element_type=F32)
    n2 = layer_norm(hidden, vectors[10], vectors[11]).astype(BF)

    n2_all = all_gather(n2, 2)
    shift_all = later(n2_all).astype(F32) * same[:, None] - n2_all.astype(F32)
    key_in = (n2_all.astype(F32) + shift_all * nu_k).astype(BF)
    before = lax.dynamic_slice_in_dim(n2_all, jnp.maximum(here - 1, 0), 1, 0)
    n2_f = n2.astype(F32)
    shift_here = jnp.concatenate([before, n2[:-1]], axis=0).astype(F32) * same_here - n2_f
    recept_in = (n2_f + shift_here * nu_r).astype(BF)
    key_pre = jnp.dot(key_in, key_weight, preferred_element_type=F32)
    lifted = jax.nn.relu(key_pre)
    squared = jnp.square(lifted).astype(BF)
    value_part = jnp.dot(squared, value_weight, preferred_element_type=F32).astype(BF)
    value_here = reduce_scatter(value_part, 3)
    gate = jax.nn.sigmoid(jnp.dot(recept_in, recept_full, preferred_element_type=F32))
    channel = (gate * value_here).astype(BF)
    result = (hidden + channel.astype(F32)).astype(BF)

    g = cotangent.astype(F32)
    grad_value = (g * gate).astype(BF)
    grad_recept = (g * value_here * (gate * (1.0 - gate))).astype(BF)
    grad_value_all = all_gather(grad_value, 4)
    grad_sq = contract(grad_value_all, value_weight, 1, 1)
    grad_key = (grad_sq * 2.0 * lifted).astype(BF)
    key_back = reduce_scatter(contract(grad_key, key_weight, 1, 1).astype(BF), 5)
    value_grad = contract(squared, grad_value_all, 0, 0)
    key_grad = contract(key_in, grad_key, 0, 0)
    recept_cols = swap(grad_recept.reshape(tokens, ring, cols).transpose(1, 0, 2), 6).reshape(group, cols)
    recept_two = jnp.concatenate([recept_cols, earlier(recept_cols) * same_next[:, None].astype(BF)], axis=1)
    recept_np = contract(n2_all, recept_two, 0, 0)
    recept_grad = (1.0 - nu_r)[:, None] * recept_np[:, :cols] + nu_r[:, None] * recept_np[:, cols:]
    recept_back = contract(grad_recept, recept_full, 1, 1)
    nu_k_grad = jnp.sum(key_back * shift_here, axis=0)
    nu_r_grad = jnp.sum(recept_back * shift_here, axis=0)
    moved = (key_back * nu_k + recept_back * nu_r) * same_here
    after = lax.ppermute(moved[:1], "sp", [(i, i - 1) for i in range(1, ring)])
    grad_n2 = key_back * (1.0 - nu_k) + recept_back * (1.0 - nu_r) + jnp.concatenate([moved[1:], after], axis=0)
    unused, pull_two = jax.vjp(layer_norm, hidden, vectors[10], vectors[11])
    grad_hidden, gain_two, bias_two = pull_two(grad_n2)
    grad_hidden = g + grad_hidden

    grad_hidden_b = grad_hidden.astype(BF)
    gz_here = contract(grad_hidden_b, out_full, 1, 1).astype(BF)
    gz = swap(gz_here.reshape(tokens, ring, cols).transpose(1, 0, 2), 7).reshape(group, cols).astype(F32)
    grad_hidden_all = lax.all_gather(grad_hidden_b, "sp", axis=0, tiled=True)
    unused, gate_pull = jax.vjp(gate_out, mixed_time, p, own[8], own[9])
    grad_time, grad_gate, gain_head, bias_head = gate_pull(gz)
    go_blk = grad_time.reshape(shape_blk)
    offsets = jnp.arange(SPAN).astype(F32)[:, None, None]
    kept_all = (seg_blk == prior[:, None]).astype(F32)
    read = r_blk * jnp.exp(lam[None] * offsets)[None] * kept_all[:, :, None, None]
    local = jnp.einsum("bihc,bihe->bhce", read, go_blk, precision=highest)
    state_grads = state_scan(carried, decay, local, True)

    def every_block(memory, r_in, k_in, v_in, lam_in, bonus_in):
        return jax.vmap(block_whole, in_axes=(0, 0, 0, 0, 0, 0, None, None))(
            memory, prior, r_in, k_in, v_in, seg_blk, lam_in, bonus_in
        )

    unused, block_pull = jax.vjp(every_block, states, r_blk, k_blk, v_blk, lam, bonus)
    unused, gr, gk, gv, lam_grad, bonus_grad = block_pull((state_grads, go_blk))
    decay_grad = (lam_grad * lam).reshape(cols)
    grads = jnp.concatenate([t.reshape(group, cols).astype(BF) for t in (gr, gk, gv, grad_gate)], axis=1)
    grads_two = jnp.concatenate([grads, earlier(grads) * same_next[:, None].astype(BF)], axis=1)
    n1_part = contract(grads_two, folded, 1, 1).astype(BF)
    mix_np = contract(n1_all, grads_two, 0, 0)
    mix_n = mix_np[:, :half].reshape(width, 4, cols).transpose(1, 0, 2)
    mix_p = mix_np[:, half:].reshape(width, 4, cols).transpose(1, 0, 2)
    mix_d = mix_p - mix_n
    mix_grad = mix_n + mu[:, :, None] * mix_d
    mu_grads = jnp.sum(mix_f * mix_d, axis=2)
    n1_back = reduce_scatter(n1_part, 8)
    out_grad = contract(z, grad_hidden_all, 0, 0)
    unused, pull_one = jax.vjp(layer_norm, x, vectors[0], vectors[1])
    grad_x, gain_one, bias_one = pull_one(n1_back)
    input_grad = grad_hidden + grad_x

    def place(part):
        return lax.dynamic_update_slice_in_dim(jnp.zeros((width,), F32), part, s * cols, 0)

    terms = jnp.stack(
        [gain_one, bias_one, mu_grads[0], mu_grads[1], mu_grads[2], mu_grads[3]]
        + [place(t) for t in (decay_grad, bonus_grad.reshape(cols), gain_head, bias_head)]
        + [gain_two, bias_two, nu_k_grad, nu_r_grad]
    )
    rows, piece = terms.shape[0], width // (nd * ring)
    terms = terms.reshape(rows, nd, ring, piece).transpose(2, 1, 0, 3).reshape(ring, nd, rows * piece)
    packed = -(-rows * piece // 1024) * 1024
    terms = jnp.pad(terms, ((0, 0), (0, 0), (0, packed - rows * piece))).reshape(ring, nd, packed // 128, 128)
    vectors_grad = vec_sum(terms, 9).reshape(packed)[: rows * piece].reshape(rows, piece)

    def over_dp(grad, dim):
        return lax.psum_scatter(grad.astype(BF), "dp", scatter_dimension=dim, tiled=True).astype(F32)

    return (
        result,
        input_grad,
        over_dp(mix_grad, 1),
        over_dp(out_grad, 1),
        over_dp(key_grad, 0),
        over_dp(value_grad, 1),
        over_dp(recept_grad, 0),
        vectors_grad,
    )


def solution(mesh):
    placed = (
        P(("dp", "sp"), None),
        P(("dp", "sp"), None),
        P(None, None, "sp"),
        P("sp", None),
        P(None, "sp"),
        P("sp", None),
        P(None, "sp"),
        P(),
        P("dp"),
    )
    return jax.shard_map(
        functools.partial(body, mesh.shape["dp"]),
        mesh=mesh,
        in_specs=placed,
        out_specs=(
            P(("dp", "sp"), None),
            P(("dp", "sp"), None),
            P(None, "dp", "sp"),
            P("sp", "dp"),
            P("dp", "sp"),
            P("sp", "dp"),
            P("dp", "sp"),
            P(None, ("dp", "sp")),
        ),
        check_vma=False,
    )
```

time: 2010 us -> 762 us (0.38)
  waiting for transfers between devices: 1270 us -> 17.2 us
  Pallas kernels: 0 us -> 342 us
  other arithmetic: 338 us -> 79.3 us
  matrix products: 230 us -> 193 us
  blocking collectives: 31.6 us -> 0 us
    unnamed x15 -> x8, waiting for transfers between devices: 634 us -> 1.48 us
    reduce_scatter x9 -> x5, waiting for transfers between devices: 398 us -> 14.1 us  [over_dp(): lax.psum_scatter(grad.astype(BF), 'dp', scatter_dimension=dim, tiled=True)]
    pallas_call x0 -> x12, Pallas kernels: none -> 342 us  [the longest x3 137 us: all_gather(): pl.pallas_call(ag_kernel, out_shape=jax.ShapeDtypeStruct((16 * R, C), a.d...]
    all_gather x4 -> x3, waiting for transfers between devices: 239 us -> 0.02 us  [the longest x1 0.02 us: body(): grad_hidden_all = lax.all_gather(grad_hidden_b, 'sp', axis=0, tiled=True)]
    mul x67 -> x1, other arithmetic: 87.1 us -> 0.34 us  [body(): earlier(recept_cols) * same_next[:, None].astype(BF)]
    add x66 -> x2, other arithmetic: 62.3 us -> 2.99 us  [the longest x1 2.98 us: body(): input_grad = grad_hidden + grad_x]
    reduce_sum x6 -> x7, other arithmetic: 66.2 us -> 14.2 us  [the longest x1 4.81 us: block_output(): out = out + reward[:, :, None] * v]
    dot_general x16 -> x10, matrix products: 124 us -> 75.7 us  [contract(): lax.dot_general(left, right, (((left_dim,), (right_dim,)), ((), ())), pre...]
  transfers between devices with their start and end apart: 14 -> 9, of which waited for: 9 -> 2; matrix products, arithmetic and copies ran while one was open for 18% -> 41% of each run, Pallas kernels for 0% -> 25%
where the time goes in v1:
time: 762 us; the launch traced here: 756 us
  Pallas kernels  342 us (45%)
  matrix products  193 us (25%)
  local copies, waits for them, and re-layouts  106 us (14%)
  other arithmetic  79.3 us (10%)
  waiting for transfers between devices  17.2 us (2%)
  between operations  16.4 us (2%)
    pallas_call x3, Pallas kernels, all_gather(): pl.pallas_call(ag_kernel, out_shape=jax.ShapeDtypeStruct((16 * R, C), a.d...  137 us
    pallas_call x3, Pallas kernels, reduce_scatter(): pl.pallas_call(rs_kernel, out_shape=jax.ShapeDtypeStruct((R, C), jnp.floa...  131 us
    dot_general x10, matrix products, contract(): lax.dot_general(left, right, (((left_dim,), (right_dim,)), ((), ())), pre...  75.7 us
    pallas_call x3, Pallas kernels, swap(): pl.pallas_call(swap_kernel, out_shape=jax.ShapeDtypeStruct(a.shape, a.dty...  46 us
    dot_general x4, matrix products, body(): jnp.dot((n1_f + shift_one * mu[q]).astype(BF), mix_weights[q], preferred_...  35.4 us
    pallas_call x1, Pallas kernels, vec_sum(): pl.pallas_call(functools.partial(vec_kernel, nd), out_shape=jax.ShapeDtyp...  22.3 us
    unnamed x264, local copies, waits for them, and re-layouts  20.6 us
    dot_general x3, matrix products, block_carry(): return (carried, jnp.einsum('jhc,jhe->hce', k_end, v, precision=highest))  20.2 us
  transfers between devices with their start and end apart: 9, of which 2 were waited for; matrix products, arithmetic and copies ran while one was open for 41% of the time, Pallas kernels for 25%

profile of v1, /device:TPU:0, one launch (start us, length us, event | category | flops | bytes accessed | tf_op | source)
XLA Modules:
  0.0 756.3 jit_solution(5012259226831852242)
XLA Ops:
  11.6 2.3 slice_bitcast_fusion.1
  22.1 61.2 %gather_tokens.3 = bf16[2048,2048]{1,0:T(8,128)(2,1)} custom-call(bf16[128,2048]{1,0:T(8,128)(2,1)} %fusion.77.a_ref), custom_call_target="tpu_custom_call" | custom-call | tf_op jit(solution)/shard_map/gather_tokens/pallas_call | solution.py:111
  83.4 11.5 %slice.158 = f32[2047,2048]{1,0:T(8,128)} slice(bf16[2048,2048]{1,0:T(8,128)(2,1)} %gather_tokens.3), slice={[0:2047], [0:2048]} | slice | bytes 33538048 | tf_op jit(solution)/shard_map/slice | solution.py:316
  97.6 16.4 %fusion.1 = (bf16[2048,2048]{1,0:T(8,128)(2,1)}, bf16[2048,2048]{1,0:T(8,128)(2,1)S(1)}, bf16[2048,2048]{1,0:T(8,128)(2,1)S(1)}) fusion(bf16[2048,2048]{1,0:T(8,128)(2,1)} %gather_tokens.3, f32[2047,2048]{1,0:T(8,128)} %slice.158, f32[2048]{0:T(1024)S(1)} %bitcast.254, f32[2048]{0:T(1024)S(1)} %pad_maximum_fusion.3, f32[2048]{0:T(1024)S(1)} %bitcast.255, ...), kind=kLoop, calls=%fused_computation.8 | loop fusion | flops 50331648 | bytes 50356224 | tf_op jit(solution)/shard_map/convert_element_type | solution.py:412
  114.0 4.2 fusion.141
  118.3 4.2 fusion.142
  122.5 4.9 fusion.55.add_ref
  128.1 3.4 scan_states.2
  131.8 13.7 %multiply_reduce_fusion.4 = (f32[32,64,2]{1,2,0:T(2,128)S(1)}, f32[32,64,2,64]{1,3,2,0:T(8,128)}, f32[32,64,2,64]{1,3,2,0:T(8,128)S(1)}) fusion(f32[2,64]{1,0:T(2,128)S(1)} %copy-done.109, f32[32,64,2,64]{1,3,2,0:T(8,128)} %copy-done.6, bf16[32,64,2048,1]{2,1,3,0:T(8,128)(2,1)} %bitcast.217, bf16[2,64,2048,1]{2,1,0,3:T(8,128)(2,1)S(1)} %bitcast.233), kind=kOutput, calls=%fused_computation.83 | convolution fusion | flops 1074524160 | bytes 12075520 | tf_op jit(solution)/shard_map/dot_general | solution.py:412
  145.6 3.4 fusion.62
  149.1 3.5 fusion.50
  152.7 4.9 fusion.139
  158.3 4.1 copy.448
  162.5 2.1 multiply_reduce_fusion.3
  169.4 3.0 reshape.460
  172.4 13.3 %multiply_convert_fusion.3 = (bf16[2048,128]{1,0:T(8,128)(2,1)}, f32[2048,128]{1,0:T(8,128)}, f32[2048,128]{1,0:T(8,128)}) fusion(f32[128]{0:T(128)} %get-tuple-element.118, f32[128]{0:T(128)} %get-tuple-element.117, f32[2048,128]{1,0:T(8,128)} %copy.380, f32[2048,128]{1,0:T(8,128)S(1)} %reshape.460, f32[2048,128]{1,0:T(8,128)} %copy.377, ...), kind=kOutput, calls=%fused_computation.158 | convolution fusion | flops 1101529088 | bytes 31474688 | tf_op jit(solution)/shard_map/dot_general | solution.py:412
  185.8 13.9 %swap_blocks.3 = bf16[16,128,128]{2,1,0:T(8,128)(2,1)} custom-call(bf16[16,128,128]{2,1,0:T(8,128)(2,1)} %bitcast.220), custom_call_target="tpu_custom_call" | custom-call | tf_op jit(solution)/shard_map/swap_blocks/pallas_call | solution.py:231
  202.4 12.3 %copy.382 = bf16[2048,16,128]{0,2,1:T(8,128)(2,1)} copy(bf16[2048,16,128]{2,0,1:T(8,128)(2,1)} %bitcast.216) | data formatting | bytes 16777216 | tf_op jit(solution)/shard_map/transpose | solution.py:398
  214.7 4.9 fusion.140
  221.5 39.1 %gather_tokens.4 = bf16[2048,2048]{1,0:T(8,128)(2,1)} custom-call(bf16[128,2048]{1,0:T(8,128)(2,1)} %add_convert_fusion.2.a_ref), custom_call_target="tpu_custom_call" | custom-call | tf_op jit(solution)/shard_map/gather_tokens/pallas_call | solution.py:111
  261.5 11.8 %fusion.5 = bf16[2048,2048]{1,0:T(8,128)(2,1)S(1)} fusion(bf16[2048,2048]{1,0:T(8,128)(2,1)} %gather_tokens.4, f32[2048]{0:T(1024)S(1)} %bitcast.247, bf16[2047,2048]{1,0:T(8,128)(2,1)} %bitcast.207, f32[2048]{0:T(1024)S(1)} %copy-done.71), kind=kLoop, calls=%fused_computation.12 | loop fusion | flops 29360128 | bytes 25178112 | tf_op jit(solution)/shard_map/convert_element_type | solution.py:437
  273.3 3.2 copy-done.27
  276.5 5.9 fusion.143
  282.4 7.0 convolution_convert_fusion.2.a_hbm
  289.5 38.3 %sum_tokens.3 = f32[128,2048]{1,0:T(8,128)S(1)} custom-call(bf16[2048,2048]{1,0:T(8,128)(2,1)S(1)} %convolution_convert_fusion.2.a_hbm), custom_call_target="tpu_custom_call" | custom-call | tf_op jit(solution)/shard_map/sum_tokens/pallas_call | solution.py:198
  327.8 4.4 fusion.84
  332.2 36.4 %gather_tokens.5 = bf16[2048,2048]{1,0:T(8,128)(2,1)} custom-call(bf16[128,2048]{1,0:T(8,128)(2,1)} %get-tuple-element.102.a_ref), custom_call_target="tpu_custom_call" | custom-call | tf_op jit(solution)/shard_map/gather_tokens/pallas_call | solution.py:111
  368.6 9.7 %multiply_convert_fusion = bf16[2048,448]{0,1:T(8,128)(2,1)S(1)} fusion(f32[2048,448]{0,1:T(8,128)} %fusion.143, bf16[2048,2048]{1,0:T(8,128)(2,1)} %gather_tokens.5, bf16[448,2048]{1,0:T(8,128)(2,1)S(1)} %copy-done), kind=kOutput, calls=%fused_computation.30 | convolution fusion | flops 3761766400 | bytes 15728640 | tf_op jit(solution)/shard_map/dot_general | solution.py:324
  378.4 4.8 convolution_convert_fusion.1.a_hbm
  383.3 38.8 %sum_tokens.4 = f32[128,2048]{1,0:T(8,128)S(1)} custom-call(bf16[2048,2048]{1,0:T(8,128)(2,1)S(1)} %convolution_convert_fusion.1.a_hbm), custom_call_target="tpu_custom_call" | custom-call | tf_op jit(solution)/shard_map/sum_tokens/pallas_call | solution.py:198
  431.3 17.6 %swap_blocks.5 = bf16[16,128,128]{2,1,0:T(8,128)(2,1)} custom-call(bf16[16,128,128]{2,1,0:T(8,128)(2,1)} %bitcast.228), custom_call_target="tpu_custom_call" | custom-call | tf_op jit(solution)/shard_map/swap_blocks/pallas_call | solution.py:231
  450.5 6.0 fusion.91
  458.0 9.7 %convolution_convert_fusion.4 = bf16[448,2048]{1,0:T(8,128)(2,1)} fusion(bf16[2048,2048]{1,0:T(8,128)(2,1)} %gather_tokens.5, f32[2048,448]{0,1:T(8,128)} %fusion.143), kind=kOutput, calls=%fused_computation.36 | convolution fusion | flops 3761766400 | bytes 13893632 | tf_op jit(solution)/shard_map/dot_general | solution.py:324
  467.8 4.2 copy.416
  472.0 4.1 copy.374
  476.2 2.1 reshape_reshape.7
  481.2 9.3 %convolution_convert_fusion.3 = bf16[2048,448]{0,1:T(8,128)(2,1)} fusion(bf16[2048,448]{0,1:T(8,128)(2,1)} %copy-done.118, bf16[2048,2048]{1,0:T(8,128)(2,1)} %copy-done.27), kind=kOutput, calls=%fused_computation.35 | convolution fusion | flops 3759013888 | bytes 12058624 | tf_op jit(solution)/shard_map/dot_general | solution.py:324
  491.5 6.3 convolution_convert_fusion.6
  499.1 14.5 %swap_blocks.4 = bf16[16,128,128]{2,1,0:T(8,128)(2,1)} custom-call(bf16[16,128,128]{2,1,0:T(8,128)(2,1)} %bitcast.230), custom_call_target="tpu_custom_call" | custom-call | tf_op jit(solution)/shard_map/swap_blocks/pallas_call | solution.py:231
  513.6 2.5 fusion.118
  519.0 2.5 reshape.461
  523.2 4.1 copy.387
  527.4 4.8 multiply_reduce_fusion.2
  532.2 4.8 fusion.35
  537.0 4.9 fusion.39.add_ref
  541.9 3.5 fusion.37
  545.4 3.4 scan_states.3
  548.7 3.0 multiply_reduce_fusion.1
  552.2 5.0 fusion.54
  561.4 5.9 fusion.42
  567.4 5.0 fusion.65
  572.4 3.8 fusion.29
  576.8 2.5 copy.454
  579.8 10.2 %fusion.31 = (f32[64,2,64]{0,2,1:T(8,128)S(1)}, f32[64,2,64]{0,2,1:T(8,128)S(1)}, bf16[32,64,2,64]{1,3,2,0:T(8,128)(2,1)S(1)}, bf16[32,64,2,64]{1,3,2,0:T(8,128)...) fusion(f32[32,64,2,64]{1,3,2,0:T(8,128)} %copy-done.6, f32[32,64]{1,0:T(8,128)S(1)} %copy-done.50, ...), kind=kOutput, calls=%fused_computation.63 | convolution fusion | flops 206544768 | bytes 8610816 | tf_op jit(solution)/shard_map/transpose(jvp(vmap(jhc,jhe->hce)))/dot_general | solution.py:371
  595.7 2.5 copy.452
  600.8 13.0 %fusion.144 = f32[2048,1024]{0,1:T(8,128)S(1)} fusion(bf16[2048,2048]{1,0:T(8,128)(2,1)} %gather_tokens.3, bf16[2048,1024]{1,0:T(8,128)(2,1)S(1)} %fusion.28), kind=kOutput, calls=%fused_computation.278 | convolution fusion | flops 8589934592 | bytes 20971520 | tf_op jit(solution)/shard_map/dot_general | solution.py:324
  613.8 3.5 fusion.10
  617.5 2.7 pad_maximum_fusion
  621.0 9.5 %convolution_convert_fusion.a_hbm = bf16[2048,2048]{1,0:T(8,128)(2,1)S(1)} fusion(bf16[2048,1024]{1,0:T(8,128)(2,1)S(1)} %copy-done.73, bf16[2048,1024]{0,1:T(8,128)(2,1)S(1)} %bitcast.221), kind=kOutput, calls=%fused_computation.14 | convolution fusion | flops 8594128896 | bytes 16777216 | tf_op jit(solution)/shard_map/dot_general | solution.py:324
  630.5 53.5 %sum_tokens.5 = f32[128,2048]{1,0:T(8,128)S(1)} custom-call(bf16[2048,2048]{1,0:T(8,128)(2,1)S(1)} %convolution_convert_fusion.a_hbm), custom_call_target="tpu_custom_call" | custom-call | tf_op jit(solution)/shard_map/sum_tokens/pallas_call | solution.py:198
  690.5 5.6 convolution_convert_fusion.5
  700.2 22.3 %sum_vectors.1 = f32[8,128]{1,0:T(8,128)} custom-call(f32[16,8,8,128]{3,2,1,0:T(8,128)} %copy.471), custom_call_target="tpu_custom_call" | custom-call | tf_op jit(solution)/shard_map/sum_vectors/pallas_call | solution.py:281
  723.9 3.0 add_add_fusion.4
  733.7 14.1 %reduce-scatter.8.cloned.1.call-done = bf16[128,256]{1,0:T(8,128)(2,1)} async-done(((bf16[128,2048]{1,0:T(8,128)(2,1)}), bf16[128,256]{1,0:T(8,128)(2,1)}) %reduce-scatter.8.cloned.1.call-update) | async-done | bytes 65552 | tf_op jit(solution)/shard_map/reduce_scatter | solution.py:525
  (414 shorter events, 84.1 us)
Async XLA Ops:
  7.2 275.3 %copy-start = (bf16[448,2048]{1,0:T(8,128)(2,1)S(1)}, bf16[448,2048]{1,0:T(8,128)(2,1)}, u32[]{:S(2)}) copy-start(bf16[448,2048]{1,0:T(8,128)(2,1)} %param.14) | copy-start | bytes 5505028
  7.2 195.2 %all-gather.9.cloned.1.call-start = ((), (), s32[]{:S(2)}) async-start(), calls=%async_computation.12 | async-start | bytes 8912896 | tf_op jit(solution)/shard_map/all_gather | solution.py:397
  7.9 206.8 %all-gather.5.cloned.1.call-start = ((), (), s32[]{:S(2)}) async-start(), calls=%async_computation.5 | async-start | bytes 8912896 | tf_op jit(solution)/shard_map/all_gather | solution.py:396
  8.7 681.8 %all-gather.7.cloned.1.call-start = ((), (), s32[]{:S(2)}) async-start(), calls=%async_computation.7 | async-start | bytes 8912896 | tf_op jit(solution)/shard_map/all_gather | solution.py:477
  10.8 85.9 %copy-start.84 = (f32[2,64]{1,0:T(2,128)}, f32[2,64]{1,0:T(2,128)S(1)}, u32[]{:S(2)}) copy-start(f32[2,64]{1,0:T(2,128)S(1)} %exp.67) | copy-start | bytes 1540
  18.1 65.2 %copy-start.82 = (f32[128]{0:T(128)}, f32[128]{0:T(128)S(1)}, u32[]{:S(2)}) copy-start(f32[128]{0:T(128)S(1)} %broadcast_multiply_fusion.2) | copy-start | bytes 1540
  19.0 64.4 %copy-start.91 = (f32[128]{0:T(128)}, f32[128]{0:T(128)S(1)}, u32[]{:S(2)}) copy-start(f32[128]{0:T(128)S(1)} %fusion.123) | copy-start | bytes 1540
  20.9 62.5 %copy-start.51 = (f32[1,2048]{1,0:T(1,128)}, f32[1,2048]{1,0:T(1,128)S(1)}, u32[]{:S(2)}) copy-start(f32[1,2048]{1,0:T(1,128)S(1)} %get-tuple-element.115) | copy-start | bytes 24580
  83.4 11.8 %copy-start.67 = (s32[2048]{0:T(1024)S(1)}, s32[2048]{0:T(1024)}, u32[]{:S(2)}) copy-start(s32[2048]{0:T(1024)} %param.17) | copy-start | bytes 24580
  94.8 19.2 %copy-start.99 = (f32[64]{0:T(128)}, f32[64]{0:T(128)S(1)}, u32[]{:S(2)}) copy-start(f32[64]{0:T(128)S(1)} %broadcast_add_fusion) | copy-start | bytes 772
  94.8 19.2 %copy-start.95 = (f32[64]{0:T(128)}, f32[64]{0:T(128)S(1)}, u32[]{:S(2)}) copy-start(f32[64]{0:T(128)S(1)} %broadcast_subtract_fusion.4) | copy-start | bytes 772
  94.9 19.1 %copy-start.97 = (f32[64]{0:T(128)}, f32[64]{0:T(128)S(1)}, u32[]{:S(2)}) copy-start(f32[64]{0:T(128)S(1)} %iota_convert_fusion) | copy-start | bytes 772
  95.9 18.1 %copy-start.70 = (f32[2048]{0:T(1024)}, f32[2048]{0:T(1024)S(1)}, u32[]{:S(2)}) copy-start(f32[2048]{0:T(1024)S(1)} %pad_maximum_fusion.3) | copy-start | bytes 24580
  96.7 17.3 %copy-start.86 = (f32[2,64]{1,0:T(2,128)}, f32[2,64]{1,0:T(2,128)S(1)}, u32[]{:S(2)}) copy-start(f32[2,64]{1,0:T(2,128)S(1)} %get-tuple-element.126) | copy-start | bytes 1540
  96.8 25.6 %copy-start.49 = (f32[32,64]{1,0:T(8,128)}, f32[32,64]{1,0:T(8,128)S(1)}, u32[]{:S(2)}) copy-start(f32[32,64]{1,0:T(8,128)S(1)} %get-tuple-element.123) | copy-start | bytes 24580
  97.6 24.9 %copy-start.36 = (f32[64,2,64]{0,2,1:T(8,128)}, f32[64,2,64]{0,2,1:T(8,128)S(1)}, u32[]{:S(2)}) copy-start(f32[64,2,64]{0,2,1:T(8,128)S(1)} %get-tuple-element.125) | copy-start | bytes 98308
  97.6 51.5 %copy-start.38 = (f32[64,2,64]{0,2,1:T(8,128)}, f32[64,2,64]{0,2,1:T(8,128)S(1)}, u32[]{:S(2)}) copy-start(f32[64,2,64]{0,2,1:T(8,128)S(1)} %get-tuple-element.135) | copy-start | bytes 98308
  97.6 16.4 %copy-start.42 = (bf16[128,2048]{1,0:T(8,128)(2,1)S(1)}, bf16[128,2048]{1,0:T(8,128)(2,1)}, u32[]{:S(2)}) copy-start(bf16[128,2048]{1,0:T(8,128)(2,1)} %copy.361) | copy-start | bytes 1572868
  131.8 20.9 %copy-start.16 = (f32[32,64,64]{2,1,0:T(8,128)}, f32[32,64,64]{2,1,0:T(8,128)S(1)}, u32[]{:S(2)}) copy-start(f32[32,64,64]{2,1,0:T(8,128)S(1)} %and_convert_fusion) | copy-start | bytes 1572868
  131.8 13.8 %copy-start.13 = (f32[32,2,64,64]{3,2,1,0:T(8,128)S(1)}, f32[32,2,64,64]{3,2,1,0:T(8,128)}, u32[]{:S(2)}) copy-start(f32[32,2,64,64]{3,2,1,0:T(8,128)} %scan_states.2) | copy-start | bytes 3145732
  185.7 15.9 %copy-start.69 = (f32[2047]{0:T(1024)S(1)}, f32[2047]{0:T(1024)}, u32[]{:S(2)}) copy-start(f32[2047]{0:T(1024)} %copy-done.68) | copy-start | bytes 24568
  221.5 39.9 %copy-start.65 = (f32[1,2048]{1,0:T(1,128)S(1)}, f32[1,2048]{1,0:T(1,128)}, u32[]{:S(2)}) copy-start(f32[1,2048]{1,0:T(1,128)} %get-tuple-element.116) | copy-start | bytes 24580
  221.5 39.9 %copy-start.71 = (f32[2048]{0:T(1024)S(1)}, f32[2048]{0:T(1024)}, u32[]{:S(2)}) copy-start(f32[2048]{0:T(1024)} %copy-done.70) | copy-start | bytes 24580
  261.4 66.3 %copy-start.79 = (bf16[1,2048]{1,0:T(2,128)(2,1)}, bf16[1,2048]{1,0:T(2,128)(2,1)S(1)}, u32[]{:S(2)}) copy-start(bf16[1,2048]{1,0:T(2,128)(2,1)S(1)} %constant_dynamic-slice_fusion) | copy-start | bytes 12292
  261.5 15.1 %copy-start.116 = (bf16[2048,448]{0,1:T(8,128)(2,1)S(1)}, bf16[2048,448]{0,1:T(8,128)(2,1)}, u32[]{:S(2)}) copy-start(bf16[2048,448]{0,1:T(8,128)(2,1)} %param.13) | copy-start | bytes 5505028
  276.5 51.2 %slice-start = ((s8[8388608]{0:T(1024)(128)(4,1)}), s8[4194304]{0:T(1024)(128)(4,1)S(1)}, s32[]{:S(2)}) async-start(s8[8388608]{0:T(1024)(128)(4,1)} %bitcast.208), calls=%async_computation.13 | async-start | bytes 8388608
  282.4 45.3 %slice-start.1 = ((s8[8388608]{0:T(1024)(128)(4,1)}), s8[4194304]{0:T(1024)(128)(4,1)S(1)}, s32[]{:S(2)}) async-start(s8[8388608]{0:T(1024)(128)(4,1)} %bitcast.208), calls=%async_computation.14 | async-start | bytes 8388608
  289.4 38.4 %copy-start.24 = (bf16[128,2048]{1,0:T(8,128)(2,1)S(1)}, bf16[128,2048]{1,0:T(8,128)(2,1)}, u32[]{:S(2)}) copy-start(bf16[128,2048]{1,0:T(8,128)(2,1)} %add_convert_fusion.2.a_ref) | copy-start | bytes 1572868
  289.4 38.4 %copy-start.33 = (bf16[128,2048]{1,0:T(8,128)(2,1)S(1)}, bf16[128,2048]{1,0:T(8,128)(2,1)}, u32[]{:S(2)}) copy-start(bf16[128,2048]{1,0:T(8,128)(2,1)} %param.10) | copy-start | bytes 1572868
  289.4 38.4 %copy-start.63 = (f32[1,2048]{1,0:T(1,128)S(1)}, f32[1,2048]{1,0:T(1,128)}, u32[]{:S(2)}) copy-start(f32[1,2048]{1,0:T(1,128)} %get-tuple-element.107) | copy-start | bytes 24580
  289.4 38.4 %copy-start.105 = (f32[128]{0:T(128)S(1)}, f32[128]{0:T(128)}, u32[]{:S(2)}) copy-start(f32[128]{0:T(128)} %fusion.122) | copy-start | bytes 1540
  368.6 53.4 %slice-start.2 = ((s8[8388608]{0:T(1024)(128)(4,1)}), s8[4194304]{0:T(1024)(128)(4,1)S(1)}, s32[]{:S(2)}) async-start(s8[8388608]{0:T(1024)(128)(4,1)} %bitcast.211), calls=%async_computation.15 | async-start | bytes 8388608
  378.4 43.7 %slice-start.3 = ((s8[8388608]{0:T(1024)(128)(4,1)}), s8[4194304]{0:T(1024)(128)(4,1)S(1)}, s32[]{:S(2)}) async-start(s8[8388608]{0:T(1024)(128)(4,1)} %bitcast.211), calls=%async_computation.16 | async-start | bytes 8388608
  383.2 38.9 %copy-start.31 = (bf16[128,2048]{1,0:T(8,128)(2,1)S(1)}, bf16[128,2048]{1,0:T(8,128)(2,1)}, u32[]{:S(2)}) copy-start(bf16[128,2048]{1,0:T(8,128)(2,1)} %get-tuple-element.96) | copy-start | bytes 1572868
  383.2 38.9 %copy-start.64 = (f32[1,2048]{1,0:T(1,128)S(1)}, f32[1,2048]{1,0:T(1,128)}, u32[]{:S(2)}) copy-start(f32[1,2048]{1,0:T(1,128)} %get-tuple-element.107) | copy-start | bytes 24580
  383.2 38.9 %copy-start.66 = (f32[1,2048]{1,0:T(1,128)S(1)}, f32[1,2048]{1,0:T(1,128)}, u32[]{:S(2)}) copy-start(f32[1,2048]{1,0:T(1,128)} %get-tuple-element.116) | copy-start | bytes 24580
  383.2 38.9 %copy-start.80 = (bf16[1,2048]{1,0:T(2,128)(2,1)S(1)}, bf16[1,2048]{1,0:T(2,128)(2,1)}, u32[]{:S(2)}) copy-start(bf16[1,2048]{1,0:T(2,128)(2,1)} %copy-done.79) | copy-start | bytes 12292
  383.3 38.9 %copy-start.106 = (f32[128]{0:T(128)S(1)}, f32[128]{0:T(128)}, u32[]{:S(2)}) copy-start(f32[128]{0:T(128)} %fusion.122) | copy-start | bytes 1540
  424.1 3.1 collective-permute-start
  429.8 297.0 %reduce-scatter.14.cloned.1.call-start = ((), (), s32[]{:S(2)}) async-start(), calls=%async_computation.11 | async-start | bytes 589824 | tf_op jit(solution)/shard_map/reduce_scatter | solution.py:525
  429.9 20.2 %copy-start.74 = (bf16[2048]{0:T(1024)(128)(2,1)}, bf16[2048]{0:T(1024)(128)(2,1)S(1)}, u32[]{:S(2)}) copy-start(bf16[2048]{0:T(1024)(128)(2,1)S(1)} %pad_maximum_fusion.4) | copy-start | bytes 12292
  458.0 270.4 %reduce-scatter.12.cloned.1.call-start = ((), (), s32[]{:S(2)}) async-start(), calls=%async_computation.10 | async-start | bytes 2064384 | tf_op jit(solution)/shard_map/reduce_scatter | solution.py:525
  467.7 262.3 %reduce-scatter.10.cloned.1.call-start = ((), (), s32[]{:S(2)}) async-start(), calls=%async_computation.9 | async-start | bytes 2064384 | tf_op jit(solution)/shard_map/reduce_scatter | solution.py:525
  490.5 241.4 %reduce-scatter.6.cloned.1.call-start = ((), (), s32[]{:S(2)}) async-start(), calls=%async_computation.6 | async-start | bytes 2359296 | tf_op jit(solution)/shard_map/reduce_scatter | solution.py:525
  497.8 15.9 %copy-start.107 = (f32[128]{0:T(128)S(1)}, f32[128]{0:T(128)}, u32[]{:S(2)}) copy-start(f32[128]{0:T(128)} %get-tuple-element.117) | copy-start | bytes 1540
  497.8 15.9 %copy-start.108 = (f32[128]{0:T(128)S(1)}, f32[128]{0:T(128)}, u32[]{:S(2)}) copy-start(f32[128]{0:T(128)} %get-tuple-element.118) | copy-start | bytes 1540
  579.8 10.5 %copy-start.87 = (f32[2,64]{1,0:T(2,128)S(1)}, f32[2,64]{1,0:T(2,128)}, u32[]{:S(2)}) copy-start(f32[2,64]{1,0:T(2,128)} %copy-done.86) | copy-start | bytes 1540
  579.8 10.5 %copy-start.96 = (f32[64]{0:T(128)S(1)}, f32[64]{0:T(128)}, u32[]{:S(2)}) copy-start(f32[64]{0:T(128)} %copy-done.95) | copy-start | bytes 772
  579.8 10.5 %copy-start.98 = (f32[64]{0:T(128)S(1)}, f32[64]{0:T(128)}, u32[]{:S(2)}) copy-start(f32[64]{0:T(128)} %copy-done.97) | copy-start | bytes 772
  579.8 10.9 %copy-start.113 = (f32[1,128]{1,0:T(1,128)S(1)}, f32[1,128]{1,0:T(1,128)}, u32[]{:S(2)}) copy-start(f32[1,128]{1,0:T(1,128)} %reduce_sum.329) | copy-start | bytes 1540
  600.7 13.1 %copy-start.72 = (bf16[2048,1024]{1,0:T(8,128)(2,1)}, bf16[2048,1024]{1,0:T(8,128)(2,1)S(1)}, u32[]{:S(2)}) copy-start(bf16[2048,1024]{1,0:T(8,128)(2,1)S(1)} %fusion.28) | copy-start | bytes 12582916
  600.7 13.1 %copy-start.28 = (bf16[4,2048,128]{1,2,0:T(8,128)(2,1)S(1)}, bf16[4,2048,128]{1,2,0:T(8,128)(2,1)}, u32[]{:S(2)}) copy-start(bf16[4,2048,128]{1,2,0:T(8,128)(2,1)} %copy.416) | copy-start | bytes 6291460
  600.7 13.1 %copy-start.61 = (f32[4,2048]{1,0:T(4,128)S(1)}, f32[4,2048]{1,0:T(4,128)}, u32[]{:S(2)}) copy-start(f32[4,2048]{1,0:T(4,128)} %get-tuple-element.103) | copy-start | bytes 98308
  600.8 13.1 %copy-start.62 = (f32[4,2048]{1,0:T(4,128)S(1)}, f32[4,2048]{1,0:T(4,128)}, u32[]{:S(2)}) copy-start(f32[4,2048]{1,0:T(4,128)} %get-tuple-element.104) | copy-start | bytes 98308
  617.5 130.3 %reduce-scatter.8.cloned.1.call-start = ((), (), s32[]{:S(2)}) async-start(), calls=%async_computation.8 | async-start | bytes 589824 | tf_op jit(solution)/shard_map/reduce_scatter | solution.py:525
  630.4 53.5 %copy-start.19 = (bf16[128,2048]{1,0:T(8,128)(2,1)S(1)}, bf16[128,2048]{1,0:T(8,128)(2,1)}, u32[]{:S(2)}) copy-start(bf16[128,2048]{1,0:T(8,128)(2,1)} %param.9) | copy-start | bytes 1572868
  630.4 53.5 %copy-start.52 = (f32[1,2048]{1,0:T(1,128)S(1)}, f32[1,2048]{1,0:T(1,128)}, u32[]{:S(2)}) copy-start(f32[1,2048]{1,0:T(1,128)} %copy-done.51) | copy-start | bytes 24580
  630.5 53.5 %copy-start.83 = (f32[128]{0:T(128)S(1)}, f32[128]{0:T(128)}, u32[]{:S(2)}) copy-start(f32[128]{0:T(128)} %copy-done.82) | copy-start | bytes 1540
  630.5 53.9 %copy-start.115 = (f32[128]{0:T(128)S(1)}, f32[128]{0:T(128)}, u32[]{:S(2)}) copy-start(f32[128]{0:T(128)} %copy-done.114) | copy-start | bytes 1540
  630.5 53.9 %copy-start.92 = (f32[128]{0:T(128)S(1)}, f32[128]{0:T(128)}, u32[]{:S(2)}) copy-start(f32[128]{0:T(128)} %copy-done.91) | copy-start | bytes 1540
  698.8 25.0 %copy-start.112 = (f32[128]{0:T(128)S(1)}, f32[128]{0:T(128)}, u32[]{:S(2)}) copy-start(f32[128]{0:T(128)} %get-tuple-element.61) | copy-start | bytes 1540
  698.8 25.0 %copy-start.102 = (f32[128]{0:T(128)S(1)}, f32[128]{0:T(128)}, u32[]{:S(2)}) copy-start(f32[128]{0:T(128)} %copy-done.101) | copy-start | bytes 1540
  698.8 25.0 %copy-start.104 = (f32[128]{0:T(128)S(1)}, f32[128]{0:T(128)}, u32[]{:S(2)}) copy-start(f32[128]{0:T(128)} %copy-done.103) | copy-start | bytes 1540
  723.8 25.4 %copy-start.1 = (bf16[448,2048]{1,0:T(8,128)(2,1)S(1)}, bf16[448,2048]{1,0:T(8,128)(2,1)}, u32[]{:S(2)}) copy-start(bf16[448,2048]{1,0:T(8,128)(2,1)} %param.14) | copy-start | bytes 5505028
  (68 other events, 282.1 us)
Sparse Core Ops, SparseCore 0:
  10.4 91.3 all-gather.8
  104.2 70.8 all-gather.4
  429.9 76.2 all-gather.6
  508.5 35.5 reduce-scatter.13
  546.5 45.8 reduce-scatter.11
  594.8 49.5 reduce-scatter.9
  646.9 61.3 reduce-scatter.5
  710.8 36.9 reduce-scatter.7

commit v2 on v1

v2 whole, which is shorter than its diff:
```python
import functools

import jax
import jax.numpy as jnp
from jax import lax
from jax.experimental import pallas as pl
from jax.experimental.pallas import tpu as pltpu
from jax.sharding import PartitionSpec as P

MESH = pl.DeviceIdType.MESH
VMEM = pltpu.VMEM
DMA = pltpu.SemaphoreType.DMA
BF = jnp.bfloat16
F32 = jnp.float32

ATTENTION_WIDTH = 64


class Place:
    def __init__(self):
        self.dp = lax.axis_index("dp")
        s = lax.axis_index("sp")
        self.s = s
        self.x, self.z, self.c = s // 4, (s // 2) % 2, s % 2

    def at(self, dx=0, dz=0, dc=0):
        x = (self.x + dx) % 4
        z = (self.z + dz) % 2
        c = (self.c + dc) % 2
        return x * 4 + z * 2 + c

    def dev(self, s):
        return (self.dp, s)


def greet(place, peers):
    barrier = pltpu.get_barrier_semaphore()
    for peer in peers:
        pl.semaphore_signal(barrier, inc=1, device_id=place.dev(peer), device_id_type=MESH)
    pl.semaphore_wait(barrier, len(peers))


class Traffic:
    def __init__(self, place, ss, rs):
        self.place, self.ss, self.rs, self.sent = place, ss, rs, []

    def copy(self, k, src, dst, to):
        return pltpu.make_async_remote_copy(
            src_ref=src, dst_ref=dst, send_sem=self.ss.at[k], recv_sem=self.rs.at[k],
            device_id=self.place.dev(to), device_id_type=MESH,
        )

    def send(self, k, src, dst, to):
        cp = self.copy(k, src, dst, to)
        cp.start()
        self.sent.append(cp)

    def landed(self, k, ref):
        self.copy(k, ref, ref, self.place.s).wait_recv()

    def finish(self):
        for cp in self.sent:
            cp.wait_send()


def gather_steps(p, t, a_ref, land):
    H = a_ref.shape[0] // 2
    upper, lower = pl.ds(0, H), pl.ds(H, H)
    core, xp, xm, zz = p.at(dc=1), p.at(dx=1), p.at(dx=-1), p.at(dz=1)
    here = p.s
    t.send(0, a_ref, land.at[here], xp)
    t.send(1, a_ref, land.at[here], xm)
    t.send(2, a_ref, land.at[here], zz)
    t.send(3, a_ref, land.at[here], core)
    yield []
    t.landed(3, land.at[core])
    yield [core]
    d2, zxm, zxp, zd2 = p.at(dx=2), p.at(dx=-1, dz=1), p.at(dx=1, dz=1), p.at(dx=2, dz=1)

    def other(**k):
        return p.at(dc=1, **k)

    t.landed(0, land.at[xm])
    t.send(4, land.at[xm, upper], land.at[xm, upper], xp)
    t.landed(1, land.at[xp])
    t.send(5, land.at[xp, lower], land.at[xp, lower], xm)
    t.send(6, land.at[xm], land.at[xm], core)
    t.send(7, land.at[xp], land.at[xp], core)
    t.landed(2, land.at[zz])
    t.send(8, land.at[zz], land.at[zz], xp)
    t.send(9, land.at[zz], land.at[zz], xm)
    t.send(10, land.at[zz], land.at[zz], core)
    yield [xm, xp, zz]
    t.landed(6, land.at[other(dx=-1)])
    yield [other(dx=-1)]
    t.landed(4, land.at[d2, upper])
    t.send(11, land.at[d2, upper], land.at[d2, upper], zz)
    t.landed(5, land.at[d2, lower])
    t.send(12, land.at[d2, lower], land.at[d2, lower], zz)
    t.send(13, land.at[d2], land.at[d2], core)
    yield [d2]
    t.landed(7, land.at[other(dx=1)])
    t.landed(10, land.at[other(dz=1)])
    yield [other(dx=1), other(dz=1)]
    t.landed(13, land.at[other(dx=2)])
    yield [other(dx=2)]
    t.landed(8, land.at[zxm])
    t.send(14, land.at[zxm], land.at[zxm], core)
    t.landed(9, land.at[zxp])
    t.send(15, land.at[zxp], land.at[zxp], core)
    yield [zxm, zxp]
    t.landed(11, land.at[zd2, upper])
    t.send(16, land.at[zd2, upper], land.at[zd2, upper], core)
    t.landed(12, land.at[zd2, lower])
    t.send(17, land.at[zd2, lower], land.at[zd2, lower], core)
    t.landed(14, land.at[other(dx=-1, dz=1)])
    t.landed(15, land.at[other(dx=1, dz=1)])
    yield [other(dx=-1, dz=1), other(dx=1, dz=1), zd2]
    t.landed(16, land.at[other(dx=2, dz=1), upper])
    t.landed(17, land.at[other(dx=2, dz=1), lower])
    yield [other(dx=2, dz=1)]


def run_gather(a_ref, land, ss, rs, work):
    p = Place()
    t = Traffic(p, ss, rs)
    greet(p, [p.at(dc=1), p.at(dx=1), p.at(dx=-1), p.at(dz=1)])
    steps = gather_steps(p, t, a_ref, land)
    next(steps)
    land[p.s] = a_ref[...]
    ready = [p.s]
    for arrived in steps:
        ready += arrived
        for unused in range(min(2, len(ready))):
            work(ready.pop(0))
    for b in ready:
        work(b)
    return t


def save_blocks(land, all_ref, sem):
    R = land.shape[1]

    def start(b):
        pltpu.make_async_copy(land.at[b], all_ref.at[pl.ds(pl.multiple_of(b * R, 16), R)], sem.at[b]).start()

    def wait():
        for b in range(16):
            pltpu.make_async_copy(land.at[b], all_ref.at[pl.ds(b * R, R)], sem.at[b]).wait()

    return start, wait


def heads_of_blocks(land):
    R = land.shape[1]
    first = [land[b, 0:16, :].astype(F32)[0:1] for b in range(16)]
    before = [jnp.zeros_like(first[0])] + [land[b, R - 16 : R, :].astype(F32)[15:16] for b in range(15)]
    return jnp.concatenate(first, axis=0), jnp.concatenate(before, axis=0)


def shifted(n, same):
    rows = lax.broadcasted_iota(jnp.int32, n.shape, 0)
    before = jnp.where(rows == 0, 0.0, pltpu.roll(n, 1, 0))
    return before * same - n


def project_kernel(a_ref, w_ref, mu_ref, same_ref, all_ref, o_ref, land, ss, rs, ls):
    R = a_ref.shape[0]
    Q, cols = w_ref.shape[0], w_ref.shape[2]
    start, wait = save_blocks(land, all_ref, ls)

    def work(b):
        start(b)
        rows = pl.ds(pl.multiple_of(b * R, 16), R)
        n = land[b].astype(F32)
        shift = shifted(n, same_ref[rows, :])
        for q in range(Q):
            m = (n + shift * mu_ref[q : q + 1, :]).astype(BF)
            o_ref[rows, q * cols : (q + 1) * cols] = jnp.dot(m, w_ref[q], preferred_element_type=F32)

    t = run_gather(a_ref, land, ss, rs, work)
    first, before = heads_of_blocks(land)
    same = jnp.concatenate([same_ref[b * R : b * R + 1, :] for b in range(16)], axis=0)
    shift = before * same - first
    for q in range(Q):
        m = (first + shift * mu_ref[q : q + 1, :]).astype(BF)
        out = jnp.dot(m, w_ref[q], preferred_element_type=F32)
        for b in range(16):
            o_ref[b * R : b * R + 1, q * cols : (q + 1) * cols] = out[b : b + 1]
    wait()
    t.finish()


def project(a, w, mu, same, cid):
    R, C = a.shape
    Q, cols = w.shape[0], w.shape[2]
    return pl.pallas_call(
        project_kernel,
        out_shape=(jax.ShapeDtypeStruct((16 * R, C), BF), jax.ShapeDtypeStruct((16 * R, Q * cols), F32)),
        in_specs=[pl.BlockSpec(memory_space=VMEM)] * 4,
        out_specs=(pl.BlockSpec(memory_space=pl.ANY), pl.BlockSpec(memory_space=VMEM)),
        scratch_shapes=[VMEM((16, R, C), BF), DMA((18,)), DMA((18,)), DMA((16,))],
        compiler_params=pltpu.CompilerParams(collective_id=cid, has_side_effects=True, vmem_limit_bytes=48 * 2**20),
        name="gather_project",
    )(a, w, mu, same)


def key_kernel(a_ref, w_ref, nu_ref, same_ref, all_ref, in_ref, lift_ref, sq_ref, land, mixed, ss, rs, ls, ms):
    R = a_ref.shape[0]
    start, wait = save_blocks(land, all_ref, ls)

    def put(b, rows, m):
        e = jnp.maximum(jnp.dot(m, w_ref[...], preferred_element_type=F32), 0.0)
        lift_ref[rows, :] = e
        sq_ref[rows, :] = (e * e).astype(BF)

    def work(b):
        start(b)
        n = land[b].astype(F32)
        rows = pl.ds(pl.multiple_of(b * R, 16), R)
        m = (n + shifted(n, same_ref[rows, :]) * nu_ref[...]).astype(BF)
        mixed[b] = m
        put(b, rows, m)

    t = run_gather(a_ref, land, ss, rs, work)
    first, before = heads_of_blocks(land)
    same = jnp.concatenate([same_ref[b * R : b * R + 1, :] for b in range(16)], axis=0)
    head = first + (before * same - first) * nu_ref[...]
    e = jnp.maximum(jnp.dot(head.astype(BF), w_ref[...], preferred_element_type=F32), 0.0)
    sq = e * e
    copies = []
    for b in range(16):
        rows = slice(b * R, b * R + 16)
        top = lax.broadcasted_iota(jnp.int32, (16, 1), 0) == 0
        mixed[b, 0:16, :] = jnp.where(top, head[b : b + 1], mixed[b, 0:16, :].astype(F32)).astype(BF)
        lift_ref[b * R : b * R + 1, :] = e[b : b + 1]
        sq_ref[rows, :] = jnp.where(top, sq[b : b + 1], sq_ref[rows, :].astype(F32)).astype(BF)
        cp = pltpu.make_async_copy(mixed.at[b], in_ref.at[pl.ds(b * R, R)], ms.at[b])
        cp.start()
        copies.append(cp)
    for cp in copies:
        cp.wait()
    wait()
    t.finish()


def key_side(a, w, nu, same, cid):
    R, C = a.shape
    units = w.shape[1]
    return pl.pallas_call(
        key_kernel,
        out_shape=(
            jax.ShapeDtypeStruct((16 * R, C), BF),
            jax.ShapeDtypeStruct((16 * R, C), BF),
            jax.ShapeDtypeStruct((16 * R, units), F32),
            jax.ShapeDtypeStruct((16 * R, units), BF),
        ),
        in_specs=[pl.BlockSpec(memory_space=VMEM)] * 4,
        out_specs=(pl.BlockSpec(memory_space=pl.ANY), pl.BlockSpec(memory_space=pl.ANY), pl.BlockSpec(memory_space=VMEM), pl.BlockSpec(memory_space=VMEM)),
        scratch_shapes=[VMEM((16, R, C), BF), VMEM((16, R, C), BF), DMA((18,)), DMA((18,)), DMA((16,)), DMA((16,))],
        compiler_params=pltpu.CompilerParams(collective_id=cid, has_side_effects=True, vmem_limit_bytes=56 * 2**20),
        name="gather_key",
    )(a, w, nu, same)


def back_kernel(a_ref, w_ref, lift_ref, all_ref, o_ref, land, ss, rs, ls):
    R = a_ref.shape[0]
    start, wait = save_blocks(land, all_ref, ls)

    def work(b):
        start(b)
        rows = pl.ds(pl.multiple_of(b * R, 16), R)
        gs = jnp.dot(land[b], w_ref[...], preferred_element_type=F32)
        o_ref[rows, :] = (gs * 2.0 * lift_ref[rows, :]).astype(BF)

    t = run_gather(a_ref, land, ss, rs, work)
    wait()
    t.finish()


def value_back(a, w, lift, cid):
    R, C = a.shape
    units = w.shape[1]
    return pl.pallas_call(
        back_kernel,
        out_shape=(jax.ShapeDtypeStruct((16 * R, C), BF), jax.ShapeDtypeStruct((16 * R, units), BF)),
        in_specs=[pl.BlockSpec(memory_space=VMEM)] * 3,
        out_specs=(pl.BlockSpec(memory_space=pl.ANY), pl.BlockSpec(memory_space=VMEM)),
        scratch_shapes=[VMEM((16, R, C), BF), DMA((18,)), DMA((18,)), DMA((16,))],
        compiler_params=pltpu.CompilerParams(collective_id=cid, has_side_effects=True, vmem_limit_bytes=48 * 2**20),
        name="gather_value_back",
    )(a, w, lift)


def sum_kernel(l_ref, w_ref, o_ref, pa, cb, zt, xs, zf, hv, xf, ss, rs):
    p = Place()
    t = Traffic(p, ss, rs)
    R = o_ref.shape[0]
    H = R // 2
    core, xp, xm, zz = p.at(dc=1), p.at(dx=1), p.at(dx=-1), p.at(dz=1)
    order = [(2, 1), (-1, 1), (1, 1), (2, 0), (0, 1), (1, 0), (-1, 0), (0, 0)]
    greet(p, [core, xp, xm, zz])

    def term(i, dc):
        b = p.at(order[i][0], order[i][1], dc)
        rows = l_ref[pl.ds(pl.multiple_of(b * R, 16), R), :]
        return jnp.dot(rows, w_ref[...], preferred_element_type=F32)

    def give(i):
        pa[i, 0] = term(i, 1).astype(BF)
        t.send(i, pa.at[i, 0], cb.at[i], core)

    def pair(i):
        pa[i, 1] = term(i, 0).astype(BF)
        t.landed(i, cb.at[i])
        pa[i, 1] = (pa[i, 1].astype(F32) + cb[i].astype(F32)).astype(BF)

    upper, lower = pl.ds(0, H), pl.ds(H, H)
    give(0)
    give(1)
    pair(0)
    t.send(8, pa.at[0, 1], zt, zz)
    give(2)
    pair(1)
    t.send(9, pa.at[1, 1], xs.at[1], xm)
    give(3)
    pair(2)
    t.send(10, pa.at[2, 1], xs.at[0], xp)
    give(4)
    give(5)
    pair(3)
    give(6)
    pair(4)
    pair(5)
    t.send(11, pa.at[5, 1, lower], xf.at[0, lower], xp)
    give(7)
    pair(6)
    t.send(12, pa.at[6, 1, upper], xf.at[1, upper], xm)
    pair(7)
    t.landed(8, zt)
    pa[3, 1] = (pa[3, 1].astype(F32) + zt[...].astype(F32)).astype(BF)
    t.send(13, pa.at[3, 1, upper], hv.at[0], xp)
    t.send(14, pa.at[3, 1, lower], hv.at[1], xm)
    t.landed(9, xs.at[1])
    t.landed(10, xs.at[0])
    pa[4, 1] = (pa[4, 1].astype(F32) + xs[0].astype(F32) + xs[1].astype(F32)).astype(BF)
    t.send(15, pa.at[4, 1], zf, zz)
    t.landed(13, hv.at[0])
    pa[5, 1, upper] = (pa[5, 1, upper].astype(F32) + hv[0].astype(F32)).astype(BF)
    t.send(16, pa.at[5, 1, upper], xf.at[0, upper], xp)
    t.landed(14, hv.at[1])
    pa[6, 1, lower] = (pa[6, 1, lower].astype(F32) + hv[1].astype(F32)).astype(BF)
    t.send(17, pa.at[6, 1, lower], xf.at[1, lower], xm)
    t.landed(11, xf.at[0, lower])
    t.landed(12, xf.at[1, upper])
    t.landed(15, zf)
    o_ref[...] = pa[7, 1].astype(F32) + zf[...].astype(F32)
    t.landed(16, xf.at[0, upper])
    t.landed(17, xf.at[1, lower])
    o_ref[...] = o_ref[...] + xf[0].astype(F32) + xf[1].astype(F32)
    t.finish()


def matmul_sum(l, w, cid):
    R, C = l.shape[0] // 16, w.shape[1]
    return pl.pallas_call(
        sum_kernel,
        out_shape=jax.ShapeDtypeStruct((R, C), F32),
        in_specs=[pl.BlockSpec(memory_space=VMEM)] * 2,
        out_specs=pl.BlockSpec(memory_space=VMEM),
        scratch_shapes=[
            VMEM((8, 2, R, C), BF), VMEM((8, R, C), BF), VMEM((R, C), BF), VMEM((2, R, C), BF), VMEM((R, C), BF),
            VMEM((2, R // 2, C), BF), VMEM((2, R, C), BF), DMA((18,)), DMA((18,)),
        ],
        compiler_params=pltpu.CompilerParams(collective_id=cid, has_side_effects=True, vmem_limit_bytes=48 * 2**20),
        name="matmul_sum",
    )(l, w)


def swap_kernel(a_ref, o_ref, ss, rs, ls):
    p = Place()
    n = 16
    greet(p, [(p.s + k) % n for k in range(1, n)])
    cps = []
    for k in range(1, n):
        to = (p.s + k) % n
        cp = pltpu.make_async_remote_copy(src_ref=a_ref.at[to], dst_ref=o_ref.at[p.s], send_sem=ss.at[k], recv_sem=rs.at[k], device_id=p.dev(to), device_id_type=MESH)
        cp.start()
        cps.append(cp)
    own = pltpu.make_async_copy(a_ref.at[p.s], o_ref.at[p.s], ls.at[0])
    own.start()
    own.wait()
    for cp in cps:
        cp.wait()


def swap(a, cid, space=VMEM):
    n = a.shape[0]
    return pl.pallas_call(
        swap_kernel,
        out_shape=jax.ShapeDtypeStruct(a.shape, a.dtype),
        in_specs=[pl.BlockSpec(memory_space=space)],
        out_specs=pl.BlockSpec(memory_space=space),
        scratch_shapes=[DMA((n,)), DMA((n,)), DMA((1,))],
        compiler_params=pltpu.CompilerParams(collective_id=cid, has_side_effects=True),
        name="swap_blocks",
    )(a)


def vec_kernel(nd, a_ref, o_ref, b1, t1, b2, ss, rs, ss2, rs2):
    p = Place()
    n = 16
    d = p.dp
    barrier = pltpu.get_barrier_semaphore()
    for k in range(1, n):
        pl.semaphore_signal(barrier, inc=1, device_id=(d, (p.s + k) % n), device_id_type=MESH)
    for k in range(1, nd):
        pl.semaphore_signal(barrier, inc=1, device_id=((d + k) % nd, p.s), device_id_type=MESH)
    pl.semaphore_wait(barrier, n + nd - 2)
    cps = []
    for k in range(1, n):
        to = (p.s + k) % n
        cp = pltpu.make_async_remote_copy(src_ref=a_ref.at[to], dst_ref=b1.at[k - 1], send_sem=ss.at[k], recv_sem=rs.at[k], device_id=(d, to), device_id_type=MESH)
        cp.start()
        cps.append(cp)
    total = a_ref[p.s]
    for k in range(1, n):
        cps[k - 1].wait_recv()
        total = total + b1[k - 1]
    t1[...] = total
    cps2 = []
    for k in range(1, nd):
        to = (d + k) % nd
        cp = pltpu.make_async_remote_copy(src_ref=t1.at[to], dst_ref=b2.at[k - 1], send_sem=ss2.at[k], recv_sem=rs2.at[k], device_id=(to, p.s), device_id_type=MESH)
        cp.start()
        cps2.append(cp)
    acc = t1[d]
    for k in range(1, nd):
        cps2[k - 1].wait_recv()
        acc = acc + b2[k - 1]
    o_ref[...] = acc
    for cp in cps + cps2:
        cp.wait_send()


def vec_sum(a, cid):
    n, nd = a.shape[:2]
    piece = a.shape[2:]
    return pl.pallas_call(
        functools.partial(vec_kernel, nd),
        out_shape=jax.ShapeDtypeStruct(piece, a.dtype),
        in_specs=[pl.BlockSpec(memory_space=VMEM)],
        out_specs=pl.BlockSpec(memory_space=VMEM),
        scratch_shapes=[VMEM((n - 1, nd) + piece, a.dtype), VMEM((nd,) + piece, a.dtype), VMEM((max(nd - 1, 1),) + piece, a.dtype), DMA((n,)), DMA((n,)), DMA((nd,)), DMA((nd,))],
        compiler_params=pltpu.CompilerParams(collective_id=cid, has_side_effects=True),
        name="sum_vectors",
    )(a)


CHUNK = 128


def halves(a):
    high = a.astype(BF)
    return high, (a - high.astype(F32)).astype(BF)


def dot3(a, b, dims):
    def one(x, y):
        return lax.dot_general(x, y, (dims, ((), ())), preferred_element_type=F32)

    return one(a[0], b[0]) + (one(a[0], b[1]) + one(a[1], b[0]))


NN, NT, TN = ((1,), (0,)), ((1,), (1,)), ((0,), (0,))


def head_sums(a, ones):
    high, rest = a.astype(BF), a - a.astype(BF).astype(F32)
    mid = rest.astype(BF)
    low = (rest - mid.astype(F32)).astype(BF)

    def one(x):
        return lax.dot_general(x, ones, (NN, ((), ())), preferred_element_type=F32)

    return one(high) + (one(mid) + one(low))


def iota(shape, dim):
    return lax.broadcasted_iota(jnp.int32, shape, dim)


def head_ones(width, dtype):
    return (iota((width, width), 0) // ATTENTION_WIDTH == iota((width, width), 1) // ATTENTION_WIDTH).astype(dtype)


def by_head(pair):
    lane = iota(pair[0].shape, 1) // ATTENTION_WIDTH
    heads = pair[0].shape[1] // ATTENTION_WIDTH
    zero = jnp.zeros_like(pair[0])
    return tuple(jnp.concatenate([jnp.where(lane == h, a, zero) for h in range(heads)], axis=0) for a in pair)


def pick_heads(a, rows):
    lane = iota((rows, a.shape[1]), 1) // ATTENTION_WIDTH
    out = a[:rows]
    for h in range(1, a.shape[1] // ATTENTION_WIDTH):
        out = jnp.where(lane == h, a[h * rows : (h + 1) * rows], out)
    return out


def powers(lam, tab):
    L = tab.shape[1]
    at = iota((L, 1), 0).astype(F32)
    mid = L // 2
    tab[0] = jnp.exp(lam * (at - mid))
    tab[1] = jnp.exp(-lam * (at + (1.0 - mid)))
    tab[2] = jnp.exp(lam * at)
    tab[3] = jnp.exp(lam * (L - 1.0 - at))


def chunk_mask(col, row):
    L = col.shape[0]
    return (iota((L, L), 1) < iota((L, L), 0)) & (col == row)


def forward_kernel(x_ref, col_ref, row_ref, keep_ref, vec_ref, z_ref, o_ref, s_ref, tab, state):
    chunks, L = row_ref.shape[0], row_ref.shape[2]
    W = vec_ref.shape[1]
    heads = W // ATTENTION_WIDTH
    lam, bonus, gain, bias = (vec_ref[q : q + 1, :] for q in range(4))
    powers(lam, tab)
    ones = head_ones(W, BF)
    diag = head_ones(W, F32)
    decay = vec_ref[8 : 8 + W, :]
    state[...] = jnp.zeros_like(state)

    def step(i, unused):
        rows = pl.ds(pl.multiple_of(i * L, L), L)
        r, k, v, p = (x_ref[rows, q * W : (q + 1) * W] for q in range(4))
        col = col_ref[rows, :]
        seg, kept, tail = col[:, 0:1], col[:, 1:2], col[:, 2:3]
        mask = chunk_mask(seg, row_ref[i])
        mask = jnp.concatenate([mask] * heads, axis=1)
        rs, ks = halves(r * tab[0]), halves(k * tab[1])
        scores = jnp.where(mask, dot3(rs, by_head(ks), NT), 0.0)
        vh = halves(v)
        out = dot3(halves(scores), by_head(vh), NN) + head_sums(r * k * bonus, ones) * v
        memory = state[...]
        s_ref[i] = memory
        out = out + kept * dot3(halves(r * tab[2]), halves(memory), NN)
        state[...] = keep_ref[i] * decay * memory + diag * dot3(halves(k * tab[3] * tail), vh, TN)
        o_ref[rows, :] = out
        center = out - head_sums(out, ones) * (1.0 / ATTENTION_WIDTH)
        spread = head_sums(center * center, ones) * (1.0 / ATTENTION_WIDTH)
        normed = center * lax.rsqrt(spread + 0.00064) * gain + bias
        z_ref[rows, :] = (normed * (p * (1.0 / (1.0 + jnp.exp(-p))))).astype(BF)
        return 0

    lax.fori_loop(0, chunks, step, 0, unroll=2)


def recurrence(x, cols, rows, keep, vec):
    T, W = x.shape[0], vec.shape[1]
    chunks, L = rows.shape[0], rows.shape[2]
    return pl.pallas_call(
        forward_kernel,
        out_shape=(jax.ShapeDtypeStruct((T, W), BF), jax.ShapeDtypeStruct((T, W), F32), jax.ShapeDtypeStruct((chunks, W, W), F32)),
        in_specs=[pl.BlockSpec(memory_space=VMEM)] * 3 + [pl.BlockSpec(memory_space=pltpu.SMEM), pl.BlockSpec(memory_space=VMEM)],
        out_specs=(pl.BlockSpec(memory_space=VMEM),) * 3,
        scratch_shapes=[VMEM((4, L, W), F32), VMEM((W, W), F32)],
        compiler_params=pltpu.CompilerParams(vmem_limit_bytes=40 * 2**20),
        name="recurrence",
    )(x, cols, rows, keep, vec)


def backward_kernel(x_ref, o_ref, s_ref, gz_ref, col_ref, row_ref, keep_ref, vec_ref, g_ref, sums_ref, tab, grad_state, acc, carry):
    chunks, L = row_ref.shape[0], row_ref.shape[2]
    W = vec_ref.shape[1]
    heads = W // ATTENTION_WIDTH
    lam, bonus, gain, bias = (vec_ref[q : q + 1, :] for q in range(4))
    powers(lam, tab)
    ones = head_ones(W, BF)
    diag = head_ones(W, F32)
    decay = vec_ref[8 : 8 + W, :]
    at = iota((L, 1), 0).astype(F32)
    mid = float(L // 2)
    grad_state[...] = jnp.zeros_like(grad_state)
    acc[...] = jnp.zeros_like(acc)
    carry[...] = jnp.zeros_like(carry)
    sums_ref[...] = jnp.zeros_like(sums_ref)

    def add(q, term):
        sums_ref[q : q + 1, :] += jnp.sum(term, axis=0, keepdims=True)

    def step(n, unused):
        i = chunks - 1 - n
        rows = pl.ds(pl.multiple_of(i * L, L), L)
        r, k, v, p = (x_ref[rows, q * W : (q + 1) * W] for q in range(4))
        col = col_ref[rows, :]
        seg, kept, tail, same_next = col[:, 0:1], col[:, 1:2], col[:, 2:3], col[:, 3:4]
        o = o_ref[rows, :]
        gz = gz_ref[rows, :].astype(F32)
        center = o - head_sums(o, ones) * (1.0 / ATTENTION_WIDTH)
        spread = head_sums(center * center, ones) * (1.0 / ATTENTION_WIDTH)
        scale = lax.rsqrt(spread + 0.00064)
        normed = center * scale
        gate = 1.0 / (1.0 + jnp.exp(-p))
        silu = p * gate
        gy = gz * silu
        gp = gz * (normed * gain + bias) * (gate * (1.0 + p * (1.0 - gate)))
        add(2, gy * normed)
        add(3, gy)
        gn = gy * gain
        go = scale * (
            gn
            - head_sums(gn, ones) * (1.0 / ATTENTION_WIDTH)
            - normed * (head_sums(gn * normed, ones) * (1.0 / ATTENTION_WIDTH))
        )
        mask = chunk_mask(seg, row_ref[i])
        mask = jnp.concatenate([mask] * heads, axis=1)
        rs_f, ks_f = r * tab[0], k * tab[1]
        r0_f, ke_f = r * tab[2] * kept, k * tab[3] * tail
        rs, ks, vh, goh = halves(rs_f), halves(ks_f), halves(v), halves(go)
        ks_by, v_by = by_head(ks), by_head(vh)
        scores = halves(jnp.where(mask, dot3(rs, ks_by, NT), 0.0))
        grad_scores = halves(jnp.where(mask, dot3(goh, v_by, NT), 0.0))
        memory = s_ref[i]
        gs = grad_state[...]
        mh, gsh = halves(memory), halves(gs)
        reward = head_sums(r * k * bonus, ones)
        grad_reward = head_sums(go * v, ones)
        g_rs = dot3(grad_scores, ks_by, NN)
        g_r0 = dot3(goh, mh, NT)
        g_ks = pick_heads(dot3(grad_scores, rs, TN), L)
        g_ke = dot3(vh, gsh, NT)
        gv = pick_heads(dot3(scores, goh, TN), L) + reward * go + dot3(halves(ke_f), gsh, NN)
        keep = keep_ref[i]
        acc[...] += keep * memory * gs
        grad_state[...] = keep * decay * gs + diag * dot3(halves(r0_f), goh, TN)
        gr = g_rs * tab[0] + g_r0 * (tab[2] * kept) + grad_reward * bonus * k
        gk = g_ks * tab[1] + g_ke * (tab[3] * tail) + grad_reward * bonus * r
        add(1, grad_reward * r * k)
        add(0, (at - mid) * (g_rs * rs_f) - (at + (1.0 - mid)) * (g_ks * ks_f) + at * (g_r0 * r0_f) + (L - 1.0 - at) * (g_ke * ke_f))
        grads = jnp.concatenate([gr, gk, gv, gp], axis=1).astype(BF).astype(F32)
        last = iota((L, 1), 0) == L - 1
        after = jnp.where(last, carry[0:1, :], pltpu.roll(grads, L - 1, 0)) * same_next
        carry[0:1, :] = grads[0:1, :]
        g_ref[rows, : 4 * W] = grads.astype(BF)
        g_ref[rows, 4 * W :] = after.astype(BF)
        return 0

    lax.fori_loop(0, chunks, step, 0)
    whole = dot3(halves(jnp.ones((8, W), F32)), halves(acc[...] * decay), NT)
    sums_ref[0:1, :] = (sums_ref[0:1, :] + L * whole[0:1, :]) * lam


def recurrence_back(x, o, states, gz, cols, rows, keep, vec):
    T, W = x.shape[0], vec.shape[1]
    chunks, L = rows.shape[0], rows.shape[2]
    return pl.pallas_call(
        backward_kernel,
        out_shape=(jax.ShapeDtypeStruct((T, 8 * W), BF), jax.ShapeDtypeStruct((8, W), F32)),
        in_specs=[pl.BlockSpec(memory_space=VMEM)] * 6 + [pl.BlockSpec(memory_space=pltpu.SMEM), pl.BlockSpec(memory_space=VMEM)],
        out_specs=(pl.BlockSpec(memory_space=VMEM),) * 2,
        scratch_shapes=[VMEM((4, L, W), F32), VMEM((W, W), F32), VMEM((W, W), F32), VMEM((8, 4 * W), F32)],
        compiler_params=pltpu.CompilerParams(vmem_limit_bytes=48 * 2**20),
        name="recurrence_back",
    )(x, o, states, gz, cols, rows, keep, vec)


def layer_norm(tensor, gain_row, bias_row):
    center = tensor - jnp.mean(tensor, axis=-1, keepdims=True)
    spread = jnp.mean(center * center, axis=-1, keepdims=True)
    return center * lax.rsqrt(spread + 1e-05) * gain_row + bias_row


def earlier(tensor):
    return jnp.concatenate([tensor[1:], jnp.zeros_like(tensor[:1])], axis=0)


def contract(left, right, left_dim, right_dim):
    return lax.dot_general(left, right, (((left_dim,), (right_dim,)), ((), ())), preferred_element_type=F32)


def body(nd, inputs, cotangent, mix_weights, out_weight, key_weight, value_weight, recept_weight, vectors, segment_ids):
    tokens, width = inputs.shape
    group = segment_ids.shape[0]
    cols = mix_weights.shape[2]
    s = lax.axis_index("sp")
    ring = group // tokens
    own = lax.dynamic_slice_in_dim(vectors, s * cols, cols, 1)
    same = jnp.concatenate([jnp.zeros((1,), F32), (segment_ids[1:] == segment_ids[:-1]).astype(F32)])
    same_next = earlier(same)
    here = s * tokens
    same_here = lax.dynamic_slice_in_dim(same, here, tokens, 0)[:, None]
    mu = vectors[2:6]
    nu_k, nu_r = vectors[12], vectors[13]

    out_full = lax.all_gather(out_weight, "sp", axis=0, tiled=True)
    recept_full = lax.all_gather(recept_weight.T, "sp", axis=0, tiled=True)

    mix_f = mix_weights.astype(F32)
    folded = jnp.concatenate(
        [((1.0 - mu)[:, :, None] * mix_f).astype(BF), (mu[:, :, None] * mix_f).astype(BF)], axis=0
    )
    folded = folded.transpose(0, 2, 1).reshape(8 * cols, width)
    x = inputs.astype(F32)
    n1 = layer_norm(x, vectors[0], vectors[1]).astype(BF)
    half = 4 * cols
    n1_all, projected = project(n1, mix_weights, mu, same[:, None], 0)

    chunks = group // CHUNK
    seg = segment_ids.reshape(chunks, CHUNK)
    last = seg[:, CHUNK - 1 :]
    prior = jnp.concatenate([jnp.full((1, 1), -1, jnp.int32), last[:-1]], axis=0)
    tok_cols = jnp.stack(
        [t.astype(F32).reshape(group) for t in (seg, seg == prior, seg == last, same_next.reshape(seg.shape))], axis=1
    )
    tok_rows = seg.astype(F32)[:, None, :]
    keep = (last == prior).astype(F32).reshape(chunks)
    lam = -jnp.exp(own[6])
    decay = jnp.broadcast_to(jnp.exp(lam * CHUNK)[:, None], (cols, cols))
    vec = jnp.concatenate([lam[None], own[7:10], jnp.zeros((4, cols), F32), decay], axis=0)
    z, mixed_time, states = recurrence(projected, tok_cols, tok_rows, keep, vec)

    z_here = swap(z.reshape(ring, tokens, cols), 1).transpose(1, 0, 2).reshape(tokens, width)
    hidden = x + jnp.dot(z_here, out_full, preferred_element_type=F32)
    n2 = layer_norm(hidden, vectors[10], vectors[11]).astype(BF)

    n2_all, key_in, lifted, squared = key_side(n2, key_weight, nu_k[None], same[:, None], 2)
    before = lax.dynamic_slice_in_dim(n2_all, jnp.maximum(here - 1, 0), 1, 0)
    n2_f = n2.astype(F32)
    shift_here = jnp.concatenate([before, n2[:-1]], axis=0).astype(F32) * same_here - n2_f
    recept_in = (n2_f + shift_here * nu_r).astype(BF)
    value_here = matmul_sum(squared, value_weight, 3)
    gate = jax.nn.sigmoid(contract(recept_in, recept_full, 1, 1))
    channel = (gate * value_here).astype(BF)
    result = (hidden + channel.astype(F32)).astype(BF)

    g = cotangent.astype(F32)
    grad_value = (g * gate).astype(BF)
    grad_recept = (g * value_here * (gate * (1.0 - gate))).astype(BF)
    grad_value_all, grad_key = value_back(grad_value, value_weight.T, lifted, 4)
    key_back = matmul_sum(grad_key, key_weight.T, 5)
    value_grad = contract(squared, grad_value_all, 0, 0)
    key_grad = contract(key_in, grad_key, 0, 0)
    recept_cols = swap(grad_recept.reshape(tokens, ring, cols).transpose(1, 0, 2), 6).reshape(group, cols)
    recept_two = jnp.concatenate([recept_cols, earlier(recept_cols) * same_next[:, None].astype(BF)], axis=1)
    recept_np = contract(n2_all, recept_two, 0, 0)
    recept_grad = (1.0 - nu_r)[:, None] * recept_np[:, :cols] + nu_r[:, None] * recept_np[:, cols:]
    recept_back = contract(grad_recept, recept_full, 1, 0)
    nu_k_grad = jnp.sum(key_back * shift_here, axis=0)
    nu_r_grad = jnp.sum(recept_back * shift_here, axis=0)
    moved = (key_back * nu_k + recept_back * nu_r) * same_here
    after = lax.ppermute(moved[:1], "sp", [(i, i - 1) for i in range(1, ring)])
    grad_n2 = key_back * (1.0 - nu_k) + recept_back * (1.0 - nu_r) + jnp.concatenate([moved[1:], after], axis=0)
    unused, pull_two = jax.vjp(layer_norm, hidden, vectors[10], vectors[11])
    grad_hidden, gain_two, bias_two = pull_two(grad_n2)
    grad_hidden = g + grad_hidden

    grad_hidden_b = grad_hidden.astype(BF)
    gz_here = contract(grad_hidden_b, out_full, 1, 1).astype(BF)
    gz = swap(gz_here.reshape(tokens, ring, cols).transpose(1, 0, 2), 7).reshape(group, cols)
    grad_hidden_all = lax.all_gather(grad_hidden_b, "sp", axis=0, tiled=True)
    grads_two, head_sums_grad = recurrence_back(projected, mixed_time, states, gz, tok_cols, tok_rows, keep, vec)
    mix_np = contract(n1_all, grads_two, 0, 0)
    mix_n = mix_np[:, :half].reshape(width, 4, cols).transpose(1, 0, 2)
    mix_p = mix_np[:, half:].reshape(width, 4, cols).transpose(1, 0, 2)
    mix_d = mix_p - mix_n
    mix_grad = mix_n + mu[:, :, None] * mix_d
    mu_grads = jnp.sum(mix_f * mix_d, axis=2)
    n1_back = matmul_sum(grads_two, folded, 8)
    out_grad = contract(z, grad_hidden_all, 0, 0)
    unused, pull_one = jax.vjp(layer_norm, x, vectors[0], vectors[1])
    grad_x, gain_one, bias_one = pull_one(n1_back)
    input_grad = grad_hidden + grad_x

    def place(part):
        return lax.dynamic_update_slice_in_dim(jnp.zeros((width,), F32), part, s * cols, 0)

    terms = jnp.stack(
        [gain_one, bias_one, mu_grads[0], mu_grads[1], mu_grads[2], mu_grads[3]]
        + [place(head_sums_grad[q]) for q in range(4)]
        + [gain_two, bias_two, nu_k_grad, nu_r_grad]
    )
    rows, piece = terms.shape[0], width // (nd * ring)
    terms = terms.reshape(rows, nd, ring, piece).transpose(2, 1, 0, 3).reshape(ring, nd, rows * piece)
    packed = -(-rows * piece // 1024) * 1024
    terms = jnp.pad(terms, ((0, 0), (0, 0), (0, packed - rows * piece))).reshape(ring, nd, packed // 128, 128)
    vectors_grad = vec_sum(terms, 9).reshape(packed)[: rows * piece].reshape(rows, piece)

    def over_dp(grad, dim):
        return lax.psum_scatter(grad.astype(BF), "dp", scatter_dimension=dim, tiled=True).astype(F32)

    return (
        result,
        input_grad,
        over_dp(mix_grad, 1),
        over_dp(out_grad, 1),
        over_dp(key_grad, 0),
        over_dp(value_grad, 1),
        over_dp(recept_grad, 0),
        vectors_grad,
    )


def solution(mesh):
    placed = (
        P(("dp", "sp"), None),
        P(("dp", "sp"), None),
        P(None, None, "sp"),
        P("sp", None),
        P(None, "sp"),
        P("sp", None),
        P(None, "sp"),
        P(),
        P("dp"),
    )
    return jax.shard_map(
        functools.partial(body, mesh.shape["dp"]),
        mesh=mesh,
        in_specs=placed,
        out_specs=(
            P(("dp", "sp"), None),
            P(("dp", "sp"), None),
            P(None, "dp", "sp"),
            P("sp", "dp"),
            P("dp", "sp"),
            P("sp", "dp"),
            P("dp", "sp"),
            P(None, ("dp", "sp")),
        ),
        check_vma=False,
    )
```

time: 762 us -> 686 us (0.900)
  matrix products: 193 us -> 68.7 us
  Pallas kernels: 342 us -> 421 us
  other arithmetic: 79.3 us -> 37.7 us
  waiting for transfers between devices: 17.2 us -> 56.2 us
  local copies, waits for them, and re-layouts: 106 us -> 73.4 us
    dot_general x19 -> x0, matrix products: 113 us -> none  [the longest x4 35.4 us: body(): jnp.dot((n1_f + shift_one * mu[q]).astype(BF), mix_weights[q], preferred_...]
    pallas_call x8, Pallas kernels: 274 us -> 346 us  [the longest x3 147 us: matmul_sum(): pl.pallas_call(sum_kernel, out_shape=jax.ShapeDtypeStruct((R, C), F32), i...]
    reduce_scatter x5, waiting for transfers between devices: 14.1 us -> 53 us  [over_dp(): lax.psum_scatter(grad.astype(BF), 'dp', scatter_dimension=dim, tiled=True)]
    convert_element_type x6 -> x4, other arithmetic: 29.3 us -> 2.39 us  [the longest x2 1.47 us: body(): t.astype(F32).reshape(group)]
    reduce_sum x9 -> x0, other arithmetic: 15.7 us -> none  [the longest x1 4.81 us: block_output(): out = out + reward[:, :, None] * v]
    dot_general x10 -> x8, matrix products: 75.7 us -> 63.8 us  [contract(): lax.dot_general(left, right, (((left_dim,), (right_dim,)), ((), ())), pre...]
    pallas_call x3, Pallas kernels: 46 us -> 55.7 us  [swap(): pl.pallas_call(swap_kernel, out_shape=jax.ShapeDtypeStruct(a.shape, a.dty...]
    another operation x3 -> x1, local copies, waits for them, and re-layouts: 9.21 us -> 0.37 us  [body(): jnp.stack([t.astype(F32).reshape(group) for t in (seg, seg == prior, seg...]
  transfers between devices with their start and end apart: 9 -> 9, of which waited for: 2 -> 3; matrix products, arithmetic and copies ran while one was open for 41% -> 22% of each run, Pallas kernels for 25% -> 51%
where the time goes in v2:
time: 686 us; the launch traced here: 674 us
  Pallas kernels  421 us (61%)
  local copies, waits for them, and re-layouts  73.4 us (11%)
  matrix products  68.7 us (10%)
  waiting for transfers between devices  56.2 us (8%)
  other arithmetic  37.7 us (5%)
  between operations  15.3 us (2%)
    pallas_call x3, Pallas kernels, matmul_sum(): pl.pallas_call(sum_kernel, out_shape=jax.ShapeDtypeStruct((R, C), F32), i...  147 us
    dot_general x8, matrix products, contract(): lax.dot_general(left, right, (((left_dim,), (right_dim,)), ((), ())), pre...  63.8 us
    pallas_call x1, Pallas kernels, project(): pl.pallas_call(project_kernel, out_shape=(jax.ShapeDtypeStruct((16 * R, C...  63.7 us
    pallas_call x1, Pallas kernels, key_side(): pl.pallas_call(key_kernel, out_shape=(jax.ShapeDtypeStruct((16 * R, C), B...  61.7 us
    pallas_call x3, Pallas kernels, swap(): pl.pallas_call(swap_kernel, out_shape=jax.ShapeDtypeStruct(a.shape, a.dty...  55.7 us
    reduce_scatter x5, waiting for transfers between devices, over_dp(): lax.psum_scatter(grad.astype(BF), 'dp', scatter_dimension=dim, tiled=True)  53 us
    pallas_call x1, Pallas kernels, value_back(): pl.pallas_call(back_kernel, out_shape=(jax.ShapeDtypeStruct((16 * R, C),...  38.4 us
    unnamed x88, local copies, waits for them, and re-layouts  27 us
  transfers between devices with their start and end apart: 9, of which 3 were waited for; matrix products, arithmetic and copies ran while one was open for 22% of the time, Pallas kernels for 51%

profile of v2, /device:TPU:0, one launch (start us, length us, event | category | flops | bytes accessed | tf_op | source)
XLA Modules:
  0.0 674.3 jit_solution(17187857260897903465)
XLA Ops:
  9.6 0.8 dynamic-slice.1
  11.9 0.8 fusion.32
  12.8 0.9 slice_reduce_fusion
  13.7 0.8 fusion.33
  15.3 4.2 copy.76.w_ref
  19.5 3.9 copy.78
  24.9 1.6 copy-done.3
  26.5 63.7 %gather_project.1 = (bf16[2048,2048]{1,0:T(8,128)(2,1)}, f32[2048,512]{1,0:T(8,128)}) custom-call(bf16[128,2048]{1,0:T(8,128)(2,1)S(1)} %fusion.14.a_ref, bf16[4,2048,128]{2,1,0:T(8,128)(2,1)S(1)} %copy-done.3, f32[4,2048]{1,0:T(4,128)S(1)} %get-tuple-element.59.mu_ref, f32[2048,1]{1,0:T(8,128)S(1)} %copy.73.same_ref), custom_call_target="tpu_custom_call" | custom-call | tf_op jit(solution)/shard_map/gather_project/pallas_call | solution.py:197
  90.5 2.2 copy-done
  92.7 11.8 %recurrence.1 = (bf16[2048,128]{1,0:T(8,128)(2,1)S(1)}, f32[2048,128]{1,0:T(8,128)S(1)}, f32[16,128,128]{2,1,0:T(8,128)S(1)}) custom-call(f32[2048,512]{1,0:T(8,128)S(1)} %copy-done, f32[2048,4]{1,0:T(8,128)S(1)} %copy.74.col_ref, f32[16,1,128]{2,1,0:T(1,128)S(1)} %bitcast.87, f32[16]{0:T(128)S(1)} %convert_reduce_fusion.1.keep_ref, ...), custom_call_target="tpu_custom_call" | custom-call | tf_op jit(solution)/shard_map/recurrence/pallas_call | solution.py:566
  104.5 0.8 copy-done.7
  105.3 1.0 copy-done.14
  106.3 1.0 copy-done.16
  107.2 17.9 %swap_blocks.3 = bf16[16,128,128]{2,1,0:T(8,128)(2,1)} custom-call(bf16[16,128,128]{2,1,0:T(8,128)(2,1)} %bitcast.84), custom_call_target="tpu_custom_call" | custom-call | tf_op jit(solution)/shard_map/swap_blocks/pallas_call | solution.py:399
  125.1 1.3 copy.75
  126.5 4.9 fusion.48
  131.7 1.1 add_convert_fusion.1.a_ref
  132.7 61.7 %gather_key.1 = (bf16[2048,2048]{1,0:T(8,128)(2,1)}, bf16[2048,2048]{1,0:T(8,128)(2,1)}, f32[2048,448]{1,0:T(8,128)}, bf16[2048,448]{1,0:T(8,128)(2,1)}) custom-call(bf16[128,2048]{1,0:T(8,128)(2,1)} %add_convert_fusion.1.a_ref, bf16[2048,448]{1,0:T(8,128)(2,1)} %copy.76.w_ref, f32[1,2048]{1,0:T(1,128)} %get-tuple-element.67.nu_ref, f32[2048,1]{1,0:T(8,128)} %copy-done.1), custom_call_target="tpu_custom_call" | custom-call | tf_op jit(solution)/shard_map/gather_key/pallas_call | solution.py:250
  194.4 1.7 copy-done.11
  196.1 40.5 %matmul_sum.3 = f32[128,2048]{1,0:T(8,128)S(1)} custom-call(bf16[2048,448]{1,0:T(8,128)(2,1)S(1)} %copy-done.11, bf16[448,2048]{1,0:T(8,128)(2,1)S(1)} %copy-done.5), custom_call_target="tpu_custom_call" | custom-call | tf_op jit(solution)/shard_map/matmul_sum/pallas_call | solution.py:366
  236.6 0.8 constant_dynamic-slice_fusion
  237.4 6.7 fusion.21
  244.1 38.4 %gather_value_back.1 = (bf16[2048,2048]{1,0:T(8,128)(2,1)}, bf16[2048,448]{1,0:T(8,128)(2,1)S(1)}) custom-call(bf16[128,2048]{1,0:T(8,128)(2,1)S(1)} %get-tuple-element.57.a_ref, bf16[2048,448]{1,0:T(8,128)(2,1)S(1)} %bitcast.82, f32[2048,448]{1,0:T(8,128)} %get-tuple-element.25.lift_ref), custom_call_target="tpu_custom_call" | custom-call | tf_op jit(solution)/shard_map/gather_value_back/pallas_call | solution.py:284
  282.5 40.0 %matmul_sum.4 = f32[128,2048]{1,0:T(8,128)S(1)} custom-call(bf16[2048,448]{1,0:T(8,128)(2,1)S(1)} %get-tuple-element.26.l_ref, bf16[448,2048]{1,0:T(8,128)(2,1)S(1)} %bitcast.83), custom_call_target="tpu_custom_call" | custom-call | tf_op jit(solution)/shard_map/matmul_sum/pallas_call | solution.py:366
  322.6 6.5 multiply_reduce_fusion
  329.1 1.3 collective-permute-start
  330.5 1.7 collective-permute-done
  333.2 1.1 fusion.28
  334.9 1.3 copy.85
  336.2 1.0 copy.86
  337.2 18.6 %swap_blocks.5 = bf16[16,128,128]{2,1,0:T(8,128)(2,1)} custom-call(bf16[16,128,128]{2,1,0:T(8,128)(2,1)} %bitcast.98), custom_call_target="tpu_custom_call" | custom-call | tf_op jit(solution)/shard_map/swap_blocks/pallas_call | solution.py:399
  355.8 1.2 slice.123
  357.4 6.1 fusion.24
  363.5 1.4 fusion.23
  364.9 9.4 %convolution_convert_fusion.1 = bf16[2048,448]{0,1:T(8,128)(2,1)} fusion(bf16[2048,2048]{1,0:T(8,128)(2,1)} %get-tuple-element.31, bf16[2048,448]{1,0:T(8,128)(2,1)} %copy-done.13), kind=kOutput, calls=%fused_computation.11 | convolution fusion | flops 3759013888 | bytes 12058624 | tf_op jit(solution)/shard_map/dot_general | solution.py:683
  374.4 9.0 %convolution_convert_fusion = bf16[448,2048]{1,0:T(8,128)(2,1)} fusion(bf16[2048,448]{1,0:T(8,128)(2,1)S(1)} %copy-done.12, bf16[2048,2048]{1,0:T(8,128)(2,1)} %get-tuple-element.32), kind=kOutput, calls=%fused_computation.10 | convolution fusion | flops 3759013888 | bytes 12058624 | tf_op jit(solution)/shard_map/dot_general | solution.py:683
  383.7 7.5 %convolution_convert_fusion.3 = bf16[128,2048]{1,0:T(8,128)(2,1)} fusion(bf16[128,2048]{1,0:T(8,128)(2,1)} %fusion.28, bf16[2048,2048]{1,0:T(8,128)(2,1)} %all-gather.4.cloned.1.call-done), kind=kOutput, calls=%fused_computation.18 | convolution fusion | flops 1074003968 | bytes 9437184 | tf_op jit(solution)/shard_map/dot_general | solution.py:683
  391.1 2.1 copy.79
  393.2 2.1 copy.80
  395.2 19.2 %swap_blocks.4 = bf16[16,128,128]{2,1,0:T(8,128)(2,1)} custom-call(bf16[16,128,128]{2,1,0:T(8,128)(2,1)} %bitcast.100), custom_call_target="tpu_custom_call" | custom-call | tf_op jit(solution)/shard_map/swap_blocks/pallas_call | solution.py:399
  414.5 1.0 copy-done.10
  415.5 23.4 %recurrence_back.1 = (bf16[2048,1024]{1,0:T(8,128)(2,1)}, f32[8,128]{1,0:T(8,128)S(1)}) custom-call(f32[2048,512]{1,0:T(8,128)} %get-tuple-element.21.x_ref, f32[2048,128]{1,0:T(8,128)S(1)} %copy-done.15, f32[16,128,128]{2,1,0:T(8,128)S(1)} %copy-done.17, bf16[2048,128]{1,0:T(8,128)(2,1)S(1)} %bitcast.85, f32[2048,4]{1,0:T(8,128)S(1)} %copy.74.col_ref, ...), custom_call_target="tpu_custom_call" | custom-call | tf_op jit(solution)/shard_map/recurrence_back/pallas_call | solution.py:661
  438.9 13.2 %fusion.49 = f32[2048,1024]{0,1:T(8,128)S(1)} fusion(bf16[2048,2048]{1,0:T(8,128)(2,1)} %get-tuple-element.30, bf16[2048,1024]{1,0:T(8,128)(2,1)} %get-tuple-element.29.l_ref), kind=kOutput, calls=%fused_computation.127 | convolution fusion | flops 8589934592 | bytes 20971520 | tf_op jit(solution)/shard_map/dot_general | solution.py:683
  452.1 3.8 fusion.47
  455.9 5.3 copy.84
  461.3 5.5 copy.83
  466.8 8.2 %fusion.2 = (f32[4,2048]{1,0:T(4,128)S(1)}, bf16[4,2048,128]{2,1,0:T(8,128)(2,1)}, bf16[4,2048,128]{2,1,0:T(8,128)(2,1)}, bf16[4,2048,128]{2,1,0:T(8,128)(2,1)}) fusion(bf16[4,2048,128]{2,1,0:T(8,128)(2,1)S(1)} %copy-done.4, f32[2048,4,128]{2,0,1:T(8,128)} %copy.83, f32[2048,4,128]{2,0,1:T(8,128)} %copy.84, f32[4,2048]{1,0:T(4,128)S(1)} %get-tuple-element.59.mu_ref, ...), kind=kLoop, calls=%fused_computation.5 | loop fusion | flops 11526144 | bytes 16875520 | tf_op jit(solution)/shard_map/reduce_sum | solution.py:772
  484.2 3.9 maximum_bitcast_fusion
  488.1 6.7 copy.82
  494.9 2.2 copy-done.9
  497.1 66.2 %matmul_sum.5 = f32[128,2048]{1,0:T(8,128)S(1)} custom-call(bf16[2048,1024]{1,0:T(8,128)(2,1)S(1)} %copy-done.9, bf16[1024,2048]{1,0:T(8,128)(2,1)} %bitcast.89), custom_call_target="tpu_custom_call" | custom-call | tf_op jit(solution)/shard_map/matmul_sum/pallas_call | solution.py:366
  570.2 5.5 convolution_convert_fusion.2
  577.0 2.7 copy.87
  579.7 1.6 reshape.229
  581.3 0.9 copy.90
  582.2 19.7 %sum_vectors.1 = f32[8,128]{1,0:T(8,128)} custom-call(f32[16,8,8,128]{3,2,1,0:T(8,128)} %copy.90), custom_call_target="tpu_custom_call" | custom-call | tf_op jit(solution)/shard_map/sum_vectors/pallas_call | solution.py:449
  603.3 2.5 add_add_fusion.2
  605.8 1.5 convert_element_type.162
  607.3 1.7 convert_element_type.157
  609.1 1.7 convert_element_type.159
  610.8 14.1 %reduce-scatter.6.cloned.1.call-done = bf16[4,256,128]{2,1,0:T(8,128)(2,1)} async-done(((bf16[4,2048,128]{2,1,0:T(8,128)(2,1)}), bf16[4,256,128]{2,1,0:T(8,128)(2,1)}) %reduce-scatter.6.cloned.1.call-update) | async-done | bytes 262160 | tf_op jit(solution)/shard_map/reduce_scatter | solution.py:794
  624.9 1.8 convert_element_type.153
  626.6 38.9 %reduce-scatter.8.cloned.1.call-done = bf16[128,256]{1,0:T(8,128)(2,1)} async-done(((bf16[128,2048]{1,0:T(8,128)(2,1)}), bf16[128,256]{1,0:T(8,128)(2,1)}) %reduce-scatter.8.cloned.1.call-update) | async-done | bytes 65552 | tf_op jit(solution)/shard_map/reduce_scatter | solution.py:794
  665.5 1.5 convert_element_type.155
  (162 shorter events, 28.0 us)
Async XLA Ops:
  7.2 119.3 %all-gather.4.cloned.1.call-start = ((), (), s32[]{:S(2)}) async-start(), calls=%async_computation.5 | async-start | bytes 8912896 | tf_op jit(solution)/shard_map/all_gather | solution.py:700
  7.9 229.5 %all-gather.6.cloned.1.call-start = ((), (), s32[]{:S(2)}) async-start(), calls=%async_computation.6 | async-start | bytes 8912896 | tf_op jit(solution)/shard_map/all_gather | solution.py:701
  8.6 561.6 %all-gather.8.cloned.1.call-start = ((), (), s32[]{:S(2)}) async-start(), calls=%async_computation.8 | async-start | bytes 8912896 | tf_op jit(solution)/shard_map/all_gather | solution.py:765
  15.2 9.7 %copy-start.1 = (f32[2048,1]{1,0:T(8,128)}, f32[2048,1]{1,0:T(8,128)S(1)}, u32[]{:S(2)}) copy-start(f32[2048,1]{1,0:T(8,128)S(1)} %copy.73.same_ref) | copy-start | bytes 24580
  15.3 8.1 %copy-start.18 = (bf16[128,2048]{1,0:T(8,128)(2,1)S(1)}, bf16[128,2048]{1,0:T(8,128)(2,1)}, u32[]{:S(2)}) copy-start(bf16[128,2048]{1,0:T(8,128)(2,1)} %param.9) | copy-start | bytes 1572868
  15.3 8.6 %copy-start.36 = (f32[14,2048]{1,0:T(8,128)S(1)}, f32[14,2048]{1,0:T(8,128)}, u32[]{:S(2)}) copy-start(f32[14,2048]{1,0:T(8,128)} %param.16) | copy-start | bytes 344068
  19.5 70.7 %copy-start.26 = (s32[2048]{0:T(1024)S(1)}, s32[2048]{0:T(1024)}, u32[]{:S(2)}) copy-start(s32[2048]{0:T(1024)} %param.17) | copy-start | bytes 24580
  24.9 1.6 copy-start.3
  90.5 2.2 copy-start
  104.5 0.8 copy-start.7
  105.2 1.0 copy-start.14
  106.3 1.0 copy-start.16
  131.4 63.0 %copy-start.5 = (bf16[448,2048]{1,0:T(8,128)(2,1)S(1)}, bf16[448,2048]{1,0:T(8,128)(2,1)}, u32[]{:S(2)}) copy-start(bf16[448,2048]{1,0:T(8,128)(2,1)} %w_ref.4) | copy-start | bytes 5505028
  194.4 1.7 copy-start.11
  237.4 6.7 copy-start.2
  244.1 78.5 %copy-start.24 = (bf16[128,2048]{1,0:T(8,128)(2,1)}, bf16[128,2048]{1,0:T(8,128)(2,1)S(1)}, u32[]{:S(2)}) copy-start(bf16[128,2048]{1,0:T(8,128)(2,1)S(1)} %get-tuple-element.55) | copy-start | bytes 1572868
  244.1 38.4 %copy-start.6 = (bf16[2048,448]{0,1:T(8,128)(2,1)S(1)}, bf16[2048,448]{0,1:T(8,128)(2,1)}, u32[]{:S(2)}) copy-start(bf16[2048,448]{0,1:T(8,128)(2,1)} %param.13) | copy-start | bytes 5505028
  282.5 46.6 %copy-start.13 = (bf16[2048,448]{1,0:T(8,128)(2,1)}, bf16[2048,448]{1,0:T(8,128)(2,1)S(1)}, u32[]{:S(2)}) copy-start(bf16[2048,448]{1,0:T(8,128)(2,1)S(1)} %get-tuple-element.26.l_ref) | copy-start | bytes 5505028
  282.5 40.1 %copy-start.22 = (bf16[128,2048]{1,0:T(8,128)(2,1)S(1)}, bf16[128,2048]{1,0:T(8,128)(2,1)}, u32[]{:S(2)}) copy-start(bf16[128,2048]{1,0:T(8,128)(2,1)} %add_convert_fusion.1.a_ref) | copy-start | bytes 1572868
  282.5 40.1 %copy-start.35 = (f32[1,2048]{1,0:T(1,128)S(1)}, f32[1,2048]{1,0:T(1,128)}, u32[]{:S(2)}) copy-start(f32[1,2048]{1,0:T(1,128)} %get-tuple-element.67.nu_ref) | copy-start | bytes 24580
  329.1 3.1 collective-permute-start
  332.2 1.0 copy-start.25
  333.2 30.3 %copy-start.20 = (f32[128,2048]{1,0:T(8,128)}, f32[128,2048]{1,0:T(8,128)S(1)}, u32[]{:S(2)}) copy-start(f32[128,2048]{1,0:T(8,128)S(1)} %get-tuple-element.44) | copy-start | bytes 3145732
  334.3 271.5 %reduce-scatter.14.cloned.1.call-start = ((), (), s32[]{:S(2)}) async-start(), calls=%async_computation.12 | async-start | bytes 589824 | tf_op jit(solution)/shard_map/reduce_scatter | solution.py:794
  364.9 242.4 %reduce-scatter.10.cloned.1.call-start = ((), (), s32[]{:S(2)}) async-start(), calls=%async_computation.10 | async-start | bytes 2064384 | tf_op jit(solution)/shard_map/reduce_scatter | solution.py:794
  364.9 9.5 %copy-start.12 = (bf16[2048,448]{1,0:T(8,128)(2,1)S(1)}, bf16[2048,448]{1,0:T(8,128)(2,1)}, u32[]{:S(2)}) copy-start(bf16[2048,448]{1,0:T(8,128)(2,1)} %get-tuple-element.24.l_ref) | copy-start | bytes 5505028
  374.4 234.7 %reduce-scatter.12.cloned.1.call-start = ((), (), s32[]{:S(2)}) async-start(), calls=%async_computation.11 | async-start | bytes 2064384 | tf_op jit(solution)/shard_map/reduce_scatter | solution.py:794
  383.4 31.1 %copy-start.15 = (f32[2048,128]{1,0:T(8,128)S(1)}, f32[2048,128]{1,0:T(8,128)}, u32[]{:S(2)}) copy-start(f32[2048,128]{1,0:T(8,128)} %copy-done.14) | copy-start | bytes 3145732
  383.4 31.1 %copy-start.17 = (f32[16,128,128]{2,1,0:T(8,128)S(1)}, f32[16,128,128]{2,1,0:T(8,128)}, u32[]{:S(2)}) copy-start(f32[16,128,128]{2,1,0:T(8,128)} %copy-done.16) | copy-start | bytes 3145732
  383.4 241.4 %reduce-scatter.6.cloned.1.call-start = ((), (), s32[]{:S(2)}) async-start(), calls=%async_computation.7 | async-start | bytes 2359296 | tf_op jit(solution)/shard_map/reduce_scatter | solution.py:794
  414.5 1.0 copy-start.10
  461.3 5.5 copy-start.4
  475.0 9.2 %copy-start.23 = (bf16[4,2048,128]{2,1,0:T(8,128)(2,1)S(1)}, bf16[4,2048,128]{2,1,0:T(8,128)(2,1)}, u32[]{:S(2)}) copy-start(bf16[4,2048,128]{2,1,0:T(8,128)(2,1)} %get-tuple-element.52) | copy-start | bytes 6291460
  475.1 190.5 %reduce-scatter.8.cloned.1.call-start = ((), (), s32[]{:S(2)}) async-start(), calls=%async_computation.9 | async-start | bytes 589824 | tf_op jit(solution)/shard_map/reduce_scatter | solution.py:794
  494.9 2.2 copy-start.9
  497.1 66.2 %copy-start.19 = (bf16[128,2048]{1,0:T(8,128)(2,1)S(1)}, bf16[128,2048]{1,0:T(8,128)(2,1)}, u32[]{:S(2)}) copy-start(bf16[128,2048]{1,0:T(8,128)(2,1)} %param.9) | copy-start | bytes 1572868
  497.1 69.4 %copy-start.34 = (f32[1,8,16,16]{3,2,1,0:T(8,128)S(1)}, f32[1,8,16,16]{3,2,1,0:T(8,128)}, u32[]{:S(2)}) copy-start(f32[1,8,16,16]{3,2,1,0:T(8,128)} %stack.46) | copy-start | bytes 24580
  563.3 3.8 copy-start.31
  563.3 4.4 copy-start.33
  563.3 5.0 copy-start.32
  563.3 5.6 copy-start.29
  563.4 6.2 copy-start.30
  563.4 6.9 %copy-start.8 = (bf16[2048,128]{1,0:T(8,128)(2,1)S(1)}, bf16[2048,128]{1,0:T(8,128)(2,1)}, u32[]{:S(2)}) copy-start(bf16[2048,128]{1,0:T(8,128)(2,1)} %copy-done.7) | copy-start | bytes 1572868
  570.2 5.5 copy-start.28
  570.2 6.2 copy-start.27
  575.7 27.5 %copy-start.21 = (f32[128,2048]{1,0:T(8,128)S(1)}, f32[128,2048]{1,0:T(8,128)}, u32[]{:S(2)}) copy-start(f32[128,2048]{1,0:T(8,128)} %copy-done.20) | copy-start | bytes 3145732
Sparse Core Ops, SparseCore 0:
  10.4 88.8 all-gather.3
  101.6 99.6 all-gather.5
  334.5 83.2 all-gather.7
  420.0 35.3 reduce-scatter.13
  457.8 45.9 reduce-scatter.9
  506.3 60.4 reduce-scatter.11
  569.3 55.4 reduce-scatter.5
  627.3 38.1 reduce-scatter.7

commit v3 on v2

--- a/solution.py
+++ b/solution.py
@@ -121,12 +121,15 @@
     yield [other(dx=2, dz=1)]
 
 
-def run_gather(a_ref, land, ss, rs, work):
+def run_gather(a_ref, land, ss, rs, work, met=False, between=None):
     p = Place()
     t = Traffic(p, ss, rs)
-    greet(p, [p.at(dc=1), p.at(dx=1), p.at(dx=-1), p.at(dz=1)])
+    if not met:
+        greet(p, [p.at(dc=1), p.at(dx=1), p.at(dx=-1), p.at(dz=1)])
     steps = gather_steps(p, t, a_ref, land)
     next(steps)
+    if between is not None:
+        between()
     land[p.s] = a_ref[...]
     ready = [p.s]
     for arrived in steps:
@@ -263,43 +266,16 @@
     )(a, w, nu, same)
 
 
-def back_kernel(a_ref, w_ref, lift_ref, all_ref, o_ref, land, ss, rs, ls):
-    R = a_ref.shape[0]
-    start, wait = save_blocks(land, all_ref, ls)
-
-    def work(b):
-        start(b)
-        rows = pl.ds(pl.multiple_of(b * R, 16), R)
-        gs = jnp.dot(land[b], w_ref[...], preferred_element_type=F32)
-        o_ref[rows, :] = (gs * 2.0 * lift_ref[rows, :]).astype(BF)
-
-    t = run_gather(a_ref, land, ss, rs, work)
-    wait()
-    t.finish()
-
-
-def value_back(a, w, lift, cid):
-    R, C = a.shape
-    units = w.shape[1]
-    return pl.pallas_call(
-        back_kernel,
-        out_shape=(jax.ShapeDtypeStruct((16 * R, C), BF), jax.ShapeDtypeStruct((16 * R, units), BF)),
-        in_specs=[pl.BlockSpec(memory_space=VMEM)] * 3,
-        out_specs=(pl.BlockSpec(memory_space=pl.ANY), pl.BlockSpec(memory_space=VMEM)),
-        scratch_shapes=[VMEM((16, R, C), BF), DMA((18,)), DMA((18,)), DMA((16,))],
-        compiler_params=pltpu.CompilerParams(collective_id=cid, has_side_effects=True, vmem_limit_bytes=48 * 2**20),
-        name="gather_value_back",
-    )(a, w, lift)
-
-
-def sum_kernel(l_ref, w_ref, o_ref, pa, cb, zt, xs, zf, hv, xf, ss, rs):
+def sum_steps(l_ref, w_ref, o_ref, pa, cb, zt, xs, zf, hv, xf, ss, rs, jobs=(), met=False):
+    jobs = list(jobs) + [lambda: None] * (7 - len(jobs))
     p = Place()
     t = Traffic(p, ss, rs)
     R = o_ref.shape[0]
     H = R // 2
     core, xp, xm, zz = p.at(dc=1), p.at(dx=1), p.at(dx=-1), p.at(dz=1)
     order = [(2, 1), (-1, 1), (1, 1), (2, 0), (0, 1), (1, 0), (-1, 0), (0, 0)]
-    greet(p, [core, xp, xm, zz])
+    if not met:
+        greet(p, [core, xp, xm, zz])
 
     def term(i, dc):
         b = p.at(order[i][0], order[i][1], dc)
@@ -337,28 +313,46 @@
     pair(6)
     t.send(12, pa.at[6, 1, upper], xf.at[1, upper], xm)
     pair(7)
+    jobs[0]()
+    jobs[1]()
     t.landed(8, zt)
     pa[3, 1] = (pa[3, 1].astype(F32) + zt[...].astype(F32)).astype(BF)
     t.send(13, pa.at[3, 1, upper], hv.at[0], xp)
     t.send(14, pa.at[3, 1, lower], hv.at[1], xm)
+    jobs[2]()
     t.landed(9, xs.at[1])
     t.landed(10, xs.at[0])
     pa[4, 1] = (pa[4, 1].astype(F32) + xs[0].astype(F32) + xs[1].astype(F32)).astype(BF)
     t.send(15, pa.at[4, 1], zf, zz)
+    jobs[3]()
     t.landed(13, hv.at[0])
     pa[5, 1, upper] = (pa[5, 1, upper].astype(F32) + hv[0].astype(F32)).astype(BF)
     t.send(16, pa.at[5, 1, upper], xf.at[0, upper], xp)
     t.landed(14, hv.at[1])
     pa[6, 1, lower] = (pa[6, 1, lower].astype(F32) + hv[1].astype(F32)).astype(BF)
     t.send(17, pa.at[6, 1, lower], xf.at[1, lower], xm)
+    jobs[4]()
+    jobs[5]()
     t.landed(11, xf.at[0, lower])
     t.landed(12, xf.at[1, upper])
     t.landed(15, zf)
     o_ref[...] = pa[7, 1].astype(F32) + zf[...].astype(F32)
+    jobs[6]()
     t.landed(16, xf.at[0, upper])
     t.landed(17, xf.at[1, lower])
     o_ref[...] = o_ref[...] + xf[0].astype(F32) + xf[1].astype(F32)
     t.finish()
+
+
+def sum_kernel(*refs):
+    sum_steps(*refs)
+
+
+def sum_scratch(R, C):
+    return [
+        VMEM((8, 2, R, C), BF), VMEM((8, R, C), BF), VMEM((R, C), BF), VMEM((2, R, C), BF), VMEM((R, C), BF),
+        VMEM((2, R // 2, C), BF), VMEM((2, R, C), BF),
+    ]
 
 
 def matmul_sum(l, w, cid):
@@ -368,10 +362,7 @@
         out_shape=jax.ShapeDtypeStruct((R, C), F32),
         in_specs=[pl.BlockSpec(memory_space=VMEM)] * 2,
         out_specs=pl.BlockSpec(memory_space=VMEM),
-        scratch_shapes=[
-            VMEM((8, 2, R, C), BF), VMEM((8, R, C), BF), VMEM((R, C), BF), VMEM((2, R, C), BF), VMEM((R, C), BF),
-            VMEM((2, R // 2, C), BF), VMEM((2, R, C), BF), DMA((18,)), DMA((18,)),
-        ],
+        scratch_shapes=sum_scratch(R, C) + [DMA((18,)), DMA((18,))],
         compiler_params=pltpu.CompilerParams(collective_id=cid, has_side_effects=True, vmem_limit_bytes=48 * 2**20),
         name="matmul_sum",
     )(l, w)
@@ -404,56 +395,6 @@
         scratch_shapes=[DMA((n,)), DMA((n,)), DMA((1,))],
         compiler_params=pltpu.CompilerParams(collective_id=cid, has_side_effects=True),
         name="swap_blocks",
-    )(a)
-
-
-def vec_kernel(nd, a_ref, o_ref, b1, t1, b2, ss, rs, ss2, rs2):
-    p = Place()
-    n = 16
-    d = p.dp
-    barrier = pltpu.get_barrier_semaphore()
-    for k in range(1, n):
-        pl.semaphore_signal(barrier, inc=1, device_id=(d, (p.s + k) % n), device_id_type=MESH)
-    for k in range(1, nd):
-        pl.semaphore_signal(barrier, inc=1, device_id=((d + k) % nd, p.s), device_id_type=MESH)
-    pl.semaphore_wait(barrier, n + nd - 2)
-    cps = []
-    for k in range(1, n):
-        to = (p.s + k) % n
-        cp = pltpu.make_async_remote_copy(src_ref=a_ref.at[to], dst_ref=b1.at[k - 1], send_sem=ss.at[k], recv_sem=rs.at[k], device_id=(d, to), device_id_type=MESH)
-        cp.start()
-        cps.append(cp)
-    total = a_ref[p.s]
-    for k in range(1, n):
-        cps[k - 1].wait_recv()
-        total = total + b1[k - 1]
-    t1[...] = total
-    cps2 = []
-    for k in range(1, nd):
-        to = (d + k) % nd
-        cp = pltpu.make_async_remote_copy(src_ref=t1.at[to], dst_ref=b2.at[k - 1], send_sem=ss2.at[k], recv_sem=rs2.at[k], device_id=(to, p.s), device_id_type=MESH)
-        cp.start()
-        cps2.append(cp)
-    acc = t1[d]
-    for k in range(1, nd):
-        cps2[k - 1].wait_recv()
-        acc = acc + b2[k - 1]
-    o_ref[...] = acc
-    for cp in cps + cps2:
-        cp.wait_send()
-
-
-def vec_sum(a, cid):
-    n, nd = a.shape[:2]
-    piece = a.shape[2:]
-    return pl.pallas_call(
-        functools.partial(vec_kernel, nd),
-        out_shape=jax.ShapeDtypeStruct(piece, a.dtype),
-        in_specs=[pl.BlockSpec(memory_space=VMEM)],
-        out_specs=pl.BlockSpec(memory_space=VMEM),
-        scratch_shapes=[VMEM((n - 1, nd) + piece, a.dtype), VMEM((nd,) + piece, a.dtype), VMEM((max(nd - 1, 1),) + piece, a.dtype), DMA((n,)), DMA((n,)), DMA((nd,)), DMA((nd,))],
-        compiler_params=pltpu.CompilerParams(collective_id=cid, has_side_effects=True),
-        name="sum_vectors",
     )(a)
 
 
@@ -574,7 +515,7 @@
     )(x, cols, rows, keep, vec)
 
 
-def backward_kernel(x_ref, o_ref, s_ref, gz_ref, col_ref, row_ref, keep_ref, vec_ref, g_ref, sums_ref, tab, grad_state, acc, carry):
+def back_chunk(x_ref, o_ref, s_ref, gz_ref, col_ref, row_ref, keep_ref, vec_ref, g_ref, sums_ref, tab, grad_state, acc, carry, turned):
     chunks, L = row_ref.shape[0], row_ref.shape[2]
     W = vec_ref.shape[1]
     heads = W // ATTENTION_WIDTH
@@ -593,14 +534,14 @@
     def add(q, term):
         sums_ref[q : q + 1, :] += jnp.sum(term, axis=0, keepdims=True)
 
-    def step(n, unused):
+    def step(n):
         i = chunks - 1 - n
         rows = pl.ds(pl.multiple_of(i * L, L), L)
         r, k, v, p = (x_ref[rows, q * W : (q + 1) * W] for q in range(4))
         col = col_ref[rows, :]
         seg, kept, tail, same_next = col[:, 0:1], col[:, 1:2], col[:, 2:3], col[:, 3:4]
         o = o_ref[rows, :]
-        gz = gz_ref[rows, :].astype(F32)
+        gz = gz_ref[i].astype(F32)
         center = o - head_sums(o, ones) * (1.0 / ATTENTION_WIDTH)
         spread = head_sums(center * center, ones) * (1.0 / ATTENTION_WIDTH)
         scale = lax.rsqrt(spread + 0.00064)
@@ -648,25 +589,499 @@
         carry[0:1, :] = grads[0:1, :]
         g_ref[rows, : 4 * W] = grads.astype(BF)
         g_ref[rows, 4 * W :] = after.astype(BF)
+        turned[0 : 4 * W, rows] = grads.T.astype(BF)
+        turned[4 * W :, rows] = after.T.astype(BF)
+
+    return step
+
+
+def back_finish(vec_ref, sums_ref, acc, L):
+    W = vec_ref.shape[1]
+    whole = dot3(halves(jnp.ones((8, W), F32)), halves(acc[...] * vec_ref[8 : 8 + W, :]), NT)
+    sums_ref[0:1, :] = (sums_ref[0:1, :] + L * whole[0:1, :]) * vec_ref[0:1, :]
+
+
+class Copies:
+    def __init__(self, ss, rs):
+        self.ss, self.rs, self.items = ss, rs, {}
+
+    def add(self, k, src, dst, to):
+        self.items[k] = (src, dst, to)
+
+    def make(self, k, src, dst, to):
+        return pltpu.make_async_remote_copy(
+            src_ref=src, dst_ref=dst, send_sem=self.ss.at[k], recv_sem=self.rs.at[k], device_id=to, device_id_type=MESH
+        )
+
+    def start(self, *ks):
+        for k in ks:
+            self.make(k, *self.items[k]).start()
+
+    def landed(self, k, ref):
+        self.make(k, ref, ref, self.items[k][2]).wait_recv()
+
+    def finish(self):
+        for k in self.items:
+            self.make(k, *self.items[k]).wait_send()
+
+
+def meet(devices):
+    barrier = pltpu.get_barrier_semaphore()
+    for device in devices:
+        pl.semaphore_signal(barrier, inc=1, device_id=device, device_id_type=MESH)
+    pl.semaphore_wait(barrier, len(devices))
+
+
+def ring_mates(p):
+    return [p.dev((p.s + k) % 16) for k in range(1, 16)]
+
+
+def dp_mates(p, nd):
+    return [((p.dp + k) % nd, p.s) for k in range(1, nd)]
+
+
+def swap_copies(p, c, base, src, dst):
+    for k in range(1, 16):
+        to = (p.s + k) % 16
+        c.add(base + k - 1, src.at[to], dst.at[p.s], p.dev(to))
+    keys = range(base, base + 15)
+
+    def start():
+        c.start(*keys)
+
+    def wait():
+        for k in range(1, 16):
+            c.landed(base + k - 1, dst.at[(p.s + 16 - k) % 16])
+
+    return start, wait
+
+
+def gather_plan(p, c, base, a_ref, land):
+    H = a_ref.shape[0] // 2
+    up, lo = pl.ds(0, H), pl.ds(H, H)
+    core, xp, xm, zz = p.at(dc=1), p.at(dx=1), p.at(dx=-1), p.at(dz=1)
+    d2, zxm, zxp, zd2 = p.at(dx=2), p.at(dx=-1, dz=1), p.at(dx=1, dz=1), p.at(dx=2, dz=1)
+    L = land.at
+
+    def add(k, src, dst, to):
+        c.add(base + k, src, dst, p.dev(to))
+
+    def relay(k, ref, to):
+        add(k, ref, ref, to)
+
+    for k, to in enumerate((xp, xm, zz, core)):
+        add(k, a_ref, L[p.s], to)
+    relay(4, L[xm, up], xp)
+    relay(5, L[xp, lo], xm)
+    relay(6, L[xm], core)
+    relay(7, L[xp], core)
+    relay(8, L[zz], xp)
+    relay(9, L[zz], xm)
+    relay(10, L[zz], core)
+    relay(11, L[d2, up], zz)
+    relay(12, L[d2, lo], zz)
+    relay(13, L[d2], core)
+    relay(14, L[zxm], core)
+    relay(15, L[zxp], core)
+    relay(16, L[zd2, up], core)
+    relay(17, L[zd2, lo], core)
+
+    def start(*ks):
+        c.start(*(base + k for k in ks))
+
+    def landed(k, ref):
+        c.landed(base + k, ref)
+
+    def one():
+        start(0, 1, 2, 3)
+
+    def two():
+        landed(0, L[xm])
+        start(4)
+        landed(1, L[xp])
+        start(5, 6, 7)
+        landed(2, L[zz])
+        start(8, 9, 10)
+
+    def three():
+        landed(4, L[d2, up])
+        start(11)
+        landed(5, L[d2, lo])
+        start(12, 13)
+
+    def four():
+        landed(8, L[zxm])
+        start(14)
+        landed(9, L[zxp])
+        start(15)
+
+    def five():
+        landed(11, L[zd2, up])
+        start(16)
+        landed(12, L[zd2, lo])
+        start(17)
+
+    def other(**k):
+        return p.at(dc=1, **k)
+
+    def six():
+        landed(3, L[core])
+        landed(6, L[other(dx=-1)])
+        landed(7, L[other(dx=1)])
+        landed(10, L[other(dz=1)])
+        landed(13, L[other(dx=2)])
+        landed(14, L[other(dx=-1, dz=1)])
+        landed(15, L[other(dx=1, dz=1)])
+        landed(16, L[other(dx=2, dz=1), up])
+        landed(17, L[other(dx=2, dz=1), lo])
+
+    return [one, two, three, four, five, six]
+
+
+def dp_scratch(J, C):
+    return [VMEM((2, 2, J // 2, C), BF), VMEM((2, 2, J // 2, C), BF), VMEM((2, 2, J, C), BF), VMEM((2, J, C), BF)]
+
+
+def dp_plan(p, nd, c, base, g_ref, o_ref, scratch):
+    hv, stage, xf, zb = scratch
+    J = g_ref.shape[1]
+    H = J // 2
+    up, lo = pl.ds(0, H), pl.ds(H, H)
+    ny = nd // 2
+    y, zl = p.dp // 2, p.dp % 2
+    yp, ym, yo = (y + 1) % ny, (y + ny - 1) % ny, (y + 2) % ny
+
+    def pay(at, rows):
+        return g_ref.at[pl.ds(2 * at, 2), rows]
+
+    to_p, to_m, to_z = (2 * yp + zl, p.s), (2 * ym + zl, p.s), (2 * y + 1 - zl, p.s)
+    c.add(base, pay(yo, up), hv.at[0], to_p)
+    c.add(base + 1, pay(yo, lo), hv.at[1], to_m)
+    c.add(base + 2, pay(yp, lo), xf.at[0, :, lo], to_p)
+    c.add(base + 3, pay(ym, up), xf.at[1, :, up], to_m)
+    c.add(base + 4, stage.at[0], xf.at[0, :, up], to_p)
+    c.add(base + 5, stage.at[1], xf.at[1, :, lo], to_m)
+    c.add(base + 6, zb.at[0], zb.at[1], to_z)
+
+    def one():
+        c.start(base, base + 1, base + 2, base + 3)
+
+    def two():
+        c.landed(base, hv.at[0])
+        stage[0] = (g_ref[pl.ds(2 * yp, 2), up].astype(F32) + hv[0].astype(F32)).astype(BF)
+        c.start(base + 4)
+        c.landed(base + 1, hv.at[1])
+        stage[1] = (g_ref[pl.ds(2 * ym, 2), lo].astype(F32) + hv[1].astype(F32)).astype(BF)
+        c.start(base + 5)
+
+    def total(which):
+        return g_ref[2 * y + which].astype(F32) + xf[0, which].astype(F32) + xf[1, which].astype(F32)
+
+    def three():
+        c.landed(base + 2, xf.at[0, :, lo])
+        c.landed(base + 3, xf.at[1, :, up])
+        c.landed(base + 4, xf.at[0, :, up])
+        c.landed(base + 5, xf.at[1, :, lo])
+        zb[0] = total(1 - zl).astype(BF)
+        c.start(base + 6)
+        o_ref[0] = total(zl)
+
+    def four():
+        c.landed(base + 6, zb.at[1])
+        o_ref[0] += zb[1].astype(F32)
+
+    return [one, two, three, four]
+
+
+def value_back_kernel(a_ref, w_ref, lift_ref, gf_ref, all_ref, o_ref, rc_ref, land, ss, rs, ls, cs, cr):
+    R = a_ref.shape[0]
+    start, wait = save_blocks(land, all_ref, ls)
+    p = Place()
+    c = Copies(cs, cr)
+    begin, end = swap_copies(p, c, 0, gf_ref, rc_ref)
+
+    def work(b):
+        start(b)
+        rows = pl.ds(pl.multiple_of(b * R, 16), R)
+        gs = jnp.dot(land[b], w_ref[...], preferred_element_type=F32)
+        o_ref[rows, :] = (gs * 2.0 * lift_ref[rows, :]).astype(BF)
+
+    meet(ring_mates(p))
+    t = run_gather(a_ref, land, ss, rs, work, met=True, between=begin)
+    rc_ref[p.s] = gf_ref[p.s]
+    end()
+    wait()
+    t.finish()
+    c.finish()
+
+
+def value_back(a, w, lift, gf, cid):
+    R, C = a.shape
+    units = w.shape[1]
+    return pl.pallas_call(
+        value_back_kernel,
+        out_shape=(
+            jax.ShapeDtypeStruct((16 * R, C), BF),
+            jax.ShapeDtypeStruct((16 * R, units), BF),
+            jax.ShapeDtypeStruct(gf.shape, BF),
+        ),
+        in_specs=[pl.BlockSpec(memory_space=VMEM)] * 4,
+        out_specs=(pl.BlockSpec(memory_space=pl.ANY), pl.BlockSpec(memory_space=VMEM), pl.BlockSpec(memory_space=VMEM)),
+        scratch_shapes=[VMEM((16, R, C), BF), DMA((18,)), DMA((18,)), DMA((16,)), DMA((15,)), DMA((15,))],
+        compiler_params=pltpu.CompilerParams(collective_id=cid, has_side_effects=True, vmem_limit_bytes=48 * 2**20),
+        name="gather_value_back",
+    )(a, w, lift, gf)
+
+
+def column_tiles(refs, tile, sem):
+    C = tile.shape[2]
+
+    def copy(u, ref):
+        return pltpu.make_async_copy(ref.at[:, pl.ds(pl.multiple_of((u % 8) * C, C), C)], tile.at[u % 2], sem.at[u % 2])
+
+    def start(u, kind):
+        copy(u, refs[kind]).start()
+
+    def wait(u, kind):
+        copy(u, refs[kind]).wait()
+
+    return start, wait
+
+
+def key_back_kernel(l_ref, w_ref, s_ref, rt_ref, nu_ref, gkv_hbm, in_hbm, n2_hbm, o_ref, gg_ref,
+                    pa, cb, zt, xs, zf, hv, xf, lt, tile, ss, rs, ts):
+    T, U = l_ref.shape
+    K = rt_ref.shape[1] // 2
+    C = tile.shape[2]
+    refs = (gkv_hbm, in_hbm, n2_hbm)
+    fetch, have = column_tiles(refs, tile, ts)
+    fetch(0, 0)
+
+    def turn():
+        for r in range(0, T, 256):
+            rows = slice(r, r + 256)
+            lt[0:U, rows] = s_ref[rows, :].T
+            lt[U : 2 * U, rows] = l_ref[rows, :].T
+            lt[2 * U :, rows] = rt_ref[rows, :].T
+
+    def grads(kind, lo, hi):
+        def unit(d, unused):
+            u = 8 * kind + d
+            if hi < 8:
+                fetch(u + 1, kind)
+            elif kind < 2:
+                @pl.when(d < 7)
+                def _():
+                    fetch(u + 1, kind)
+
+                @pl.when(d == 7)
+                def _():
+                    fetch(u + 1, kind + 1)
+            else:
+                @pl.when(d < 7)
+                def _():
+                    fetch(u + 1, kind)
+            have(u, kind)
+            rhs = tile[d % 2]
+            if kind < 2:
+                out = jnp.dot(lt[kind * U : (kind + 1) * U, :], rhs, preferred_element_type=F32)
+                gg_ref[d, kind * U : (kind + 1) * U, :] = out.astype(BF)
+            else:
+                out = jnp.dot(lt[2 * U :, :], rhs, preferred_element_type=F32)
+                nu = nu_ref[:, pl.ds(pl.multiple_of(d * C, C), C)]
+                gg_ref[d, 2 * U :, :] = (out[:K] + nu * (out[K:] - out[:K])).astype(BF)
+            return 0
+
+        lax.fori_loop(lo, hi, unit, 0)
+
+    jobs = [turn] + [functools.partial(grads, kind, lo, lo + 4) for kind in range(3) for lo in (0, 4)]
+    sum_steps(l_ref, w_ref, o_ref, pa, cb, zt, xs, zf, hv, xf, ss, rs, jobs)
+
+
+def key_back(l, w, s, rt, nu, gkv_all, key_in, n2_all, cid):
+    R, C = l.shape[0] // 16, w.shape[1]
+    U, K = l.shape[1], rt.shape[1] // 2
+    return pl.pallas_call(
+        key_back_kernel,
+        out_shape=(jax.ShapeDtypeStruct((R, C), F32), jax.ShapeDtypeStruct((8, 2 * U + K, C // 8), BF)),
+        in_specs=[pl.BlockSpec(memory_space=VMEM)] * 5 + [pl.BlockSpec(memory_space=pl.ANY)] * 3,
+        out_specs=(pl.BlockSpec(memory_space=VMEM),) * 2,
+        scratch_shapes=sum_scratch(R, C)
+        + [VMEM((2 * U + 2 * K, 16 * R), BF), VMEM((2, 16 * R, C // 8), BF), DMA((18,)), DMA((18,)), DMA((2,))],
+        compiler_params=pltpu.CompilerParams(collective_id=cid, has_side_effects=True, vmem_limit_bytes=56 * 2**20),
+        name="key_back",
+    )(l, w, s, rt, nu, gkv_all, key_in, n2_all)
+
+
+def time_back_kernel(nd, x_ref, o_ref, s_ref, gz_ref, col_ref, row_ref, keep_ref, vec_ref, gh_ref, z_ref, mixt_ref, mu_ref, early_ref,
+                     n1_hbm, g_ref, sums_ref, gg_ref, mug_ref, dp_ref,
+                     tab, grad_state, acc, carry, gz, land, turned, tile, d0, d1, d2, d3, cs, cr, ts):
+    p = Place()
+    c = Copies(cs, cr)
+    W = vec_ref.shape[1]
+    chunks, L = row_ref.shape[0], row_ref.shape[2]
+    C = tile.shape[2]
+    begin, end = swap_copies(p, c, 0, gz_ref, gz)
+    gather = gather_plan(p, c, 15, gh_ref, land)
+    fetch, have = column_tiles((n1_hbm,), tile, ts)
+    mates = ring_mates(p)
+    if nd > 1:
+        sums = dp_plan(p, nd, c, 33, early_ref, dp_ref, (d0, d1, d2, d3))
+        mates = mates + dp_mates(p, nd)
+    else:
+        sums = [lambda: None] * 3 + [lambda: dp_ref.__setitem__(Ellipsis, early_ref[...].astype(F32))]
+    meet(mates)
+    begin()
+    gather[0]()
+    sums[0]()
+    fetch(0, 0)
+    land[p.s] = gh_ref[...]
+    gz[p.s] = gz_ref[p.s]
+    when = {4: [gather[1]], 8: [gather[2]], 10: [sums[1]], 12: [gather[3]]}
+    chunk = back_chunk(x_ref, o_ref, s_ref, gz, col_ref, row_ref, keep_ref, vec_ref, g_ref, sums_ref, tab, grad_state, acc, carry, turned)
+    end()
+
+    def step(n, unused):
+        chunk(n)
+        for at, parts in when.items():
+            @pl.when(n == at)
+            def _():
+                for part in parts:
+                    part()
         return 0
 
     lax.fori_loop(0, chunks, step, 0)
-    whole = dot3(halves(jnp.ones((8, W), F32)), halves(acc[...] * decay), NT)
-    sums_ref[0:1, :] = (sums_ref[0:1, :] + L * whole[0:1, :]) * lam
-
-
-def recurrence_back(x, o, states, gz, cols, rows, keep, vec):
+    gather[4]()
+    sums[2]()
+    back_finish(vec_ref, sums_ref, acc, L)
+    mug_ref[...] = jnp.zeros_like(mug_ref)
+
+    def mix(d, unused):
+        @pl.when(d < 7)
+        def _():
+            fetch(d + 1, 0)
+
+        have(d, 0)
+        rhs = tile[d % 2]
+        cols = pl.ds(pl.multiple_of(d * C, C), C)
+        for q in range(4):
+            a = jnp.dot(turned[q * W : (q + 1) * W, :], rhs, preferred_element_type=F32)
+            b = jnp.dot(turned[(4 + q) * W : (5 + q) * W, :], rhs, preferred_element_type=F32)
+            diff = b - a
+            gg_ref[d, q * W : (q + 1) * W, :] = (a + mu_ref[q : q + 1, cols] * diff).astype(BF)
+            mug_ref[q : q + 1, cols] = jnp.sum(mixt_ref[q * W : (q + 1) * W, cols].astype(F32) * diff, axis=0, keepdims=True)
+        return 0
+
+    lax.fori_loop(0, 8, mix, 0)
+    gather[5]()
+    sums[3]()
+    T = x_ref.shape[0]
+    for r in range(0, T, 256):
+        turned[0:W, r : r + 256] = z_ref[r : r + 256, :].T
+
+    def out(d, unused):
+        cols = pl.ds(pl.multiple_of(d * C, C), C)
+        rhs = jnp.concatenate([land[b, :, cols] for b in range(16)], axis=0)
+        gg_ref[d, 4 * W :, :] = jnp.dot(turned[0:W, :], rhs, preferred_element_type=F32).astype(BF)
+        return 0
+
+    lax.fori_loop(0, 8, out, 0)
+    c.finish()
+
+
+def time_back(nd, x, o, states, gz, cols, rows, keep, vec, gh, z, mixt, mu, early, n1_all, cid):
     T, W = x.shape[0], vec.shape[1]
-    chunks, L = rows.shape[0], rows.shape[2]
+    L = rows.shape[2]
+    R, C = gh.shape
+    J = early.shape[1]
+    vm, hbm = pl.BlockSpec(memory_space=VMEM), pl.BlockSpec(memory_space=pl.ANY)
     return pl.pallas_call(
-        backward_kernel,
-        out_shape=(jax.ShapeDtypeStruct((T, 8 * W), BF), jax.ShapeDtypeStruct((8, W), F32)),
-        in_specs=[pl.BlockSpec(memory_space=VMEM)] * 6 + [pl.BlockSpec(memory_space=pltpu.SMEM), pl.BlockSpec(memory_space=VMEM)],
-        out_specs=(pl.BlockSpec(memory_space=VMEM),) * 2,
-        scratch_shapes=[VMEM((4, L, W), F32), VMEM((W, W), F32), VMEM((W, W), F32), VMEM((8, 4 * W), F32)],
-        compiler_params=pltpu.CompilerParams(vmem_limit_bytes=48 * 2**20),
-        name="recurrence_back",
-    )(x, o, states, gz, cols, rows, keep, vec)
+        functools.partial(time_back_kernel, nd),
+        out_shape=(
+            jax.ShapeDtypeStruct((T, 8 * W), BF),
+            jax.ShapeDtypeStruct((8, W), F32),
+            jax.ShapeDtypeStruct((8, 5 * W, C // 8), BF),
+            jax.ShapeDtypeStruct((4, C), F32),
+            jax.ShapeDtypeStruct((8 // nd, J, C // 8), F32),
+        ),
+        in_specs=[vm] * 6 + [pl.BlockSpec(memory_space=pltpu.SMEM)] + [vm] * 6 + [hbm],
+        out_specs=(vm,) * 5,
+        scratch_shapes=[
+            VMEM((4, L, W), F32), VMEM((W, W), F32), VMEM((W, W), F32), VMEM((8, 4 * W), F32),
+            VMEM((16, R, W), BF), VMEM((16, R, C), BF), VMEM((8 * W, T), BF), VMEM((2, T, C // 8), BF),
+        ]
+        + dp_scratch(J, C // 8)
+        + [DMA((40,)), DMA((40,)), DMA((2,))],
+        compiler_params=pltpu.CompilerParams(collective_id=cid, has_side_effects=True, vmem_limit_bytes=60 * 2**20),
+        name="time_back",
+    )(x, o, states, gz, cols, rows, keep, vec, gh, z, mixt, mu, early, n1_all)
+
+
+def last_kernel(nd, l_ref, w_ref, gg_ref, x_ref, gh_ref, gain_ref, terms_ref, ig_ref, dp_ref, v_ref,
+                pa, cb, zt, xs, zf, hv, xf, o_ref, d0, d1, d2, d3, tv, b1, t1, b2, ss, rs, cs, cr):
+    p = Place()
+    c = Copies(cs, cr)
+    mates = ring_mates(p)
+    if nd > 1:
+        sums = dp_plan(p, nd, c, 0, gg_ref, dp_ref, (d0, d1, d2, d3))
+        mates = mates + dp_mates(p, nd)
+    else:
+        sums = [lambda: None] * 3 + [lambda: dp_ref.__setitem__(Ellipsis, gg_ref[...].astype(F32))]
+    meet(mates)
+    sums[0]()
+    nothing = lambda: None
+    sum_steps(l_ref, w_ref, o_ref, pa, cb, zt, xs, zf, hv, xf, ss, rs, [nothing, sums[1], nothing, sums[2], nothing, nothing, sums[3]], met=True)
+    x = x_ref[...].astype(F32)
+    gn = o_ref[...]
+    width = x.shape[1]
+    center = x - jnp.sum(x, axis=1, keepdims=True) * (1.0 / width)
+    scale = lax.rsqrt(jnp.sum(center * center, axis=1, keepdims=True) * (1.0 / width) + 1e-05)
+    normed = center * scale
+    tv[...] = terms_ref[...]
+    tv[0:1, :] = jnp.sum(gn * normed, axis=0, keepdims=True)
+    tv[1:2, :] = jnp.sum(gn, axis=0, keepdims=True)
+    C = width // nd
+    for k in range(1, nd):
+        to = (p.dp + k) % nd
+        c.add(6 + k, tv.at[:, pl.ds(pl.multiple_of(to * C, 128), C)], b1.at[k - 1], (to, p.s))
+        c.start(6 + k)
+    gx = gn * gain_ref[...]
+    inner = gx - jnp.sum(gx, axis=1, keepdims=True) * (1.0 / width)
+    inner = inner - normed * (jnp.sum(gx * normed, axis=1, keepdims=True) * (1.0 / width))
+    ig_ref[...] = gh_ref[...] + scale * inner
+    total = tv[:, pl.ds(pl.multiple_of(p.dp * C, 128), C)]
+    for k in range(1, nd):
+        c.landed(6 + k, b1.at[k - 1])
+        total = total + b1[k - 1]
+    t1[...] = total
+    for k in range(1, 16):
+        c.add(14 + k, t1, b2.at[k - 1], p.dev((p.s + k) % 16))
+        c.start(14 + k)
+    for k in range(1, 16):
+        c.landed(14 + k, b2.at[k - 1])
+        total = total + b2[k - 1]
+    v_ref[...] = total
+    c.finish()
+
+
+def last(nd, l, w, gg, x, gh, gain, terms, cid):
+    R, C = x.shape
+    J = gg.shape[1]
+    vm = pl.BlockSpec(memory_space=VMEM)
+    piece = (terms.shape[0], C // nd)
+    return pl.pallas_call(
+        functools.partial(last_kernel, nd),
+        out_shape=(jax.ShapeDtypeStruct((R, C), F32), jax.ShapeDtypeStruct((8 // nd, J, C // 8), F32), jax.ShapeDtypeStruct(piece, F32)),
+        in_specs=[vm] * 7,
+        out_specs=(vm,) * 3,
+        scratch_shapes=sum_scratch(R, C)
+        + [VMEM((R, C), F32)]
+        + dp_scratch(J, C // 8)
+        + [VMEM(terms.shape, F32), VMEM((max(nd - 1, 1),) + piece, F32), VMEM(piece, F32), VMEM((15,) + piece, F32)]
+        + [DMA((18,)), DMA((18,)), DMA((30,)), DMA((30,))],
+        compiler_params=pltpu.CompilerParams(collective_id=cid, has_side_effects=True, vmem_limit_bytes=60 * 2**20),
+        name="last_sums",
+    )(l, w, gg, x, gh, gain, terms)
 
 
 def layer_norm(tensor, gain_row, bias_row):
@@ -712,13 +1127,13 @@
 
     chunks = group // CHUNK
     seg = segment_ids.reshape(chunks, CHUNK)
-    last = seg[:, CHUNK - 1 :]
-    prior = jnp.concatenate([jnp.full((1, 1), -1, jnp.int32), last[:-1]], axis=0)
+    ending = seg[:, CHUNK - 1 :]
+    prior = jnp.concatenate([jnp.full((1, 1), -1, jnp.int32), ending[:-1]], axis=0)
     tok_cols = jnp.stack(
-        [t.astype(F32).reshape(group) for t in (seg, seg == prior, seg == last, same_next.reshape(seg.shape))], axis=1
+        [t.astype(F32).reshape(group) for t in (seg, seg == prior, seg == ending, same_next.reshape(seg.shape))], axis=1
     )
     tok_rows = seg.astype(F32)[:, None, :]
-    keep = (last == prior).astype(F32).reshape(chunks)
+    keep = (ending == prior).astype(F32).reshape(chunks)
     lam = -jnp.exp(own[6])
     decay = jnp.broadcast_to(jnp.exp(lam * CHUNK)[:, None], (cols, cols))
     vec = jnp.concatenate([lam[None], own[7:10], jnp.zeros((4, cols), F32), decay], axis=0)
@@ -741,66 +1156,58 @@
     g = cotangent.astype(F32)
     grad_value = (g * gate).astype(BF)
     grad_recept = (g * value_here * (gate * (1.0 - gate))).astype(BF)
-    grad_value_all, grad_key = value_back(grad_value, value_weight.T, lifted, 4)
-    key_back = matmul_sum(grad_key, key_weight.T, 5)
-    value_grad = contract(squared, grad_value_all, 0, 0)
-    key_grad = contract(key_in, grad_key, 0, 0)
-    recept_cols = swap(grad_recept.reshape(tokens, ring, cols).transpose(1, 0, 2), 6).reshape(group, cols)
+    grad_value_all, grad_key, recept_cols = value_back(
+        grad_value, value_weight.T, lifted, grad_recept.reshape(tokens, ring, cols).transpose(1, 0, 2), 4
+    )
+    recept_cols = recept_cols.reshape(group, cols)
     recept_two = jnp.concatenate([recept_cols, earlier(recept_cols) * same_next[:, None].astype(BF)], axis=1)
-    recept_np = contract(n2_all, recept_two, 0, 0)
-    recept_grad = (1.0 - nu_r)[:, None] * recept_np[:, :cols] + nu_r[:, None] * recept_np[:, cols:]
+    key_sum, early = key_back(
+        grad_key, key_weight.T, squared, recept_two, nu_r[None], grad_value_all, key_in, n2_all, 5
+    )
     recept_back = contract(grad_recept, recept_full, 1, 0)
-    nu_k_grad = jnp.sum(key_back * shift_here, axis=0)
+    nu_k_grad = jnp.sum(key_sum * shift_here, axis=0)
     nu_r_grad = jnp.sum(recept_back * shift_here, axis=0)
-    moved = (key_back * nu_k + recept_back * nu_r) * same_here
+    moved = (key_sum * nu_k + recept_back * nu_r) * same_here
     after = lax.ppermute(moved[:1], "sp", [(i, i - 1) for i in range(1, ring)])
-    grad_n2 = key_back * (1.0 - nu_k) + recept_back * (1.0 - nu_r) + jnp.concatenate([moved[1:], after], axis=0)
+    grad_n2 = key_sum * (1.0 - nu_k) + recept_back * (1.0 - nu_r) + jnp.concatenate([moved[1:], after], axis=0)
     unused, pull_two = jax.vjp(layer_norm, hidden, vectors[10], vectors[11])
     grad_hidden, gain_two, bias_two = pull_two(grad_n2)
     grad_hidden = g + grad_hidden
 
     grad_hidden_b = grad_hidden.astype(BF)
     gz_here = contract(grad_hidden_b, out_full, 1, 1).astype(BF)
-    gz = swap(gz_here.reshape(tokens, ring, cols).transpose(1, 0, 2), 7).reshape(group, cols)
-    grad_hidden_all = lax.all_gather(grad_hidden_b, "sp", axis=0, tiled=True)
-    grads_two, head_sums_grad = recurrence_back(projected, mixed_time, states, gz, tok_cols, tok_rows, keep, vec)
-    mix_np = contract(n1_all, grads_two, 0, 0)
-    mix_n = mix_np[:, :half].reshape(width, 4, cols).transpose(1, 0, 2)
-    mix_p = mix_np[:, half:].reshape(width, 4, cols).transpose(1, 0, 2)
-    mix_d = mix_p - mix_n
-    mix_grad = mix_n + mu[:, :, None] * mix_d
-    mu_grads = jnp.sum(mix_f * mix_d, axis=2)
-    n1_back = matmul_sum(grads_two, folded, 8)
-    out_grad = contract(z, grad_hidden_all, 0, 0)
-    unused, pull_one = jax.vjp(layer_norm, x, vectors[0], vectors[1])
-    grad_x, gain_one, bias_one = pull_one(n1_back)
-    input_grad = grad_hidden + grad_x
+    gz = gz_here.reshape(tokens, ring, cols).transpose(1, 0, 2)
+    mixt = mix_weights.transpose(0, 2, 1).reshape(4 * cols, width)
+    grads_two, head_sums_grad, late, mu_grads, early_sum = time_back(
+        nd, projected, mixed_time, states, gz, tok_cols, tok_rows, keep, vec, grad_hidden_b, z, mixt, mu, early, n1_all, 7
+    )
 
     def place(part):
         return lax.dynamic_update_slice_in_dim(jnp.zeros((width,), F32), part, s * cols, 0)
 
+    none = jnp.zeros((width,), F32)
     terms = jnp.stack(
-        [gain_one, bias_one, mu_grads[0], mu_grads[1], mu_grads[2], mu_grads[3]]
+        [none, none, mu_grads[0], mu_grads[1], mu_grads[2], mu_grads[3]]
         + [place(head_sums_grad[q]) for q in range(4)]
-        + [gain_two, bias_two, nu_k_grad, nu_r_grad]
+        + [gain_two, bias_two, nu_k_grad, nu_r_grad, none, none]
     )
-    rows, piece = terms.shape[0], width // (nd * ring)
-    terms = terms.reshape(rows, nd, ring, piece).transpose(2, 1, 0, 3).reshape(ring, nd, rows * piece)
-    packed = -(-rows * piece // 1024) * 1024
-    terms = jnp.pad(terms, ((0, 0), (0, 0), (0, packed - rows * piece))).reshape(ring, nd, packed // 128, 128)
-    vectors_grad = vec_sum(terms, 9).reshape(packed)[: rows * piece].reshape(rows, piece)
-
-    def over_dp(grad, dim):
-        return lax.psum_scatter(grad.astype(BF), "dp", scatter_dimension=dim, tiled=True).astype(F32)
-
+    input_grad, late_sum, vector_sum = last(nd, grads_two, folded, late, inputs, grad_hidden, vectors[0:1], terms, 8)
+    piece = width // (nd * ring)
+    vectors_grad = lax.dynamic_slice_in_dim(vector_sum[:14], s * piece, piece, 1)
+
+    def columns(part):
+        return part.transpose(1, 0, 2).reshape(part.shape[1], width // nd)
+
+    early_sum, late_sum = columns(early_sum), columns(late_sum)
+    units = key_weight.shape[1]
     return (
         result,
         input_grad,
-        over_dp(mix_grad, 1),
-        over_dp(out_grad, 1),
-        over_dp(key_grad, 0),
-        over_dp(value_grad, 1),
-        over_dp(recept_grad, 0),
+        late_sum[:half].reshape(4, cols, width // nd).transpose(0, 2, 1),
+        late_sum[half:],
+        early_sum[units : 2 * units].T,
+        early_sum[:units],
+        early_sum[2 * units :].T,
         vectors_grad,
     )
 

time: 686 us -> 541 us (0.79)
  the two profiles are of different devices: /device:TPU:0 before, /device:TPU:1 now
where the time goes in v3:
time: 541 us; the launch traced here: 531 us
  Pallas kernels  418 us (77%)
  local copies, waits for them, and re-layouts  45.1 us (8%)
  matrix products  26.2 us (5%)
  other arithmetic  22.6 us (4%)
  between operations  15 us (3%)
    pallas_call x1, Pallas kernels, time_back(): pl.pallas_call(functools.partial(time_back_kernel, nd), out_shape=(jax.Sh...  68.2 us
    pallas_call x1, Pallas kernels, project(): pl.pallas_call(project_kernel, out_shape=(jax.ShapeDtypeStruct((16 * R, C...  65.8 us
    pallas_call x1, Pallas kernels, last(): pl.pallas_call(functools.partial(last_kernel, nd), out_shape=(jax.ShapeDt...  65 us
    pallas_call x1, Pallas kernels, key_side(): pl.pallas_call(key_kernel, out_shape=(jax.ShapeDtypeStruct((16 * R, C), B...  58.5 us
    pallas_call x1, Pallas kernels, value_back(): pl.pallas_call(value_back_kernel, out_shape=(jax.ShapeDtypeStruct((16 * R...  49 us
    pallas_call x1, Pallas kernels, key_back(): pl.pallas_call(key_back_kernel, out_shape=(jax.ShapeDtypeStruct((R, C), F...  47.7 us
    pallas_call x1, Pallas kernels, matmul_sum(): pl.pallas_call(sum_kernel, out_shape=jax.ShapeDtypeStruct((R, C), F32), i...  38.1 us
    dot_general x3, matrix products, contract(): lax.dot_general(left, right, (((left_dim,), (right_dim,)), ((), ())), pre...  21.5 us
  transfers between devices with their start and end apart: 3, of which 0 were waited for; matrix products, arithmetic and copies ran while one was open for 8% of the time, Pallas kernels for 35%

profile of v3, /device:TPU:1, one launch (start us, length us, event | category | flops | bytes accessed | tf_op | source)
XLA Modules:
  0.0 531.0 jit_solution(15117560088507685539)
XLA Ops:
  7.2 0.7 all-gather.3.cloned.1.call-update
  8.0 0.7 all-gather.5.cloned.1.call-update
  8.7 0.7 convert_element_type.98
  9.4 0.8 fusion.18
  10.3 0.4 copy.72.same_ref
  10.7 0.8 slice.133
  11.5 0.9 slice_reduce_fusion
  12.4 0.8 fusion.19
  13.2 1.3 copy.73.col_ref
  14.5 0.9 dynamic-slice.1
  15.4 0.8 exponential_bitcast_fusion
  16.3 1.2 convert_reduce_fusion
  17.5 1.3 fusion.7
  18.9 0.6 broadcast_subtract_fusion.2
  19.5 1.5 fusion.10.a_ref
  21.0 65.8 %gather_project.1 = (bf16[2048,2048]{1,0:T(8,128)(2,1)}, f32[2048,512]{1,0:T(8,128)}) custom-call(bf16[128,2048]{1,0:T(8,128)(2,1)S(1)} %fusion.10.a_ref, bf16[4,2048,128]{2,1,0:T(8,128)(2,1)S(1)} %copy-done, f32[4,2048]{1,0:T(4,128)S(1)} %get-tuple-element.113.mu_ref, f32[2048,1]{1,0:T(8,128)S(1)} %copy.72.same_ref), custom_call_target="tpu_custom_call" | custom-call | tf_op jit(solution)/shard_map/gather_project/pallas_call | solution.py:200
  87.2 2.2 copy-done.1
  89.4 11.7 %recurrence.1 = (bf16[2048,128]{1,0:T(8,128)(2,1)S(1)}, f32[2048,128]{1,0:T(8,128)S(1)}, f32[16,128,128]{2,1,0:T(8,128)S(1)}) custom-call(f32[2048,512]{1,0:T(8,128)S(1)} %copy-done.1, f32[2048,4]{1,0:T(8,128)S(1)} %copy-done.3, f32[16,1,128]{2,1,0:T(1,128)S(1)} %bitcast.79, f32[16]{0:T(128)S(1)} %convert_reduce_fusion.1.keep_ref, ...), custom_call_target="tpu_custom_call" | custom-call | tf_op jit(solution)/shard_map/recurrence/pallas_call | solution.py:507
  101.1 0.8 copy-done.8
  101.9 1.0 copy-done.9
  102.9 1.0 copy-done.10
  103.9 13.9 %swap_blocks.1 = bf16[16,128,128]{2,1,0:T(8,128)(2,1)} custom-call(bf16[16,128,128]{2,1,0:T(8,128)(2,1)} %bitcast.75), custom_call_target="tpu_custom_call" | custom-call | tf_op jit(solution)/shard_map/swap_blocks/pallas_call | solution.py:390
  117.8 1.3 copy.74
  119.1 3.8 copy.75.w_ref
  122.9 3.9 copy.77
  127.0 4.7 fusion
  131.8 4.7 fusion.30
  136.8 1.1 add_convert_fusion.1.a_ref
  137.9 58.5 %gather_key.1 = (bf16[2048,2048]{1,0:T(8,128)(2,1)}, bf16[2048,2048]{1,0:T(8,128)(2,1)}, f32[2048,448]{1,0:T(8,128)}, bf16[2048,448]{1,0:T(8,128)(2,1)}) custom-call(bf16[128,2048]{1,0:T(8,128)(2,1)} %add_convert_fusion.1.a_ref, bf16[2048,448]{1,0:T(8,128)(2,1)} %copy.75.w_ref, f32[1,2048]{1,0:T(1,128)} %get-tuple-element.121.nu_ref, f32[2048,1]{1,0:T(8,128)} %copy-done.2), custom_call_target="tpu_custom_call" | custom-call | tf_op jit(solution)/shard_map/gather_key/pallas_call | solution.py:253
  196.4 1.7 copy-done.4
  198.1 38.1 %matmul_sum.1 = f32[128,2048]{1,0:T(8,128)S(1)} custom-call(bf16[2048,448]{1,0:T(8,128)(2,1)S(1)} %copy-done.4, bf16[448,2048]{1,0:T(8,128)(2,1)S(1)} %copy-done.6), custom_call_target="tpu_custom_call" | custom-call | tf_op jit(solution)/shard_map/matmul_sum/pallas_call | solution.py:360
  236.2 0.8 constant_dynamic-slice_fusion.1
  237.1 7.0 %fusion.14 = (bf16[128,2048]{1,0:T(8,128)(2,1)S(1)}, bf16[128,2048]{1,0:T(8,128)(2,1)}, bf16[128,2048]{1,0:T(8,128)(2,1)S(1)}) fusion(f32[128,2048]{1,0:T(8,128)S(1)} %matmul_sum.1, bf16[128,2048]{1,0:T(8,128)(2,1)} %param.10, f32[128,2048]{1,0:T(8,128)} %copy-done.15, bf16[2048,2048]{0,1:T(8,128)(2,1)} %all-gather.5.cloned.1.call-done, ...), kind=kOutput, calls=%fused_computation.29 | convolution fusion | flops 1080557568 | bytes 13640192 | tf_op jit(solution)/shard_map/dot_general | solution.py:1098
  244.2 0.7 copy-done.23
  244.9 49.0 %gather_value_back.1 = (bf16[2048,2048]{1,0:T(8,128)(2,1)}, bf16[2048,448]{1,0:T(8,128)(2,1)S(1)}, bf16[16,128,128]{2,1,0:T(8,128)(2,1)S(1)}) custom-call(bf16[128,2048]{1,0:T(8,128)(2,1)S(1)} %get-tuple-element.109.a_ref, bf16[2048,448]{1,0:T(8,128)(2,1)S(1)} %bitcast.74, f32[2048,448]{1,0:T(8,128)} %get-tuple-element.36.lift_ref, ...), custom_call_target="tpu_custom_call" | custom-call | tf_op jit(solution)/shard_map/gather_value_back/pallas_call | solution.py:821
  293.9 1.3 copy-done.7
  295.4 0.3 pad_multiply_fusion
  295.7 1.1 pad_maximum_fusion.rt_ref
  296.8 47.7 %key_back.1 = (f32[128,2048]{1,0:T(8,128)}, bf16[8,1024,256]{2,1,0:T(8,128)(2,1)}) custom-call(bf16[2048,448]{1,0:T(8,128)(2,1)} %copy-done.7, bf16[448,2048]{1,0:T(8,128)(2,1)} %bitcast.85, bf16[2048,448]{1,0:T(8,128)(2,1)} %get-tuple-element.33.refs_0_.s_ref, bf16[2048,256]{1,0:T(8,128)(2,1)} %pad_maximum_fusion.rt_ref, f32[1,2048]{1,0:T(1,128)} %copy-done.29, ...), custom_call_target="tpu_custom_call" | custom-call | tf_op jit(solution)/shard_map/key_back/pallas_call | solution.py:904
  344.6 8.0 %multiply_reduce_fusion = (f32[2048]{0:T(1024)S(1)}, f32[2048]{0:T(1024)S(1)}, f32[128,2048]{1,0:T(8,128)S(1)}, f32[128,2048]{1,0:T(8,128)}) fusion(bf16[128,2048]{1,0:T(8,128)(2,1)S(1)} %copy-done.18, f32[128]{0:T(128)S(1)} %fusion.22, bf16[127,2048]{1,0:T(8,128)(2,1)S(1)} %bitcast.83, bf16[1,2048]{1,0:T(2,128)(2,1)S(1)} %constant_dynamic-slice_fusion.1, ...), kind=kOutput, calls=%fused_computation.32 | convolution fusion | flops 1077669888 | bytes 13140480 | tf_op jit(solution)/shard_map/dot_general | solution.py:1098
  352.5 2.6 collective-permute-start
  355.2 2.4 maximum_bitcast_fusion
  357.5 2.7 copy.81
  360.2 6.7 %copy.83 = bf16[8,128,2048]{2,1,0:T(8,128)(2,1)} copy(bf16[8,128,2048]{1,2,0:T(8,128)(2,1)} %maximum_bitcast_fusion) | data formatting | bytes 8388608 | tf_op jit(solution)/shard_map/transpose | solution.py:1122
  367.0 1.9 multiply_reduce_fusion.2
  369.0 0.4 fusion.28
  369.4 1.2 fusion.27
  370.6 6.4 %convolution_convert_fusion = bf16[128,2048]{1,0:T(8,128)(2,1)S(1)} fusion(bf16[128,2048]{1,0:T(8,128)(2,1)S(1)} %get-tuple-element.97.gh_ref, bf16[2048,2048]{1,0:T(8,128)(2,1)} %all-gather.3.cloned.1.call-done), kind=kOutput, calls=%fused_computation.10 | convolution fusion | flops 1074003968 | bytes 9437184 | tf_op jit(solution)/shard_map/dot_general | solution.py:1098
  377.0 0.3 copy.79
  377.3 1.0 copy.80
  378.3 68.2 %time_back.1 = (bf16[2048,1024]{1,0:T(8,128)(2,1)}, f32[8,128]{1,0:T(8,128)}, bf16[8,640,256]{2,1,0:T(8,128)(2,1)}, f32[4,2048]{1,0:T(4,128)}, f32[1,1024,256]{2,1,0:T(8,128)}) custom-call(f32[2048,512]{1,0:T(8,128)} %get-tuple-element.30.x_ref, f32[2048,128]{1,0:T(8,128)} %copy-done.9, f32[16,128,128]{2,1,0:T(8,128)} %copy-done.10, ...), custom_call_target="tpu_custom_call" | custom-call | tf_op jit(solution)/shard_map/time_back/pallas_call | solution.py:998
  446.6 0.7 constant_dynamic-update-slice_fusion.3
  447.3 0.7 constant_dynamic-update-slice_fusion.2
  448.0 0.7 constant_dynamic-update-slice_fusion.1
  448.6 0.7 constant_dynamic-update-slice_fusion
  449.3 2.1 stack.24.terms_ref
  451.5 65.0 %last_sums.1 = (f32[128,2048]{1,0:T(8,128)}, f32[1,640,256]{2,1,0:T(8,128)}, f32[16,256]{1,0:T(8,128)}) custom-call(bf16[2048,1024]{1,0:T(8,128)(2,1)} %get-tuple-element.44.l_ref, bf16[1024,2048]{1,0:T(8,128)(2,1)} %bitcast.81, bf16[8,640,256]{2,1,0:T(8,128)(2,1)} %get-tuple-element.45.gg_ref, bf16[128,2048]{1,0:T(8,128)(2,1)} %x_ref.1, ...), custom_call_target="tpu_custom_call" | custom-call | tf_op jit(solution)/shard_map/last_sums/pallas_call | solution.py:1072
  516.6 1.2 slice.123
  517.7 1.6 slice_bitcast_fusion.3
  519.3 1.0 slice_bitcast_fusion
  520.3 1.0 copy.84
  521.3 0.8 copy.85
  522.0 0.7 constant_dynamic-slice_fusion
  522.7 1.0 copy.93
  (93 shorter events, 1.7 us)
Async XLA Ops:
  7.2 11.7 %copy-start.32 = (f32[14,2048]{1,0:T(8,128)S(1)}, f32[14,2048]{1,0:T(8,128)}, u32[]{:S(2)}) copy-start(f32[14,2048]{1,0:T(8,128)} %param.16) | copy-start | bytes 344068
  7.2 13.8 %copy-start = (bf16[4,2048,128]{2,1,0:T(8,128)(2,1)S(1)}, bf16[4,2048,128]{2,1,0:T(8,128)(2,1)}, u32[]{:S(2)}) copy-start(bf16[4,2048,128]{2,1,0:T(8,128)(2,1)} %w_ref.2) | copy-start | bytes 6291460
  7.2 124.6 %all-gather.3.cloned.1.call-start = ((), (), s32[]{:S(2)}) async-start(), calls=%async_computation | async-start | bytes 8912896 | tf_op jit(solution)/shard_map/all_gather | solution.py:1115
  7.9 229.1 %all-gather.5.cloned.1.call-start = ((), (), s32[]{:S(2)}) async-start(), calls=%async_computation.1 | async-start | bytes 8912896 | tf_op jit(solution)/shard_map/all_gather | solution.py:1116
  9.4 77.8 %copy-start.13 = (f32[2048]{0:T(1024)}, f32[2048]{0:T(1024)S(1)}, u32[]{:S(2)}) copy-start(f32[2048]{0:T(1024)S(1)} %convert_element_type.98) | copy-start | bytes 24580
  10.2 76.6 %copy-start.27 = (s32[2048]{0:T(1024)S(1)}, s32[2048]{0:T(1024)}, u32[]{:S(2)}) copy-start(s32[2048]{0:T(1024)} %param.17) | copy-start | bytes 24580
  10.7 90.4 %copy-start.2 = (f32[2048,1]{1,0:T(8,128)}, f32[2048,1]{1,0:T(8,128)S(1)}, u32[]{:S(2)}) copy-start(f32[2048,1]{1,0:T(8,128)S(1)} %copy.72.same_ref) | copy-start | bytes 24580
  14.5 72.6 %copy-start.3 = (f32[2048,4]{1,0:T(8,128)S(1)}, f32[2048,4]{1,0:T(8,128)}, u32[]{:S(2)}) copy-start(f32[2048,4]{1,0:T(8,128)} %copy.73.col_ref) | copy-start | bytes 98308
  19.5 81.6 %copy-start.28 = (f32[1,2048]{1,0:T(1,128)}, f32[1,2048]{1,0:T(1,128)S(1)}, u32[]{:S(2)}) copy-start(f32[1,2048]{1,0:T(1,128)S(1)} %get-tuple-element.119.gain_ref) | copy-start | bytes 24580
  19.5 217.6 %copy-start.29 = (f32[1,2048]{1,0:T(1,128)}, f32[1,2048]{1,0:T(1,128)S(1)}, u32[]{:S(2)}) copy-start(f32[1,2048]{1,0:T(1,128)S(1)} %get-tuple-element.120.nu_ref) | copy-start | bytes 24580
  19.5 107.4 %copy-start.12 = (f32[4,2048]{1,0:T(4,128)}, f32[4,2048]{1,0:T(4,128)S(1)}, u32[]{:S(2)}) copy-start(f32[4,2048]{1,0:T(4,128)S(1)} %get-tuple-element.113.mu_ref) | copy-start | bytes 98308
  87.0 35.9 %copy-start.14 = (f32[16]{0:T(128)}, f32[16]{0:T(128)S(1)}, u32[]{:S(2)}) copy-start(f32[16]{0:T(128)S(1)} %convert_reduce_fusion.1.keep_ref) | copy-start | bytes 196
  87.1 35.8 %copy-start.11 = (f32[136,128]{1,0:T(8,128)}, f32[136,128]{1,0:T(8,128)S(1)}, u32[]{:S(2)}) copy-start(f32[136,128]{1,0:T(8,128)S(1)} %maximum_maximum_fusion.vec_ref) | copy-start | bytes 208900
  87.2 2.2 copy-start.1
  101.1 0.8 copy-start.8
  101.9 1.0 copy-start.9
  102.9 1.0 copy-start.10
  122.9 8.8 %copy-start.17 = (bf16[128,2048]{1,0:T(8,128)(2,1)S(1)}, bf16[128,2048]{1,0:T(8,128)(2,1)}, u32[]{:S(2)}) copy-start(bf16[128,2048]{1,0:T(8,128)(2,1)} %x_ref.1) | copy-start | bytes 1572868
  136.5 59.9 %copy-start.15 = (f32[128,2048]{1,0:T(8,128)}, f32[128,2048]{1,0:T(8,128)S(1)}, u32[]{:S(2)}) copy-start(f32[128,2048]{1,0:T(8,128)S(1)} %get-tuple-element.127) | copy-start | bytes 3145732
  136.5 59.9 %copy-start.6 = (bf16[448,2048]{1,0:T(8,128)(2,1)S(1)}, bf16[448,2048]{1,0:T(8,128)(2,1)}, u32[]{:S(2)}) copy-start(bf16[448,2048]{1,0:T(8,128)(2,1)} %refs_1_.1) | copy-start | bytes 5505028
  196.4 1.7 copy-start.4
  237.1 7.9 %copy-start.5 = (bf16[448,2048]{0,1:T(8,128)(2,1)S(1)}, bf16[448,2048]{0,1:T(8,128)(2,1)}, u32[]{:S(2)}) copy-start(bf16[448,2048]{0,1:T(8,128)(2,1)} %copy.77) | copy-start | bytes 5505028
  244.1 0.8 copy-start.23
  293.9 1.3 copy-start.7
  296.8 47.7 %copy-start.18 = (bf16[128,2048]{1,0:T(8,128)(2,1)S(1)}, bf16[128,2048]{1,0:T(8,128)(2,1)}, u32[]{:S(2)}) copy-start(bf16[128,2048]{1,0:T(8,128)(2,1)} %add_convert_fusion.1.a_ref) | copy-start | bytes 1572868
  296.8 47.7 %copy-start.30 = (f32[1,2048]{1,0:T(1,128)S(1)}, f32[1,2048]{1,0:T(1,128)}, u32[]{:S(2)}) copy-start(f32[1,2048]{1,0:T(1,128)} %copy-done.29) | copy-start | bytes 24580
  296.8 47.7 %copy-start.31 = (f32[1,2048]{1,0:T(1,128)S(1)}, f32[1,2048]{1,0:T(1,128)}, u32[]{:S(2)}) copy-start(f32[1,2048]{1,0:T(1,128)} %get-tuple-element.121.nu_ref) | copy-start | bytes 24580
  344.5 10.6 %copy-start.19 = (bf16[4,2048,128]{2,1,0:T(8,128)(2,1)S(1)}, bf16[4,2048,128]{2,1,0:T(8,128)(2,1)}, u32[]{:S(2)}) copy-start(bf16[4,2048,128]{2,1,0:T(8,128)(2,1)} %get-tuple-element.105) | copy-start | bytes 6291460
  344.5 10.6 %copy-start.20 = (bf16[4,2048,128]{2,1,0:T(8,128)(2,1)S(1)}, bf16[4,2048,128]{2,1,0:T(8,128)(2,1)}, u32[]{:S(2)}) copy-start(bf16[4,2048,128]{2,1,0:T(8,128)(2,1)} %get-tuple-element.106) | copy-start | bytes 6291460
  352.5 14.5 %collective-permute-start = (f32[1,2048]{1,0:T(1,128)S(1)}, f32[1,2048]{1,0:T(1,128)S(1)}, u32[]{:S(2)}, u32[]{:S(2)}) collective-permute-start(f32[1,2048]{1,0:T(1,128)S(1)} %slice.138), channel_id=1, source_target_pairs={{1,0},{2,1},{3,2},{4,3},{5,4},{6,5},{7,6},{8,7},{9,8},{10,9},{11,1... | collective-permute-start | bytes 24584 | tf_op jit(solution)/shard_map/ppermute | solution.py:1171
  360.2 6.8 %copy-start.16 = (f32[128,2048]{1,0:T(8,128)S(1)}, f32[128,2048]{1,0:T(8,128)}, u32[]{:S(2)}) copy-start(f32[128,2048]{1,0:T(8,128)} %copy-done.15) | copy-start | bytes 3145732
  360.2 6.8 %copy-start.22 = (f32[128,2048]{1,0:T(8,128)S(1)}, f32[128,2048]{1,0:T(8,128)}, u32[]{:S(2)}) copy-start(f32[128,2048]{1,0:T(8,128)} %get-tuple-element.41) | copy-start | bytes 3145732
  367.0 2.3 copy-start.26
  370.6 6.5 %copy-start.21 = (bf16[128,2048]{1,0:T(8,128)(2,1)}, bf16[128,2048]{1,0:T(8,128)(2,1)S(1)}, u32[]{:S(2)}) copy-start(bf16[128,2048]{1,0:T(8,128)(2,1)S(1)} %get-tuple-element.97.gh_ref) | copy-start | bytes 1572868
  451.5 67.8 %copy-start.24 = (f32[1,1024,256]{2,1,0:T(8,128)S(1)}, f32[1,1024,256]{2,1,0:T(8,128)}, u32[]{:S(2)}) copy-start(f32[1,1024,256]{2,1,0:T(8,128)} %get-tuple-element.50) | copy-start | bytes 3145732
  516.5 5.5 %copy-start.33 = (f32[16,256]{1,0:T(8,128)S(1)}, f32[16,256]{1,0:T(8,128)}, u32[]{:S(2)}) copy-start(f32[16,256]{1,0:T(8,128)} %get-tuple-element.51) | copy-start | bytes 49156
  516.5 6.2 %copy-start.25 = (f32[128,2048]{1,0:T(8,128)S(1)}, f32[128,2048]{1,0:T(8,128)}, u32[]{:S(2)}) copy-start(f32[128,2048]{1,0:T(8,128)} %get-tuple-element.140) | copy-start | bytes 3145732
Sparse Core Ops, SparseCore 0:
  10.4 91.3 all-gather.2
  104.1 96.0 all-gather.4
